TPU v7x, 32 devices: a whole 2x2x4 slice. The times are simulated.
32 devices in a mesh: fsdp: 8 (over z, x), context: 4 (over y, core).
Axes of the slice: x: 2, y: 2, z: 4, core: 2. Of those that a mesh axis runs over, the one named last changes fastest.
Arguments:
- block_input: bfloat16 [8, 2048, 1088], P('fsdp', 'context'), may hold values from -6 to 6
- segment_ids: int32 [8, 2048], P('fsdp'), may hold values from 0 to 15, as said below
- ln1_gain: bfloat16 [1088], P('fsdp'), may hold values from 0.099609375 to 1.8984375
- ln1_bias: bfloat16 [1088], P('fsdp'), may hold values from -3 to 3
- w_qkv: bfloat16 [1088, 3264], P('fsdp'), may hold values from -0.1875 to 0.1875
- bias_query: bfloat16 [1088], P('fsdp'), may hold values from -3 to 3
- bias_value: bfloat16 [1088], P('fsdp'), may hold values from -4 to 4
- w_out: bfloat16 [1088, 1088], P('fsdp'), may hold values from -0.75 to 0.75
- bias_out: bfloat16 [1088], P('fsdp'), may hold values from -3 to 3
- ln2_gain: bfloat16 [1088], P('fsdp'), may hold values from 0.099609375 to 1.8984375
- ln2_bias: bfloat16 [1088], P('fsdp'), may hold values from -3 to 3
- w_up: bfloat16 [1088, 4352], P('fsdp'), may hold values from -0.1875 to 0.1875
- bias_up: bfloat16 [4352], P('fsdp'), may hold values from -4 to 4
- w_down: bfloat16 [4352, 1088], P('fsdp'), may hold values from -0.09375 to 0.09375
- bias_down: bfloat16 [1088], P('fsdp'), may hold values from -3 to 3
- cotangent: bfloat16 [8, 2048, 1088], P('fsdp', 'context'), may hold values from -6 to 6
Outputs:
- block_output: bfloat16 [8, 2048, 1088], P('fsdp', 'context')
- input_grad: float32 [8, 2048, 1088], P('fsdp', 'context')
- grad_ln1_gain: float32 [1088], P('fsdp')
- grad_ln1_bias: float32 [1088], P('fsdp')
- grad_w_qkv: float32 [1088, 3264], P('fsdp')
- grad_bias_query: float32 [1088], P('fsdp')
- grad_bias_value: float32 [1088], P('fsdp')
- grad_w_out: float32 [1088, 1088], P('fsdp')
- grad_bias_out: float32 [1088], P('fsdp')
- grad_ln2_gain: float32 [1088], P('fsdp')
- grad_ln2_bias: float32 [1088], P('fsdp')
- grad_w_up: float32 [1088, 4352], P('fsdp')
- grad_bias_up: float32 [4352], P('fsdp')
- grad_w_down: float32 [4352, 1088], P('fsdp')
- grad_bias_down: float32 [1088], P('fsdp')
Inputs may be any that keep to these rules, and one draw needn't show every extreme that they name: `segment_ids`: within each sequence the ids never fall; equal ids mark one document, and a token attends only to earlier tokens of its own document.
All inputs are finite; a program needn't handle non-finite values.
Results may differ from a plain program's by a relative error of at most 0.011.
Values may be sent and summed in bfloat16 or wider, within the bound.
A program may use at most 384 MiB of HBM per device.

v0:
```python
import jax
import jax.numpy as jnp
from jax import lax
from jax.sharding import PartitionSpec as P

HEAD_DIM = 64


masked_score = -1e30


def normalize(inputs, scale_vec, shift_vec):
    average = jnp.mean(inputs, axis=-1, keepdims=True)
    centered = inputs - average
    variance = jnp.mean(centered * centered, axis=-1, keepdims=True)
    return centered * lax.rsqrt(variance + 1e-05) * scale_vec + shift_vec


def gelu_tanh(pre_act):
    return jax.nn.gelu(pre_act, approximate=True)


def contract_rows(left, right):
    return lax.dot_general(
        left, right, (((0,), (0,)), ((), ())), preferred_element_type=jnp.float32
    )


def contract_cols(left, right):
    return lax.dot_general(
        left, right, (((1,), (1,)), ((), ())), preferred_element_type=jnp.float32
    )


def score_table(query_rows, key_rows, query_segs, key_segs, query_place, key_place, head_count):
    query_heads = query_rows.reshape(query_rows.shape[0], head_count, HEAD_DIM)
    key_heads = key_rows.reshape(key_rows.shape[0], head_count, HEAD_DIM)
    raw = (
        jnp.einsum("qhd,khd->hqk", query_heads, key_heads, preferred_element_type=jnp.float32)
        * 0.125
    )
    allowed = (key_place[None, :] <= query_place[:, None]) & (
        key_segs[None, :] == query_segs[:, None]
    )
    return jnp.where(allowed[None], raw, masked_score)


def local(
    block_input,
    segment_ids,
    ln1_gain,
    ln1_bias,
    w_qkv,
    bias_query,
    bias_value,
    w_out,
    bias_out,
    ln2_gain,
    ln2_bias,
    w_up,
    bias_up,
    w_down,
    bias_down,
    cotangent,
):
    sequences, stretch, features = block_input.shape
    head_count = features // HEAD_DIM
    length_all = stretch * lax.axis_size("context")
    offset = lax.axis_index("context") * stretch
    tokens = sequences * stretch
    (
        gain_one,
        shift_one,
        full_qkv,
        query_bias,
        value_bias,
        full_out,
        out_bias,
        gain_two,
        shift_two,
        full_up,
        up_bias,
        full_down,
        down_bias,
    ) = (
        lax.all_gather(ln1_gain, "fsdp", axis=0, tiled=True),
        lax.all_gather(ln1_bias, "fsdp", axis=0, tiled=True),
        lax.all_gather(w_qkv, "fsdp", axis=0, tiled=True),
        lax.all_gather(bias_query, "fsdp", axis=0, tiled=True),
        lax.all_gather(bias_value, "fsdp", axis=0, tiled=True),
        lax.all_gather(w_out, "fsdp", axis=0, tiled=True),
        lax.all_gather(bias_out, "fsdp", axis=0, tiled=True),
        lax.all_gather(ln2_gain, "fsdp", axis=0, tiled=True),
        lax.all_gather(ln2_bias, "fsdp", axis=0, tiled=True),
        lax.all_gather(w_up, "fsdp", axis=0, tiled=True),
        lax.all_gather(bias_up, "fsdp", axis=0, tiled=True),
        lax.all_gather(w_down, "fsdp", axis=0, tiled=True),
        lax.all_gather(bias_down, "fsdp", axis=0, tiled=True),
    )
    gain_one = gain_one.astype(jnp.float32)
    shift_one = shift_one.astype(jnp.float32)
    gain_two = gain_two.astype(jnp.float32)
    shift_two = shift_two.astype(jnp.float32)
    inputs = block_input.reshape(tokens, features).astype(jnp.float32)
    normed = normalize(inputs, gain_one, shift_one).astype(jnp.bfloat16)
    stacked = jnp.dot(normed, full_qkv, preferred_element_type=jnp.float32)
    queries = (stacked[:, :features] + query_bias.astype(jnp.float32)).astype(jnp.bfloat16)
    keys_own = stacked[:, features : 2 * features].astype(jnp.bfloat16)
    values_own = (stacked[:, 2 * features :] + value_bias.astype(jnp.float32)).astype(jnp.bfloat16)
    query_seqs = queries.reshape(sequences, stretch, features)
    key_seqs = keys_own.reshape(sequences, stretch, features)
    value_seqs = values_own.reshape(sequences, stretch, features)
    keys_all, values_all = (
        lax.all_gather(key_seqs, "context", axis=1, tiled=True),
        lax.all_gather(value_seqs, "context", axis=1, tiled=True),
    )
    query_place = offset + jnp.arange(stretch, dtype=jnp.int32)
    key_place = jnp.arange(length_all, dtype=jnp.int32)
    own_segs = lax.dynamic_slice_in_dim(segment_ids, offset, stretch, 1)

    def forward_one(item):
        query_rows, key_rows, value_rows, segs_own, segs_all = item
        scores = score_table(
            query_rows, key_rows, segs_own, segs_all, query_place, key_place, head_count
        )
        largest = jnp.max(scores, axis=-1, keepdims=True)
        weights = jnp.exp(scores - largest)
        totals = jnp.sum(weights, axis=-1, keepdims=True)
        probs = (weights / totals).astype(jnp.bfloat16)
        value_heads = value_rows.reshape(length_all, head_count, HEAD_DIM)
        mixed = jnp.einsum("hqk,khd->qhd", probs, value_heads, preferred_element_type=jnp.float32)
        lse_rows = largest[:, :, 0] + jnp.log(totals[:, :, 0])
        return (mixed.reshape(stretch, features).astype(jnp.bfloat16), lse_rows)

    attended, lse_kept = lax.map(
        forward_one, (query_seqs, keys_all, values_all, own_segs, segment_ids)
    )
    attended = attended.reshape(tokens, features)
    middle = (
        inputs
        + jnp.dot(attended, full_out, preferred_element_type=jnp.float32)
        + out_bias.astype(jnp.float32)
    )
    normed_two = normalize(middle, gain_two, shift_two).astype(jnp.bfloat16)
    pre_act = jnp.dot(normed_two, full_up, preferred_element_type=jnp.float32) + up_bias.astype(
        jnp.float32
    )
    hidden = gelu_tanh(pre_act).astype(jnp.bfloat16)
    result = (
        middle
        + jnp.dot(hidden, full_down, preferred_element_type=jnp.float32)
        + down_bias.astype(jnp.float32)
    )
    block_output = result.astype(jnp.bfloat16).reshape(block_input.shape)
    grad_out = cotangent.reshape(tokens, features)
    grad_out_f = grad_out.astype(jnp.float32)
    grad_w_down = contract_rows(hidden, grad_out)
    grad_b_down = jnp.sum(grad_out_f, axis=0)
    grad_hidden = contract_cols(grad_out, full_down)
    gelu_value, gelu_pull = jax.vjp(gelu_tanh, pre_act)
    grad_pre = gelu_pull(grad_hidden)[0].astype(jnp.bfloat16)
    grad_w_up = contract_rows(normed_two, grad_pre)
    grad_b_up = jnp.sum(grad_pre.astype(jnp.float32), axis=0)
    grad_normed_two = contract_cols(grad_pre, full_up)
    norm_value, norm_pull = jax.vjp(normalize, middle, gain_two, shift_two)
    grad_middle_part, grad_gain_two, grad_shift_two = norm_pull(grad_normed_two)
    grad_middle = grad_out_f + grad_middle_part
    grad_middle_low = grad_middle.astype(jnp.bfloat16)
    grad_w_out = contract_rows(attended, grad_middle_low)
    grad_b_out = jnp.sum(grad_middle_low.astype(jnp.float32), axis=0)
    grad_attended = contract_cols(grad_middle_low, full_out).astype(jnp.bfloat16)
    grad_att_seqs = grad_attended.reshape(sequences, stretch, features)

    def local_grads(item):
        query_rows, key_rows, value_rows, grad_rows, segs_own, segs_all, lse_rows = item
        scores = score_table(
            query_rows, key_rows, segs_own, segs_all, query_place, key_place, head_count
        )
        probs = jnp.exp(scores - lse_rows[:, :, None])
        grad_heads = grad_rows.reshape(stretch, head_count, HEAD_DIM)
        value_heads = value_rows.reshape(length_all, head_count, HEAD_DIM)
        key_heads = key_rows.reshape(length_all, head_count, HEAD_DIM)
        grad_probs = jnp.einsum(
            "qhd,khd->hqk", grad_heads, value_heads, preferred_element_type=jnp.float32
        )
        deltas = jnp.sum(probs * grad_probs, axis=-1)
        grad_scores = (probs * (grad_probs - deltas[:, :, None])).astype(jnp.bfloat16)
        grad_query = (
            jnp.einsum(
                "hqk,khd->qhd", grad_scores, key_heads, preferred_element_type=jnp.float32
            ).reshape(stretch, features)
            * 0.125
        )
        query_heads = query_rows.reshape(stretch, head_count, HEAD_DIM)
        key_part = (
            jnp.einsum(
                "hqk,qhd->khd", grad_scores, query_heads, preferred_element_type=jnp.float32
            ).reshape(length_all, features)
            * 0.125
        )
        value_part = jnp.einsum(
            "hqk,qhd->khd",
            probs.astype(jnp.bfloat16),
            grad_heads,
            preferred_element_type=jnp.float32,
        ).reshape(length_all, features)
        return (grad_query, key_part, value_part)

    local_items = (query_seqs, keys_all, values_all, grad_att_seqs, own_segs, segment_ids, lse_kept)
    grad_queries, key_parts, value_parts = lax.map(local_grads, local_items)
    grad_keys, grad_values = (
        lax.psum_scatter(key_parts, "context", scatter_dimension=1, tiled=True),
        lax.psum_scatter(value_parts, "context", scatter_dimension=1, tiled=True),
    )
    grad_queries = grad_queries.reshape(tokens, features).astype(jnp.bfloat16)
    grad_keys = grad_keys.reshape(tokens, features).astype(jnp.bfloat16)
    grad_values = grad_values.reshape(tokens, features).astype(jnp.bfloat16)
    grad_stacked = jnp.concatenate([grad_queries, grad_keys, grad_values], axis=1)
    grad_w_qkv = contract_rows(normed, grad_stacked)
    grad_b_query = jnp.sum(grad_queries.astype(jnp.float32), axis=0)
    grad_b_value = jnp.sum(grad_values.astype(jnp.float32), axis=0)
    grad_normed = contract_cols(grad_stacked, full_qkv)
    first_value, first_pull = jax.vjp(normalize, inputs, gain_one, shift_one)
    grad_input_part, grad_gain_one, grad_shift_one = first_pull(grad_normed)
    input_grad = (grad_middle + grad_input_part).reshape(block_input.shape)
    shares = (
        lax.psum_scatter(grad_gain_one, "fsdp", scatter_dimension=0, tiled=True),
        lax.psum_scatter(grad_shift_one, "fsdp", scatter_dimension=0, tiled=True),
        lax.psum_scatter(grad_w_qkv, "fsdp", scatter_dimension=0, tiled=True),
        lax.psum_scatter(grad_b_query, "fsdp", scatter_dimension=0, tiled=True),
        lax.psum_scatter(grad_b_value, "fsdp", scatter_dimension=0, tiled=True),
        lax.psum_scatter(grad_w_out, "fsdp", scatter_dimension=0, tiled=True),
        lax.psum_scatter(grad_b_out, "fsdp", scatter_dimension=0, tiled=True),
        lax.psum_scatter(grad_gain_two, "fsdp", scatter_dimension=0, tiled=True),
        lax.psum_scatter(grad_shift_two, "fsdp", scatter_dimension=0, tiled=True),
        lax.psum_scatter(grad_w_up, "fsdp", scatter_dimension=0, tiled=True),
        lax.psum_scatter(grad_b_up, "fsdp", scatter_dimension=0, tiled=True),
        lax.psum_scatter(grad_w_down, "fsdp", scatter_dimension=0, tiled=True),
        lax.psum_scatter(grad_b_down, "fsdp", scatter_dimension=0, tiled=True),
    )
    column_parts = (
        lax.psum_scatter(shares[2], "context", scatter_dimension=1, tiled=True),
        lax.psum_scatter(shares[5], "context", scatter_dimension=1, tiled=True),
        lax.psum_scatter(shares[9], "context", scatter_dimension=1, tiled=True),
        lax.psum_scatter(shares[11], "context", scatter_dimension=1, tiled=True),
    )
    matrices = (
        lax.all_gather(column_parts[0], "context", axis=1, tiled=True),
        lax.all_gather(column_parts[1], "context", axis=1, tiled=True),
        lax.all_gather(column_parts[2], "context", axis=1, tiled=True),
        lax.all_gather(column_parts[3], "context", axis=1, tiled=True),
    )
    vectors = lax.psum(
        (
            shares[0],
            shares[1],
            shares[3],
            shares[4],
            shares[6],
            shares[7],
            shares[8],
            shares[10],
            shares[12],
        ),
        "context",
    )
    return (
        block_output,
        input_grad,
        vectors[0],
        vectors[1],
        matrices[0],
        vectors[2],
        vectors[3],
        matrices[1],
        vectors[4],
        vectors[5],
        vectors[6],
        matrices[2],
        vectors[7],
        matrices[3],
        vectors[8],
    )


def solution(mesh):
    in_specs = (
        P("fsdp", "context", None),
        P("fsdp", None),
        P("fsdp"),
        P("fsdp"),
        P("fsdp", None),
        P("fsdp"),
        P("fsdp"),
        P("fsdp", None),
        P("fsdp"),
        P("fsdp"),
        P("fsdp"),
        P("fsdp", None),
        P("fsdp"),
        P("fsdp", None),
        P("fsdp"),
        P("fsdp", "context", None),
    )
    out_specs = (
        P("fsdp", "context", None),
        P("fsdp", "context", None),
        P("fsdp"),
        P("fsdp"),
        P("fsdp", None),
        P("fsdp"),
        P("fsdp"),
        P("fsdp", None),
        P("fsdp"),
        P("fsdp"),
        P("fsdp"),
        P("fsdp", None),
        P("fsdp"),
        P("fsdp", None),
        P("fsdp"),
    )
    return jax.shard_map(local, mesh=mesh, in_specs=in_specs, out_specs=out_specs, check_vma=False)
```

profile of v0, /device:TPU:0, one launch (start us, length us, event | category | flops | bytes accessed | tf_op | source)
XLA Modules:
  0.0 2059.7 jit_solution(1440715885156961806)
XLA Ops:
  18.3 41.3 %all-reduce.21 = (bf16[1088]{0:T(1024)(128)(2,1)S(1)}, bf16[1088]{0:T(1024)(128)(2,1)S(1)}, bf16[1088]{0:T(1024)(128)(2,1)S(1)}, bf16[1088]{0:T(1024)(128)(2,1)S...) all-reduce(bf16[1088]{0:T(1024)(128)(2,1)S(1)} %dynamic-update-slic, ...), channel_id=1, replica_groups=mesh['fsdp'=8,'context'=4] {'fsdp'}, use_global_device_ids=true, to_apply=%add.1 | all-reduce | flops 13056 | bytes 52224
  62.0 63.1 %all-gather.15.cloned.1.call-done = bf16[1088,3264]{1,0:T(8,128)(2,1)} async-done(((bf16[136,3264]{1,0:T(8,128)(2,1)}), bf16[1088,3264]{1,0:T(8,128)(2,1)}) %all-gather.15.cloned.1.call-update) | async-done | bytes 7102480 | tf_op jit(solution)/shard_map/all_gather | solution.py:88
  145.6 25.1 %all-gather.27.cloned.1.call-done = bf16[2048,1088]{0,1:T(8,128)(2,1)} async-done(((bf16[512,1088]{0,1:T(8,128)(2,1)}), bf16[2048,1088]{0,1:T(8,128)(2,1)}) %all-gather.27.cloned.1.call-update) | async-done | bytes 4456464 | tf_op jit(solution)/shard_map/all_gather | solution.py:114
  170.7 29.2 %fusion.6 = (f32[17,512]{1,0:T(8,128)S(1)}, f32[17,512,2048]{2,1,0:T(8,128)}) fusion(pred[512,2048]{1,0:T(8,128)(4,1)S(1)} %fusion.14, bf16[512,17,64]{0,2,1:T(8,128)(2,1)S(1)} %bitcast.133, bf16[2048,17,64]{0,2,1:T(8,128)(2,1)} %bitcast.130), kind=kOutput, calls=%fused_computation.11 | convolution fusion | flops 2335170048 | bytes 77957120 | tf_op jit(solution)/shard_map/while/body/eval_jaxpr/qhd,khd->hqk/dot_general | solution.py:39
  199.9 23.2 %fusion = f32[17,512]{1,0:T(8,128)S(1)} fusion(f32[17,512]{1,0:T(8,128)S(1)} %get-tuple-element.145, f32[17,512,2048]{2,1,0:T(8,128)} %get-tuple-element.146, pred[512,2048]{1,0:T(8,128)(4,1)S(1)} %fusion.14), kind=kLoop, calls=%fused_computation.6 | loop fusion | flops 71294464 | bytes 72421376 | tf_op jit(solution)/shard_map/while/body/eval_jaxpr/reduce_sum | solution.py:128
  223.2 29.5 %fusion.33 = bf16[17,64,512]{2,1,0:T(8,128)(2,1)} fusion(bf16[2048,17,64]{0,2,1:T(8,128)(2,1)} %bitcast.138, f32[17,512]{1,0:T(8,128)S(1)} %fusion, f32[17,512]{1,0:T(8,128)S(1)} %get-tuple-element.145, f32[17,512,2048]{2,1,0:T(8,128)} %get-tuple-element.146, pred[512,2048]{1,0:T(8,128)(4,1)S(1)} %fusion.14), kind=kOutput, calls=%fused_computation.66 | convolution fusion | flops 2371387392 | bytes 77991936 | tf_op jit(solution)/shard_map/while/body/eval_jaxpr/hqk,khd->qhd/dot_general | solution.py:131
  252.7 11.9 all-gather.17.cloned.1.call-done
  269.0 134.6 %all-gather.19.cloned.1.call-done = bf16[1088,4352]{1,0:T(8,128)(2,1)} async-done(((bf16[136,4352]{1,0:T(8,128)(2,1)}), bf16[1088,4352]{1,0:T(8,128)(2,1)}) %all-gather.19.cloned.1.call-update) | async-done | bytes 9469968 | tf_op jit(solution)/shard_map/all_gather | solution.py:95
  403.6 12.7 fusion.56
  416.3 132.8 %all-gather.21.cloned.1.call-done = bf16[4352,1088]{1,0:T(8,128)(2,1)} async-done(((bf16[544,1088]{1,0:T(8,128)(2,1)}), bf16[4352,1088]{1,0:T(8,128)(2,1)}) %all-gather.21.cloned.1.call-update) | async-done | bytes 9469968 | tf_op jit(solution)/shard_map/all_gather | solution.py:97
  549.1 16.0 convert_reduce_fusion
  565.2 9.1 multiply_reduce_fusion.1
  579.2 31.1 %fusion.2 = f32[17,64,2048]{2,1,0:T(8,128)} fusion(bf16[512,17,64]{0,2,1:T(8,128)(2,1)S(1)} %bitcast.147, f32[17,512]{1,0:T(8,128)S(1)} %log_add_fusion, f32[17,512,2048]{2,1,0:T(8,128)} %get-tuple-element.146, pred[512,2048]{1,0:T(8,128)(4,1)S(1)} %fusion.14), kind=kOutput, calls=%fused_computation.8 | convolution fusion | flops 2353004544 | bytes 82413568 | tf_op jit(solution)/shard_map/while/body/eval_jaxpr/hqk,qhd->khd/dot_general | solution.py:201
  610.3 56.4 %multiply_reduce_fusion = (f32[17,512]{1,0:T(8,128)S(1)}, f32[17,512,2048]{2,1,0:T(8,128)}) fusion(f32[17,512]{1,0:T(8,128)S(1)} %log_add_fusion, f32[17,512,2048]{2,1,0:T(8,128)} %get-tuple-element.146, pred[512,2048]{1,0:T(8,128)(4,1)S(1)} %fusion.14, bf16[512,17,64]{0,2,1:T(8,128)(2,1)S(1)} %bitcast.148, bf16[2048,17,64]{0,2,1:T(8,128)(2,1)} %bitcast.139), kind=kOutput, calls=%fused_computation.1 | convolution fusion | flops 2370821632 | bytes 149295104 | tf_op jit(solution)/shard_map/while/body/eval_jaxpr/qhd,khd->hqk/dot_general | solution.py:183
  666.8 56.3 %multiply_convert_fusion = bf16[17,512,2048]{2,1,0:T(8,128)(2,1)} fusion(f32[17,512,2048]{2,1,0:T(8,128)} %get-tuple-element.151, f32[17,512]{1,0:T(8,128)S(1)} %get-tuple-element.150, f32[17,512]{1,0:T(8,128)S(1)} %log_add_fusion, f32[17,512,2048]{2,1,0:T(8,128)} %get-tuple-element.146, pred[512,2048]{1,0:T(8,128)(4,1)S(1)} %fusion.14), kind=kLoop, calls=%fused_computation | loop fusion | flops 106954752 | bytes 179376128 | tf_op jit(solution)/shard_map/while/body/eval_jaxpr/convert_element_type | solution.py:187
  723.0 21.0 %broadcast_multiply_fusion = f32[17,64,2048]{2,1,0:T(8,128)} fusion(bf16[512,17,64]{0,2,1:T(8,128)(2,1)S(1)} %bitcast.134, bf16[17,512,2048]{2,1,0:T(8,128)(2,1)} %multiply_convert_fusion), kind=kOutput, calls=%fused_computation.23 | convolution fusion | flops 2283929600 | bytes 45678592 | tf_op jit(solution)/shard_map/while/body/eval_jaxpr/hqk,qhd->khd/dot_general | solution.py:196
  745.7 14.2 fusion.55
  761.2 14.6 fusion.37
  782.2 19.4 convert_reduce_fusion.5
  804.4 13.2 reduce-scatter.21.cloned.1.call-done
  820.6 10.3 fusion.35
  831.0 303.2 %reduce-scatter.27.cloned.1.call-done = f32[136,4352]{1,0:T(8,128)} async-done(((f32[1088,4352]{1,0:T(8,128)}), f32[136,4352]{1,0:T(8,128)}) %reduce-scatter.27.cloned.1.call-update) | async-done | bytes 2367504 | tf_op jit(solution)/shard_map/reduce_scatter | solution.py:236
  1139.4 329.4 %reduce-scatter.29.cloned.1.call-done = f32[544,1088]{1,0:T(8,128)} async-done(((f32[4352,1088]{1,0:T(8,128)}), f32[544,1088]{1,0:T(8,128)}) %reduce-scatter.29.cloned.1.call-update) | async-done | bytes 2367504 | tf_op jit(solution)/shard_map/reduce_scatter | solution.py:238
  1472.2 99.7 %reduce-scatter.39.cloned.1.call-done = f32[136,1088]{1,0:T(8,128)} async-done(((f32[1088,1088]{1,0:T(8,128)}), f32[136,1088]{1,0:T(8,128)}) %reduce-scatter.39.cloned.1.call-update) | async-done | bytes 591888
  1574.5 234.4 %reduce-scatter.25.cloned.1.call-done = f32[136,3264]{1,0:T(8,128)} async-done(((f32[1088,3264]{1,0:T(8,128)}), f32[136,3264]{1,0:T(8,128)}) %reduce-scatter.25.cloned.1.call-update) | async-done | bytes 1775632 | tf_op jit(solution)/shard_map/reduce_scatter | solution.py:229
  1812.3 44.4 %reduce-scatter.35.cloned.1.call-done = f32[1088,136]{1,0:T(8,128)} async-done(((f32[4352,136]{1,0:T(8,128)}), f32[1088,136]{1,0:T(8,128)}) %reduce-scatter.35.cloned.1.call-update) | async-done | bytes 591888
  1859.2 35.8 %reduce-scatter.37.cloned.1.call-done = f32[272,544]{1,0:T(8,128)} async-done(((f32[1088,544]{1,0:T(8,128)}), f32[272,544]{1,0:T(8,128)}) %reduce-scatter.37.cloned.1.call-update) | async-done | bytes 591888
  1896.5 13.0 fusion.23
  1909.5 13.3 reduce-scatter.33.cloned.1.call-done
  1923.9 40.7 %reduce-scatter.31.cloned.1.call-done = f32[816,136]{1,0:T(8,128)} async-done(((f32[3264,136]{1,0:T(8,128)}), f32[816,136]{1,0:T(8,128)}) %reduce-scatter.31.cloned.1.call-update) | async-done | bytes 443920
  1989.4 38.1 %all-reduce.19 = (f32[1088]{0:T(1024)S(1)}, f32[1088]{0:T(1024)S(1)}, f32[1088]{0:T(1024)S(1)}, f32[1088]{0:T(1024)S(1)}, f32[1088]{0:T(1024)S(1)}, /*index=5*/f...) all-reduce(f32[1088]{0:T(1024)S(1)} %get-tuple-element.101, ...), channel_id=6, replica_groups=mesh['fsdp'=8,'context'=4] {'fsdp'}, use_global_device_ids=true, to_apply=%region_14.15.clone | all-reduce | flops 13056 | bytes 104448
  2028.2 11.7 all-reduce.20
  (222 shorter events, 113.6 us)
Async XLA Ops:
  7.2 53.9 %copy-start.4 = (bf16[1,512,1088]{1,2,0:T(8,128)(2,1)S(1)}, bf16[1,512,1088]{1,2,0:T(8,128)(2,1)}, u32[]{:S(2)}) copy-start(bf16[1,512,1088]{1,2,0:T(8,128)(2,1)} %param.16) | copy-start | bytes 3342340
  7.2 118.0 %all-gather.15.cloned.1.call-start = ((), (), s32[]{:S(2)}) async-start(), calls=%async_computation.10 | async-start | bytes 8146944 | tf_op jit(solution)/shard_map/all_gather | solution.py:88
  7.9 162.8 %all-gather.27.cloned.1.call-start = ((), (), s32[]{:S(2)}) async-start(), calls=%async_computation.21 | async-start | bytes 5570560 | tf_op jit(solution)/shard_map/all_gather | solution.py:114
  59.6 72.8 %copy-start.42 = (f32[1088]{0:T(1024)}, f32[1088]{0:T(1024)S(1)}, u32[]{:S(2)}) copy-start(f32[1088]{0:T(1024)S(1)} %convert_element_type.126) | copy-start | bytes 13060
  59.6 72.8 %copy-start.25 = (f32[1088]{0:T(1024)}, f32[1088]{0:T(1024)S(1)}, u32[]{:S(2)}) copy-start(f32[1088]{0:T(1024)S(1)} %convert_element_type.125) | copy-start | bytes 13060
  61.0 71.4 %copy-start.30 = (f32[512]{0:T(512)}, f32[512]{0:T(512)S(1)}, u32[]{:S(2)}) copy-start(f32[512]{0:T(512)S(1)} %broadcast_multiply_fusion.2) | copy-start | bytes 6148
  62.0 70.4 %copy-start.37 = (f32[512]{0:T(512)}, f32[512]{0:T(512)S(1)}, u32[]{:S(2)}) copy-start(f32[512]{0:T(512)S(1)} %fusion.44) | copy-start | bytes 6148
  136.4 86.8 %all-gather.25.cloned.1.call-start = ((), (), s32[]{:S(2)}) async-start(), calls=%async_computation.20 | async-start | bytes 5570560 | tf_op jit(solution)/shard_map/all_gather | solution.py:115
  140.1 124.4 %all-gather.17.cloned.1.call-start = ((), (), s32[]{:S(2)}) async-start(), calls=%async_computation.11 | async-start | bytes 2820096 | tf_op jit(solution)/shard_map/all_gather | solution.py:91
  140.7 262.9 %all-gather.19.cloned.1.call-start = ((), (), s32[]{:S(2)}) async-start(), calls=%async_computation.12 | async-start | bytes 10653696 | tf_op jit(solution)/shard_map/all_gather | solution.py:95
  141.3 407.8 %all-gather.21.cloned.1.call-start = ((), (), s32[]{:S(2)}) async-start(), calls=%async_computation.13 | async-start | bytes 11280384 | tf_op jit(solution)/shard_map/all_gather | solution.py:97
  141.9 659.8 %reduce-scatter.23.cloned.1.call-start = ((), (), s32[]{:S(2)}) async-start(), calls=%async_computation.15 | async-start | bytes 11141120 | tf_op jit(solution)/shard_map/reduce_scatter | solution.py:213
  264.5 139.1 %copy-start.19 = (f32[1088]{0:T(1024)S(1)}, f32[1088]{0:T(1024)}, u32[]{:S(2)}) copy-start(f32[1088]{0:T(1024)} %convert_element_type.137) | copy-start | bytes 13060
  264.5 139.1 %copy-start.21 = (f32[1088]{0:T(1024)S(1)}, f32[1088]{0:T(1024)}, u32[]{:S(2)}) copy-start(f32[1088]{0:T(1024)} %convert_element_type.138) | copy-start | bytes 13060
  268.6 305.7 %copy-start = (f32[512,1088]{0,1:T(8,128)}, f32[512,1088]{0,1:T(8,128)S(1)}, u32[]{:S(2)}) copy-start(f32[512,1088]{0,1:T(8,128)S(1)} %get-tuple-element.148) | copy-start | bytes 6684676
  268.7 305.6 %copy-start.23 = (f32[512]{0:T(512)}, f32[512]{0:T(512)S(1)}, u32[]{:S(2)}) copy-start(f32[512]{0:T(512)S(1)} %broadcast_multiply_fusion.1) | copy-start | bytes 6148
  269.0 305.3 %copy-start.27 = (f32[512]{0:T(512)}, f32[512]{0:T(512)S(1)}, u32[]{:S(2)}) copy-start(f32[512]{0:T(512)S(1)} %fusion.45) | copy-start | bytes 6148
  269.0 280.1 %copy-start.32 = (f32[4352]{0:T(1024)S(1)}, f32[4352]{0:T(1024)}, u32[]{:S(2)}) copy-start(f32[4352]{0:T(1024)} %convert_element_type.140) | copy-start | bytes 52228
  610.3 207.4 %reduce-scatter.21.cloned.1.call-start = ((), (), s32[]{:S(2)}) async-start(), calls=%async_computation.14 | async-start | bytes 11141120 | tf_op jit(solution)/shard_map/reduce_scatter | solution.py:212
  666.8 56.3 %copy-start.7 = (bf16[512,1088]{0,1:T(8,128)(2,1)S(1)}, bf16[512,1088]{0,1:T(8,128)(2,1)}, u32[]{:S(2)}) copy-start(bf16[512,1088]{0,1:T(8,128)(2,1)} %copy-done.6) | copy-start | bytes 3342340
  744.1 390.1 %reduce-scatter.27.cloned.1.call-start = ((), (), s32[]{:S(2)}) async-start(), calls=%async_computation.17 | async-start | bytes 21307392 | tf_op jit(solution)/shard_map/reduce_scatter | solution.py:236
  759.9 708.8 %reduce-scatter.29.cloned.1.call-start = ((), (), s32[]{:S(2)}) async-start(), calls=%async_computation.18 | async-start | bytes 22560768 | tf_op jit(solution)/shard_map/reduce_scatter | solution.py:238
  775.8 796.2 %reduce-scatter.39.cloned.1.call-start = ((), (), s32[]{:S(2)}) async-start(), calls=%async_computation.28 | async-start | bytes 5640192
  782.2 1026.7 %reduce-scatter.25.cloned.1.call-start = ((), (), s32[]{:S(2)}) async-start(), calls=%async_computation.16 | async-start | bytes 16293888 | tf_op jit(solution)/shard_map/reduce_scatter | solution.py:229
  830.9 1025.8 %reduce-scatter.35.cloned.1.call-start = ((), (), s32[]{:S(2)}) async-start(), calls=%async_computation.26 | async-start | bytes 5570560
  1139.0 756.1 %reduce-scatter.37.cloned.1.call-start = ((), (), s32[]{:S(2)}) async-start(), calls=%async_computation.27 | async-start | bytes 3481600
  1472.2 450.6 %reduce-scatter.33.cloned.1.call-start = ((), (), s32[]{:S(2)}) async-start(), calls=%async_computation.25 | async-start | bytes 1392640
  1574.4 390.2 %reduce-scatter.31.cloned.1.call-start = ((), (), s32[]{:S(2)}) async-start(), calls=%async_computation.24 | async-start | bytes 4177920
  1812.2 84.2 %copy-start.47 = (bf16[1088]{0:T(1024)(128)(2,1)S(1)}, bf16[1088]{0:T(1024)(128)(2,1)}, u32[]{:S(2)}) copy-start(bf16[1088]{0:T(1024)(128)(2,1)} %get-tuple-element.129) | copy-start | bytes 6532
  1812.3 227.7 %all-gather.31.cloned.1.call-start = ((), (), s32[]{:S(2)}) async-start(), calls=%async_computation.23 | async-start | bytes 3133440 | tf_op jit(solution)/shard_map/all_gather | solution.py:250
  1859.2 186.1 %all-gather.23.cloned.1.call-start = ((), (), s32[]{:S(2)}) async-start(), calls=%async_computation.19 | async-start | bytes 3481600 | tf_op jit(solution)/shard_map/all_gather | solution.py:251
  1895.1 153.6 %all-gather.29.cloned.1.call-start = ((), (), s32[]{:S(2)}) async-start(), calls=%async_computation.22 | async-start | bytes 2437120 | tf_op jit(solution)/shard_map/all_gather | solution.py:248
  (36 other events, 249.7 us)
Sparse Core Ops, SparseCore 0:
  10.2 114.8 all-gather.14
  136.5 34.1 all-gather.26
  172.9 35.9 all-gather.24
  210.9 53.5 all-gather.16
  266.6 137.0 all-gather.18
  405.6 143.4 all-gather.20
  610.4 73.2 reduce-scatter.22
  744.2 73.4 reduce-scatter.20
  821.3 312.8 reduce-scatter.26
  1138.5 330.2 reduce-scatter.28
  1472.9 99.0 reduce-scatter.38
  1575.5 233.3 reduce-scatter.24
  1811.4 45.2 reduce-scatter.34
  1859.3 35.7 reduce-scatter.36
  1897.4 25.3 reduce-scatter.32
  1925.4 39.1 reduce-scatter.30
  1966.0 24.8 all-gather.30
  1992.4 26.4 all-gather.22
  2020.5 22.0 all-gather.28
where the time goes:
time: 2070 us; the launch traced here: 2060 us
  waiting for transfers between devices  1480 us (71%)
  matrix products  302 us (15%)
  blocking collectives  99.9 us (5%)
  other arithmetic  98.6 us (5%)
  local copies, waits for them, and re-layouts  55.9 us (3%)
    reduce_scatter x1, waiting for transfers between devices, local(): lax.psum_scatter(grad_w_down, 'fsdp', scatter_dimension=0, tiled=True)  329 us
    reduce_scatter x1, waiting for transfers between devices, local(): lax.psum_scatter(grad_w_up, 'fsdp', scatter_dimension=0, tiled=True)  303 us
    unnamed x24, waiting for transfers between devices  236 us
    reduce_scatter x1, waiting for transfers between devices, local(): lax.psum_scatter(grad_w_qkv, 'fsdp', scatter_dimension=0, tiled=True)  234 us
    all_gather x1, waiting for transfers between devices, local(): lax.all_gather(w_up, 'fsdp', axis=0, tiled=True)  135 us
    all_gather x1, waiting for transfers between devices, local(): lax.all_gather(w_down, 'fsdp', axis=0, tiled=True)  133 us
    unnamed x2, blocking collectives  79.4 us
    all_gather x1, waiting for transfers between devices, local(): lax.all_gather(w_qkv, 'fsdp', axis=0, tiled=True)  63.1 us
  transfers between devices with their start and end apart: 19, of which 14 were waited for; matrix products, arithmetic and copies ran while one was open for 18% of the time, Pallas kernels for 0%

commit v1 on v0

--- a/solution.py
+++ b/solution.py
@@ -30,6 +30,205 @@
     return lax.dot_general(
         left, right, (((1,), (1,)), ((), ())), preferred_element_type=jnp.float32
     )
+
+class Links:
+    def __init__(self):
+        self.shards = lax.axis_size("fsdp")
+        self.places = lax.axis_size("context")
+        self.depth = self.shards // 2
+        self.shard = lax.axis_index("fsdp")
+        self.place = lax.axis_index("context")
+        self.z = self.shard // 2
+        self.x = self.shard % 2
+        self.core = self.place % 2
+        self.even = (self.place // 2) % 2 == 0
+
+    def swap(self, value, axis, bit):
+        count = lax.axis_size(axis)
+        return lax.ppermute(value, axis, [(i, i ^ bit) for i in range(count)])
+
+    def right(self, value, distance):
+        pairs = []
+        for z in range(self.depth - 1):
+            if z + 1 >= distance:
+                pairs += [(2 * z, 2 * z + 2), (2 * z + 1, 2 * z + 3)]
+        return lax.ppermute(value, "fsdp", pairs)
+
+    def left(self, value, distance):
+        pairs = []
+        for z in range(1, self.depth):
+            if z - 1 + distance < self.depth:
+                pairs += [(2 * z, 2 * z - 2), (2 * z + 1, 2 * z - 1)]
+        return lax.ppermute(value, "fsdp", pairs)
+
+    def block_at(self, k):
+        return lax.rem(self.z + k, self.depth)
+
+    def gather_pairs(self, mine):
+        rights, lefts = [mine], [mine]
+        for distance in range(1, self.depth):
+            rights.append(self.right(rights[-1], distance))
+            lefts.append(self.left(lefts[-1], distance))
+        pairs = []
+        for k in range(self.depth):
+            if k == 0:
+                block = mine
+            else:
+                block = jnp.where(self.z + k < self.depth, lefts[k], rights[self.depth - k])
+            other = self.swap(block, "fsdp", 1)
+            pairs.append(
+                jnp.stack(
+                    [jnp.where(self.x == 0, block, other), jnp.where(self.x == 0, other, block)]
+                )
+            )
+        return pairs
+
+    def reduce_line(self, blocks):
+        from_left, from_right = None, None
+        for distance in range(self.depth - 1, 0, -1):
+            going_right = blocks[distance].astype(jnp.float32)
+            going_left = blocks[self.depth - distance].astype(jnp.float32)
+            if from_left is not None:
+                going_right = going_right + from_left.astype(jnp.float32)
+                going_left = going_left + from_right.astype(jnp.float32)
+            right_pairs, left_pairs = [], []
+            for z in range(self.depth - distance):
+                right_pairs += [(2 * z, 2 * z + 2), (2 * z + 1, 2 * z + 3)]
+            for z in range(distance, self.depth):
+                left_pairs += [(2 * z, 2 * z - 2), (2 * z + 1, 2 * z - 1)]
+            from_left = lax.ppermute(going_right.astype(jnp.bfloat16), "fsdp", right_pairs)
+            from_right = lax.ppermute(going_left.astype(jnp.bfloat16), "fsdp", left_pairs)
+        total = blocks[0].astype(jnp.float32)
+        if from_left is not None:
+            total = total + from_left.astype(jnp.float32) + from_right.astype(jnp.float32)
+        return total
+
+    def sum_same_parity(self, value):
+        bit = 4
+        while bit < self.places:
+            value = add_low(value, self.swap(value, "context", bit))
+            bit *= 2
+        return value
+
+
+def add_low(left, right):
+    return (left.astype(jnp.float32) + right.astype(jnp.float32)).astype(jnp.bfloat16)
+
+
+def set_at(buffer, block, *at):
+    at = at + (0,) * (buffer.ndim - len(at))
+    return lax.dynamic_update_slice(buffer, block, tuple(jnp.asarray(i, jnp.int32) for i in at))
+
+
+def quarters(shard, features):
+    return jnp.stack([shard[:, j * features : (j + 1) * features] for j in range(4)])
+
+
+def gather_first(links, w_qkv, w_out):
+    rows, features = w_out.shape
+    own = quarters(jnp.concatenate([w_qkv, w_out], axis=1), features)
+    mine = lax.dynamic_slice_in_dim(own, 2 * links.core, 2, 0)
+    full = jnp.zeros((4, links.shards, rows, features), jnp.bfloat16)
+    for k, pair in enumerate(links.gather_pairs(mine)):
+        block = pair.transpose(1, 0, 2, 3)
+        other = links.swap(block, "context", 1)
+        at = 2 * links.block_at(k)
+        full = set_at(full, block, 2 * links.core, at)
+        full = set_at(full, other, 2 - 2 * links.core, at)
+    return full.reshape(4, links.shards * rows, features)
+
+
+def gather_second(links, w_up, w_down):
+    rows = w_up.shape[0]
+    features = w_down.shape[1]
+    own_up = lax.dynamic_slice_in_dim(quarters(w_up, features), 2 * links.core, 2, 0)
+    own_down = lax.dynamic_index_in_dim(
+        w_down.reshape(2, 2, rows, features), links.core, 0, keepdims=False
+    )
+    mine = jnp.where(links.even, own_up, own_down)
+    up = jnp.zeros((4, links.shards, rows, features), jnp.bfloat16)
+    down = jnp.zeros((links.shards, 2, 2, rows, features), jnp.bfloat16)
+    for k, pair in enumerate(links.gather_pairs(mine)):
+        other = links.swap(pair, "context", 2)
+        up_half = jnp.where(links.even, pair, other).transpose(1, 0, 2, 3)
+        down_half = jnp.where(links.even, other, pair)
+        up_other = links.swap(up_half, "context", 1)
+        down_other = links.swap(down_half, "context", 1)
+        at = 2 * links.block_at(k)
+        up = set_at(up, up_half, 2 * links.core, at)
+        up = set_at(up, up_other, 2 - 2 * links.core, at)
+        down = set_at(down, down_half[:, None], at, links.core)
+        down = set_at(down, down_other[:, None], at, 1 - links.core)
+    return (
+        up.reshape(4, links.shards * rows, features),
+        down.reshape(4 * links.shards * rows, features),
+    )
+
+
+def other_x(links, block):
+    sent = lax.dynamic_index_in_dim(block, 1 - links.x, 0, keepdims=False)
+    kept = lax.dynamic_index_in_dim(block, links.x, 0, keepdims=False)
+    return add_low(kept, links.swap(sent, "fsdp", 1))
+
+
+def reduce_second(links, grad_up, grad_down):
+    features = grad_down.shape[1]
+    rows = features // links.shards
+    up = grad_up.reshape(2, 2, links.depth, 2, rows, features)
+    down = grad_down.reshape(links.depth, 2, 2, 2, rows, features)
+    blocks = []
+    for k in range(links.depth):
+        at = links.block_at(k)
+        up_k = lax.dynamic_index_in_dim(up, at, 2, keepdims=False).transpose(0, 2, 1, 3, 4)
+        down_k = lax.dynamic_index_in_dim(down, at, 0, keepdims=False).transpose(1, 0, 2, 3, 4)
+        both = jnp.stack([up_k, down_k])
+        sent = lax.dynamic_index_in_dim(both, 1 - links.core, 1, keepdims=False)
+        kept = lax.dynamic_index_in_dim(both, links.core, 1, keepdims=False)
+        halves = add_low(kept, links.swap(sent, "context", 1))
+        sent = jnp.where(links.even, halves[1], halves[0])
+        kept = jnp.where(links.even, halves[0], halves[1])
+        block = add_low(kept, links.swap(sent, "context", 2))
+        block = links.sum_same_parity(block)
+        blocks.append(other_x(links, block))
+    mine = links.reduce_line(blocks).astype(jnp.bfloat16)
+    other = links.swap(mine, "context", 2)
+    up_half = jnp.where(links.even, mine, other)
+    down_half = jnp.where(links.even, other, mine)
+    both = jnp.stack([up_half, down_half])
+    return join_cores(links, both)
+
+
+def join_cores(links, half):
+    other = links.swap(half, "context", 1)
+    first = jnp.where(links.core == 0, half, other)
+    last = jnp.where(links.core == 0, other, half)
+    return jnp.concatenate([first, last], axis=-3).astype(jnp.float32)
+
+
+def reduce_first(links, grads):
+    features = grads.shape[1]
+    rows = features // links.shards
+    split = grads.reshape(2, 2, links.depth, 2, rows, features)
+    blocks = []
+    for k in range(links.depth):
+        part = lax.dynamic_index_in_dim(split, links.block_at(k), 2, keepdims=False)
+        part = part.transpose(0, 2, 1, 3, 4)
+        sent = lax.dynamic_index_in_dim(part, 1 - links.core, 0, keepdims=False)
+        kept = lax.dynamic_index_in_dim(part, links.core, 0, keepdims=False)
+        blocks.append(other_x(links, add_low(kept, links.swap(sent, "context", 1))))
+    mine = links.reduce_line(blocks).astype(jnp.bfloat16)
+    mine = add_low(mine, links.swap(mine, "context", 2))
+    mine = links.sum_same_parity(mine)
+    return join_cores(links, mine)
+
+
+def sum_everywhere(links, value):
+    for axis, count in (("context", links.places), ("fsdp", links.shards)):
+        bit = 1
+        while bit < count:
+            value = value + links.swap(value, axis, bit)
+            bit *= 2
+    return value
 
 
 def score_table(query_rows, key_rows, query_segs, key_segs, query_place, key_place, head_count):
@@ -68,45 +267,41 @@
     length_all = stretch * lax.axis_size("context")
     offset = lax.axis_index("context") * stretch
     tokens = sequences * stretch
+    links = Links()
+    small = (
+        ln1_gain, ln1_bias, bias_query, bias_value, bias_out, ln2_gain, ln2_bias, bias_down, bias_up
+    )
+    small_all = lax.all_gather(jnp.concatenate(small), "fsdp", axis=0)
+    small_full, start = [], 0
+    for vector in small:
+        small_full.append(small_all[:, start : start + vector.shape[0]].reshape(-1))
+        start += vector.shape[0]
     (
         gain_one,
         shift_one,
-        full_qkv,
         query_bias,
         value_bias,
-        full_out,
         out_bias,
         gain_two,
         shift_two,
-        full_up,
+        down_bias,
         up_bias,
-        full_down,
-        down_bias,
-    ) = (
-        lax.all_gather(ln1_gain, "fsdp", axis=0, tiled=True),
-        lax.all_gather(ln1_bias, "fsdp", axis=0, tiled=True),
-        lax.all_gather(w_qkv, "fsdp", axis=0, tiled=True),
-        lax.all_gather(bias_query, "fsdp", axis=0, tiled=True),
-        lax.all_gather(bias_value, "fsdp", axis=0, tiled=True),
-        lax.all_gather(w_out, "fsdp", axis=0, tiled=True),
-        lax.all_gather(bias_out, "fsdp", axis=0, tiled=True),
-        lax.all_gather(ln2_gain, "fsdp", axis=0, tiled=True),
-        lax.all_gather(ln2_bias, "fsdp", axis=0, tiled=True),
-        lax.all_gather(w_up, "fsdp", axis=0, tiled=True),
-        lax.all_gather(bias_up, "fsdp", axis=0, tiled=True),
-        lax.all_gather(w_down, "fsdp", axis=0, tiled=True),
-        lax.all_gather(bias_down, "fsdp", axis=0, tiled=True),
-    )
+    ) = small_full
+    full_first = gather_first(links, w_qkv, w_out)
+    full_up, full_down = gather_second(links, w_up, w_down)
+    full_out = full_first[3]
     gain_one = gain_one.astype(jnp.float32)
     shift_one = shift_one.astype(jnp.float32)
     gain_two = gain_two.astype(jnp.float32)
     shift_two = shift_two.astype(jnp.float32)
     inputs = block_input.reshape(tokens, features).astype(jnp.float32)
     normed = normalize(inputs, gain_one, shift_one).astype(jnp.bfloat16)
-    stacked = jnp.dot(normed, full_qkv, preferred_element_type=jnp.float32)
-    queries = (stacked[:, :features] + query_bias.astype(jnp.float32)).astype(jnp.bfloat16)
-    keys_own = stacked[:, features : 2 * features].astype(jnp.bfloat16)
-    values_own = (stacked[:, 2 * features :] + value_bias.astype(jnp.float32)).astype(jnp.bfloat16)
+    queries, keys_own, values_own = (
+        jnp.dot(normed, full_first[j], preferred_element_type=jnp.float32) for j in range(3)
+    )
+    queries = (queries + query_bias.astype(jnp.float32)).astype(jnp.bfloat16)
+    keys_own = keys_own.astype(jnp.bfloat16)
+    values_own = (values_own + value_bias.astype(jnp.float32)).astype(jnp.bfloat16)
     query_seqs = queries.reshape(sequences, stretch, features)
     key_seqs = keys_own.reshape(sequences, stretch, features)
     value_seqs = values_own.reshape(sequences, stretch, features)
@@ -142,9 +337,10 @@
         + out_bias.astype(jnp.float32)
     )
     normed_two = normalize(middle, gain_two, shift_two).astype(jnp.bfloat16)
-    pre_act = jnp.dot(normed_two, full_up, preferred_element_type=jnp.float32) + up_bias.astype(
-        jnp.float32
-    )
+    pre_act = jnp.concatenate(
+        [jnp.dot(normed_two, full_up[j], preferred_element_type=jnp.float32) for j in range(4)],
+        axis=1,
+    ) + up_bias.astype(jnp.float32)
     hidden = gelu_tanh(pre_act).astype(jnp.bfloat16)
     result = (
         middle
@@ -154,14 +350,22 @@
     block_output = result.astype(jnp.bfloat16).reshape(block_input.shape)
     grad_out = cotangent.reshape(tokens, features)
     grad_out_f = grad_out.astype(jnp.float32)
-    grad_w_down = contract_rows(hidden, grad_out)
+    grad_w_down = contract_rows(hidden, grad_out).astype(jnp.bfloat16)
     grad_b_down = jnp.sum(grad_out_f, axis=0)
     grad_hidden = contract_cols(grad_out, full_down)
     gelu_value, gelu_pull = jax.vjp(gelu_tanh, pre_act)
     grad_pre = gelu_pull(grad_hidden)[0].astype(jnp.bfloat16)
-    grad_w_up = contract_rows(normed_two, grad_pre)
+    grad_w_up = jnp.stack(
+        [
+            contract_rows(normed_two, grad_pre[:, j * features : (j + 1) * features])
+            for j in range(4)
+        ]
+    ).astype(jnp.bfloat16)
+    second_sums = reduce_second(links, grad_w_up, grad_w_down)
     grad_b_up = jnp.sum(grad_pre.astype(jnp.float32), axis=0)
-    grad_normed_two = contract_cols(grad_pre, full_up)
+    grad_normed_two = sum(
+        contract_cols(grad_pre[:, j * features : (j + 1) * features], full_up[j]) for j in range(4)
+    )
     norm_value, norm_pull = jax.vjp(normalize, middle, gain_two, shift_two)
     grad_middle_part, grad_gain_two, grad_shift_two = norm_pull(grad_normed_two)
     grad_middle = grad_out_f + grad_middle_part
@@ -204,7 +408,7 @@
             grad_heads,
             preferred_element_type=jnp.float32,
         ).reshape(length_all, features)
-        return (grad_query, key_part, value_part)
+        return (grad_query, key_part.astype(jnp.bfloat16), value_part.astype(jnp.bfloat16))
 
     local_items = (query_seqs, keys_all, values_all, grad_att_seqs, own_segs, segment_ids, lse_kept)
     grad_queries, key_parts, value_parts = lax.map(local_grads, local_items)
@@ -215,71 +419,56 @@
     grad_queries = grad_queries.reshape(tokens, features).astype(jnp.bfloat16)
     grad_keys = grad_keys.reshape(tokens, features).astype(jnp.bfloat16)
     grad_values = grad_values.reshape(tokens, features).astype(jnp.bfloat16)
-    grad_stacked = jnp.concatenate([grad_queries, grad_keys, grad_values], axis=1)
-    grad_w_qkv = contract_rows(normed, grad_stacked)
+    grads_first = jnp.stack(
+        [contract_rows(normed, part) for part in (grad_queries, grad_keys, grad_values)]
+        + [grad_w_out]
+    ).astype(jnp.bfloat16)
+    first_sums = reduce_first(links, grads_first)
     grad_b_query = jnp.sum(grad_queries.astype(jnp.float32), axis=0)
     grad_b_value = jnp.sum(grad_values.astype(jnp.float32), axis=0)
-    grad_normed = contract_cols(grad_stacked, full_qkv)
+    grad_normed = (
+        contract_cols(grad_queries, full_first[0])
+        + contract_cols(grad_keys, full_first[1])
+        + contract_cols(grad_values, full_first[2])
+    )
     first_value, first_pull = jax.vjp(normalize, inputs, gain_one, shift_one)
     grad_input_part, grad_gain_one, grad_shift_one = first_pull(grad_normed)
     input_grad = (grad_middle + grad_input_part).reshape(block_input.shape)
-    shares = (
-        lax.psum_scatter(grad_gain_one, "fsdp", scatter_dimension=0, tiled=True),
-        lax.psum_scatter(grad_shift_one, "fsdp", scatter_dimension=0, tiled=True),
-        lax.psum_scatter(grad_w_qkv, "fsdp", scatter_dimension=0, tiled=True),
-        lax.psum_scatter(grad_b_query, "fsdp", scatter_dimension=0, tiled=True),
-        lax.psum_scatter(grad_b_value, "fsdp", scatter_dimension=0, tiled=True),
-        lax.psum_scatter(grad_w_out, "fsdp", scatter_dimension=0, tiled=True),
-        lax.psum_scatter(grad_b_out, "fsdp", scatter_dimension=0, tiled=True),
-        lax.psum_scatter(grad_gain_two, "fsdp", scatter_dimension=0, tiled=True),
-        lax.psum_scatter(grad_shift_two, "fsdp", scatter_dimension=0, tiled=True),
-        lax.psum_scatter(grad_w_up, "fsdp", scatter_dimension=0, tiled=True),
-        lax.psum_scatter(grad_b_up, "fsdp", scatter_dimension=0, tiled=True),
-        lax.psum_scatter(grad_w_down, "fsdp", scatter_dimension=0, tiled=True),
-        lax.psum_scatter(grad_b_down, "fsdp", scatter_dimension=0, tiled=True),
-    )
-    column_parts = (
-        lax.psum_scatter(shares[2], "context", scatter_dimension=1, tiled=True),
-        lax.psum_scatter(shares[5], "context", scatter_dimension=1, tiled=True),
-        lax.psum_scatter(shares[9], "context", scatter_dimension=1, tiled=True),
-        lax.psum_scatter(shares[11], "context", scatter_dimension=1, tiled=True),
-    )
-    matrices = (
-        lax.all_gather(column_parts[0], "context", axis=1, tiled=True),
-        lax.all_gather(column_parts[1], "context", axis=1, tiled=True),
-        lax.all_gather(column_parts[2], "context", axis=1, tiled=True),
-        lax.all_gather(column_parts[3], "context", axis=1, tiled=True),
-    )
-    vectors = lax.psum(
-        (
-            shares[0],
-            shares[1],
-            shares[3],
-            shares[4],
-            shares[6],
-            shares[7],
-            shares[8],
-            shares[10],
-            shares[12],
-        ),
-        "context",
-    )
+    vectors = (
+        grad_gain_one,
+        grad_shift_one,
+        grad_b_query,
+        grad_b_value,
+        grad_b_out,
+        grad_gain_two,
+        grad_shift_two,
+        grad_b_down,
+        grad_b_up,
+    )
+    vector_sums = sum_everywhere(links, jnp.concatenate(vectors))
+    mine, start = [], 0
+    for vector in vectors:
+        size = vector.shape[0]
+        own = size // links.shards
+        mine.append(lax.dynamic_slice_in_dim(vector_sums, start + links.shard * own, own, 0))
+        start += size
+    up_sum, down_sum = second_sums[0], second_sums[1]
     return (
         block_output,
         input_grad,
-        vectors[0],
-        vectors[1],
-        matrices[0],
-        vectors[2],
-        vectors[3],
-        matrices[1],
-        vectors[4],
-        vectors[5],
-        vectors[6],
-        matrices[2],
-        vectors[7],
-        matrices[3],
-        vectors[8],
+        mine[0],
+        mine[1],
+        jnp.concatenate([first_sums[j] for j in range(3)], axis=1),
+        mine[2],
+        mine[3],
+        first_sums[3],
+        mine[4],
+        mine[5],
+        mine[6],
+        jnp.concatenate([up_sum[j] for j in range(4)], axis=1),
+        mine[8],
+        down_sum.reshape(-1, features),
+        mine[7],
     )
 
 

time: 2070 us -> 1040 us (0.50)
  waiting for transfers between devices: 1480 us -> 239 us
  starting transfers between devices: 1.39 us -> 114 us
  other arithmetic: 98.6 us -> 191 us
  local copies, waits for them, and re-layouts: 55.9 us -> 117 us
  blocking collectives: 99.9 us -> 46.3 us
    reduce_scatter x3 -> x0, waiting for transfers between devices: 867 us -> none  [the longest x1 329 us: local(): lax.psum_scatter(grad_w_down, 'fsdp', scatter_dimension=0, tiled=True)]
    all_gather x7 -> x0, waiting for transfers between devices: 342 us -> none  [the longest x1 135 us: local(): lax.all_gather(w_up, 'fsdp', axis=0, tiled=True)]
    ppermute x0 -> x77, waiting for transfers between devices: none -> 239 us  [the longest x53 183 us: swap(): return lax.ppermute(value, axis, [(i, i ^ bit) for i in range(count)])]
    unnamed x24 -> x4, waiting for transfers between devices: 236 us -> 0.07 us
    ppermute x0 -> x77, starting transfers between devices: none -> 113 us  [the longest x53 53.1 us: swap(): return lax.ppermute(value, axis, [(i, i ^ bit) for i in range(count)])]
    unnamed x2 -> x1, blocking collectives: 79.4 us -> 46.3 us
    another operation x0 -> x17, other arithmetic: none -> 27.5 us  [the longest x12 13.4 us: gather_pairs(): jnp.stack([jnp.where(self.x == 0, block, other), jnp.where(self.x == 0, o...]
    unnamed x137 -> x283, local copies, waits for them, and re-layouts: 50.1 us -> 24.3 us
  transfers between devices with their start and end apart: 19 -> 81, of which waited for: 14 -> 23; matrix products, arithmetic and copies ran while one was open for 18% -> 32% of each run, Pallas kernels for 0% -> 0%
where the time goes in v1:
time: 1040 us; the launch traced here: 1030 us
  matrix products  304 us (29%)
  waiting for transfers between devices  239 us (23%)
  other arithmetic  191 us (18%)
  local copies, waits for them, and re-layouts  117 us (11%)
  starting transfers between devices  114 us (11%)
  blocking collectives  46.3 us (4%)
  between operations  17.1 us (2%)
    ppermute x53, waiting for transfers between devices, swap(): return lax.ppermute(value, axis, [(i, i ^ bit) for i in range(count)])  183 us
    convert_element_type x1, other arithmetic, local_grads(): (probs * (grad_probs - deltas[:, :, None])).astype(jnp.bfloat16)  59.5 us
    dot_general x1, matrix products, local_grads(): jnp.einsum('qhd,khd->hqk', grad_heads, value_heads, preferred_element_typ...  54.6 us
    ppermute x53, starting transfers between devices, swap(): return lax.ppermute(value, axis, [(i, i ^ bit) for i in range(count)])  53.1 us
    unnamed x1, blocking collectives  46.3 us
    dot_general x9, matrix products, contract_rows(): lax.dot_general(left, right, (((0,), (0,)), ((), ())), preferred_element_...  44.6 us
    dot_general x9, matrix products, contract_cols(): lax.dot_general(left, right, (((1,), (1,)), ((), ())), preferred_element_...  41.5 us
    ppermute x6, waiting for transfers between devices, left(): return lax.ppermute(value, 'fsdp', pairs)  36.5 us
  transfers between devices with their start and end apart: 81, of which 23 were waited for; matrix products, arithmetic and copies ran while one was open for 32% of the time, Pallas kernels for 0%

profile of v1, /device:TPU:0, one launch (start us, length us, event | category | flops | bytes accessed | tf_op | source)
XLA Modules:
  0.0 1028.5 jit_solution(2305736303606019918)
XLA Ops:
  30.9 46.3 %all-reduce = bf16[13056]{0:T(1024)(128)(2,1)S(1)} all-reduce(bf16[13056]{0:T(1024)(128)(2,1)S(1)} %dynamic-update-slice), channel_id=2, replica_groups=mesh['fsdp'=8,'context'=4] {'fsdp'}, use_global_device_ids=true, to_apply=%add | all-reduce | flops 13056 | bytes 52224
  94.0 5.8 collective-permute-done.17
  111.7 9.1 collective-permute-done.24
  122.9 10.5 %collective-permute-done.11 = bf16[2,136,1088]{2,1,0:T(8,128)(2,1)S(1)} collective-permute-done((bf16[2,136,1088]{2,1,0:T(8,128)(2,1)S(1)}, bf16[2,136,1088]{2,1,0:T(8,128)(2,1)S(1)}, u32[]{:S(2)}, u32[]{:S(2)}) %collective-permute-start.11) | collective-permute-done | bytes 591904 | tf_op jit(solution)/shard_map/ppermute | solution.py:62
  145.1 6.0 collective-permute-done.28
  173.6 9.0 collective-permute-done.21
  201.2 28.2 %collective-permute-done.22 = bf16[2,2,136,1088]{3,2,1,0:T(8,128)(2,1)} collective-permute-done((bf16[2,2,136,1088]{3,2,1,0:T(8,128)(2,1)}, bf16[2,2,136,1088]{3,2,1,0:T(8,128)(2,1)}, u32[]{:S(2)}, u32[]{:S(2)}) %collective-permute-start.22) | collective-permute-done | bytes 1183776 | tf_op jit(solution)/shard_map/ppermute | solution.py:48
  252.1 16.0 %collective-permute-done.30 = bf16[2,2,136,1088]{3,2,1,0:T(8,128)(2,1)S(1)} collective-permute-done((bf16[2,2,136,1088]{3,2,1,0:T(8,128)(2,1)S(1)}, bf16[2,2,136,1088]{3,2,1,0:T(8,128)(2,1)S(1)}, u32[]{:S(2)}, u32[]{:S(2)}) %collective-permute-start.30) | collective-permute-done | bytes 1183776 | tf_op jit(solution)/shard_map/ppermute | solution.py:48
  280.7 8.1 fusion.139
  290.5 27.7 %fusion.6 = (f32[17,512]{1,0:T(8,128)S(1)}, f32[17,512,2048]{2,1,0:T(8,128)}) fusion(pred[512,2048]{1,0:T(8,128)(4,1)S(1)} %fusion.29, bf16[512,17,64]{0,2,1:T(8,128)(2,1)S(1)} %bitcast.546, bf16[2048,17,64]{0,2,1:T(8,128)(2,1)} %bitcast.526), kind=kOutput, calls=%fused_computation.11 | convolution fusion | flops 2335170048 | bytes 77957120 | tf_op jit(solution)/shard_map/while/body/eval_jaxpr/qhd,khd->hqk/dot_general | solution.py:238
  318.1 22.8 %fusion = f32[17,512]{1,0:T(8,128)S(1)} fusion(f32[17,512]{1,0:T(8,128)S(1)} %get-tuple-element.194, f32[17,512,2048]{2,1,0:T(8,128)} %get-tuple-element.195, pred[512,2048]{1,0:T(8,128)(4,1)S(1)} %fusion.29), kind=kLoop, calls=%fused_computation.6 | loop fusion | flops 71294464 | bytes 72421376 | tf_op jit(solution)/shard_map/while/body/eval_jaxpr/reduce_sum | solution.py:323
  341.6 28.9 %fusion.79 = bf16[17,64,512]{2,1,0:T(8,128)(2,1)S(1)} fusion(bf16[2048,17,64]{0,2,1:T(8,128)(2,1)} %bitcast.547, f32[17,512]{1,0:T(8,128)} %copy-done.101, f32[17,512]{1,0:T(8,128)} %copy-done.99, f32[17,512,2048]{2,1,0:T(8,128)} %get-tuple-element.195, pred[512,2048]{1,0:T(8,128)(4,1)S(1)} %fusion.29), kind=kOutput, calls=%fused_computation.169 | convolution fusion | flops 2371387392 | bytes 77991936 | tf_op jit(solution)/shard_map/while/body/eval_jaxpr/hqk,khd->qhd/dot_general | solution.py:326
  387.4 20.4 %convert_reduce_fusion = (f32[4352]{0:T(1024)}, bf16[512,4352]{0,1:T(8,128)(2,1)}) fusion(f32[4352]{0:T(1024)S(1)} %copy-done.113, f32[512,1088]{0,1:T(8,128)} %fusion.146, f32[512,1088]{0,1:T(8,128)} %fusion.145, f32[512,1088]{0,1:T(8,128)} %fusion.144, f32[512,1088]{0,1:T(8,128)} %fusion.143, bf16[4352,1088]{1,0:T(8,128)(2,1)} %bitcast.68, ...), kind=kOutput, calls=%fused_computation.30 | convolution fusion | flops 4906545152 | bytes 23988224 | tf_op jit(solution)/shard_map/dot_general | solution.py:30
  419.0 13.9 %convolution_convert_fusion = bf16[4352,1088]{0,1:T(8,128)(2,1)} fusion(bf16[1,512,1088]{1,2,0:T(8,128)(2,1)} %param.31, f32[512,1088]{0,1:T(8,128)} %fusion.146, f32[512,1088]{0,1:T(8,128)} %fusion.145, f32[512,1088]{0,1:T(8,128)} %fusion.144, f32[512,1088]{0,1:T(8,128)} %fusion.143, f32[4352]{0:T(1024)S(1)} %copy-done.113), kind=kOutput, calls=%fused_computation.12 | convolution fusion | flops 4882317312 | bytes 19514368 | tf_op jit(solution)/shard_map/dot_general | solution.py:24
  456.8 30.4 %fusion.30 = bf16[17,64,2048]{2,1,0:T(8,128)(2,1)} fusion(bf16[512,17,64]{0,2,1:T(8,128)(2,1)S(1)} %bitcast.574, f32[17,512]{1,0:T(8,128)S(1)} %copy-done.93, f32[17,512,2048]{2,1,0:T(8,128)} %get-tuple-element.195, pred[512,2048]{1,0:T(8,128)(4,1)S(1)} %fusion.29), kind=kOutput, calls=%fused_computation.75 | convolution fusion | flops 2355232768 | bytes 77957120 | tf_op jit(solution)/shard_map/while/body/eval_jaxpr/hqk,qhd->khd/dot_general | solution.py:405
  487.2 54.6 %multiply_reduce_fusion = (f32[17,512]{1,0:T(8,128)}, f32[17,512,2048]{2,1,0:T(8,128)}) fusion(f32[17,512]{1,0:T(8,128)S(1)} %copy-done.93, f32[17,512,2048]{2,1,0:T(8,128)} %get-tuple-element.195, pred[512,2048]{1,0:T(8,128)(4,1)S(1)} %fusion.29, bf16[512,17,64]{0,2,1:T(8,128)(2,1)S(1)} %bitcast.575, bf16[2048,17,64]{0,2,1:T(8,128)(2,1)} %bitcast.548), kind=kOutput, calls=%fused_computation.1 | convolution fusion | flops 2370821632 | bytes 149295104 | tf_op jit(solution)/shard_map/while/body/eval_jaxpr/qhd,khd->hqk/dot_general | solution.py:387
  541.8 14.0 %copy.85 = bf16[4352,1088]{1,0:T(8,128)(2,1)} copy(bf16[4352,1088]{0,1:T(8,128)(2,1)} %convolution_convert_fusion) | data formatting | bytes 18939904 | tf_op jit(solution)/shard_map/convert_element_type | solution.py:353
  555.8 6.2 dynamic-slice_bitcast_fusion.3
  575.2 7.2 constant_dynamic-slice_fusion.3
  598.3 59.5 %multiply_convert_fusion = bf16[17,512,2048]{2,1,0:T(8,128)(2,1)} fusion(f32[17,512,2048]{2,1,0:T(8,128)} %get-tuple-element.200, f32[17,512]{1,0:T(8,128)} %get-tuple-element.199, f32[17,512]{1,0:T(8,128)} %log_add_fusion, f32[17,512,2048]{2,1,0:T(8,128)} %get-tuple-element.195, pred[512,2048]{1,0:T(8,128)(4,1)S(1)} %fusion.29), kind=kLoop, calls=%fused_computation | loop fusion | flops 106954752 | bytes 179376128 | tf_op jit(solution)/shard_map/while/body/eval_jaxpr/convert_element_type | solution.py:391
  657.8 20.0 %multiply_convert_fusion.1 = bf16[17,64,2048]{2,1,0:T(8,128)(2,1)} fusion(bf16[512,17,64]{0,2,1:T(8,128)(2,1)} %bitcast.545, bf16[17,512,2048]{2,1,0:T(8,128)(2,1)} %multiply_convert_fusion), kind=kOutput, calls=%fused_computation.31 | convolution fusion | flops 2286157824 | bytes 41222144 | tf_op jit(solution)/shard_map/while/body/eval_jaxpr/hqk,qhd->khd/dot_general | solution.py:400
  692.9 69.4 %collective-permute-done.67 = bf16[2,2,136,1088]{3,2,1,0:T(8,128)(2,1)S(1)} collective-permute-done((bf16[2,2,136,1088]{3,2,1,0:T(8,128)(2,1)S(1)}, bf16[2,2,136,1088]{3,2,1,0:T(8,128)(2,1)S(1)}, u32[]{:S(2)}, u32[]{:S(2)}) %collective-permute-start.67) | collective-permute-done | bytes 1183776 | tf_op jit(solution)/shard_map/ppermute | solution.py:48
  765.6 14.4 %collective-permute-done.68 = bf16[2,136,1088]{2,1,0:T(8,128)(2,1)S(1)} collective-permute-done((bf16[2,136,1088]{2,1,0:T(8,128)(2,1)S(1)}, bf16[2,136,1088]{2,1,0:T(8,128)(2,1)S(1)}, u32[]{:S(2)}, u32[]{:S(2)}) %collective-permute-start.68) | collective-permute-done | bytes 591904 | tf_op jit(solution)/shard_map/ppermute | solution.py:48
  812.9 14.6 %collective-permute-done.58 = bf16[2,2,136,1088]{3,2,1,0:T(8,128)(2,1)} collective-permute-done((bf16[2,2,136,1088]{3,2,1,0:T(8,128)(2,1)}, bf16[2,2,136,1088]{3,2,1,0:T(8,128)(2,1)}, u32[]{:S(2)}, u32[]{:S(2)}) %collective-permute-start.58) | collective-permute-done | bytes 1183776 | tf_op jit(solution)/shard_map/ppermute | solution.py:48
  839.0 18.2 %convert_reduce_fusion.5 = (f32[17,64]{1,0:T(8,128)S(1)}, bf16[17,64,512]{2,1,0:T(8,128)(2,1)S(1)}) fusion(bf16[2048,17,64]{0,2,1:T(8,128)(2,1)} %bitcast.527, bf16[17,512,2048]{2,1,0:T(8,128)(2,1)} %multiply_convert_fusion), kind=kOutput, calls=%fused_computation.159 | convolution fusion | flops 2283928576 | bytes 41226496 | tf_op jit(solution)/shard_map/while/body/eval_jaxpr/hqk,khd->qhd/dot_general | solution.py:393
  899.4 14.6 %collective-permute-done.48 = bf16[2,136,1088]{2,1,0:T(8,128)(2,1)S(1)} collective-permute-done((bf16[2,136,1088]{2,1,0:T(8,128)(2,1)S(1)}, bf16[2,136,1088]{2,1,0:T(8,128)(2,1)S(1)}, u32[]{:S(2)}, u32[]{:S(2)}) %collective-permute-start.48) | collective-permute-done | bytes 591904 | tf_op jit(solution)/shard_map/ppermute | solution.py:48
  914.1 7.9 collective-permute-start.49
  939.5 7.3 collective-permute-done.50
  963.4 5.8 collective-permute-start.51
  971.5 15.6 %fusion.46 = bf16[1,512,1088]{1,2,0:T(8,128)(2,1)} fusion(f32[512,1088]{0,1:T(8,128)S(1)} %copy-done.1, bf16[4352,1088]{1,0:T(8,128)(2,1)} %bitcast.68, f32[1088]{0:T(1024)S(1)} %reshape.635, f32[512,1088]{0,1:T(8,128)} %fusion.146, f32[512,1088]{0,1:T(8,128)} %fusion.145, f32[512,1088]{0,1:T(8,128)} %fusion.144, f32[512,1088]{0,1:T(8,128)} %fusion.143, ...), kind=kOutput, calls=%fused_computation.104 | convolution fusion | flops 4879253504 | bytes 21746944 | tf_op jit(solution)/shard_map/dot_general | solution.py:347
  996.3 7.2 collective-permute-start.39
  1007.4 6.2 collective-permute-start.40
  (619 shorter events, 385.9 us)
Async XLA Ops:
  7.2 282.8 %all-gather.8.cloned.1.call-start = ((), (), s32[]{:S(2)}) async-start(), calls=%async_computation.5 | async-start | bytes 5570560 | tf_op jit(solution)/shard_map/all_gather | solution.py:309
  11.2 76.4 %collective-permute-start.2 = (bf16[2,136,1088]{2,1,0:T(8,128)(2,1)}, bf16[2,136,1088]{2,1,0:T(8,128)(2,1)}, u32[]{:S(2)}, u32[]{:S(2)}) collective-permute-start(bf16[2,136,1088]{2,1,0:T(8,128)(2,1)} %fusion.120), channel_id=1, source_target_pairs={{8,0},{12,4},{16,8},{20,12},{24,16},{28,20},{9,1},{13,5},{17,9},{2... | collective-permute-start | bytes 1775624 | tf_op jit(solution)/shard_map/ppermute | solution.py:62
  12.4 76.6 %collective-permute-start = (bf16[2,136,1088]{2,1,0:T(8,128)(2,1)}, bf16[2,136,1088]{2,1,0:T(8,128)(2,1)}, u32[]{:S(2)}, u32[]{:S(2)}) collective-permute-start(bf16[2,136,1088]{2,1,0:T(8,128)(2,1)} %fusion.120), channel_id=1, source_target_pairs={{0,4},{4,0},{8,12},{12,8},{16,20},{20,16},{24,28},{28,24},{1,5},{5... | collective-permute-start | bytes 1775624 | tf_op jit(solution)/shard_map/ppermute | solution.py:48
  15.4 74.9 %collective-permute-start.3 = (bf16[2,136,1088]{2,1,0:T(8,128)(2,1)}, bf16[2,136,1088]{2,1,0:T(8,128)(2,1)}, u32[]{:S(2)}, u32[]{:S(2)}) collective-permute-start(bf16[2,136,1088]{2,1,0:T(8,128)(2,1)} %fusion.120), channel_id=1, source_target_pairs={{0,8},{4,12},{8,16},{12,20},{16,24},{20,28},{1,9},{5,13},{9,17},{1... | collective-permute-start | bytes 1775624 | tf_op jit(solution)/shard_map/ppermute | solution.py:55
  25.0 69.0 %collective-permute-start.18 = (bf16[2,136,1088]{2,1,0:T(8,128)(2,1)}, bf16[2,136,1088]{2,1,0:T(8,128)(2,1)}, u32[]{:S(2)}, u32[]{:S(2)}) collective-permute-start(bf16[2,136,1088]{2,1,0:T(8,128)(2,1)} %fusion.117), channel_id=1, source_target_pairs={{0,8},{4,12},{8,16},{12,20},{16,24},{20,28},{1,9},{5,13},{9,17},{1... | collective-permute-start | bytes 1775624 | tf_op jit(solution)/shard_map/ppermute | solution.py:55
  28.6 54.4 %collective-permute-start.14 = (bf16[2,136,1088]{2,1,0:T(8,128)(2,1)}, bf16[2,136,1088]{2,1,0:T(8,128)(2,1)}, u32[]{:S(2)}, u32[]{:S(2)}) collective-permute-start(bf16[2,136,1088]{2,1,0:T(8,128)(2,1)} %fusion.117), channel_id=1, source_target_pairs={{0,4},{4,0},{8,12},{12,8},{16,20},{20,16},{24,28},{28,24},{1,5},{5... | collective-permute-start | bytes 1775624 | tf_op jit(solution)/shard_map/ppermute | solution.py:48
  87.6 64.5 %collective-permute-start.15 = (bf16[2,2,136,1088]{3,2,1,0:T(8,128)(2,1)}, bf16[2,2,136,1088]{3,2,1,0:T(8,128)(2,1)}, u32[]{:S(2)}, u32[]{:S(2)}) collective-permute-start(bf16[2,2,136,1088]{3,2,1,0:T(8,128)(2,1)} %pad_maximum_fusion.3), channel_id=1, source_target_pairs={{0,2},{1,3},{2,0},{3,1},{4,6},{5,7},{6,4},{7,5},{8,10},{9,11},{10,... | collective-permute-start | bytes 3551240 | tf_op jit(solution)/shard_map/ppermute | solution.py:48
  94.0 67.6 %collective-permute-start.1 = (bf16[2,2,136,1088]{3,2,0,1:T(8,128)(2,1)}, bf16[2,2,136,1088]{3,2,0,1:T(8,128)(2,1)}, u32[]{:S(2)}, u32[]{:S(2)}) collective-permute-start(bf16[2,2,136,1088]{3,2,0,1:T(8,128)(2,1)} %maximum_bitcast_fusion), channel_id=1, source_target_pairs={{0,1},{1,0},{2,3},{3,2},{4,5},{5,4},{6,7},{7,6},{8,9},{9,8},{10,11... | collective-permute-start | bytes 3551240 | tf_op jit(solution)/shard_map/ppermute | solution.py:48
  138.4 33.1 %collective-permute-start.12 = (bf16[2,136,1088]{2,1,0:T(8,128)(2,1)}, bf16[2,136,1088]{2,1,0:T(8,128)(2,1)}, u32[]{:S(2)}, u32[]{:S(2)}) collective-permute-start(bf16[2,136,1088]{2,1,0:T(8,128)(2,1)} %broadcast_select_fusion.9), channel_id=1, source_target_pairs={{0,4},{4,0},{8,12},{12,8},{16,20},{20,16},{24,28},{28,24},{1,5},{5... | collective-permute-start | bytes 1775624 | tf_op jit(solution)/shard_map/ppermute | solution.py:48
  138.6 31.3 %collective-permute-start.6 = (bf16[2,136,1088]{2,1,0:T(8,128)(2,1)}, bf16[2,136,1088]{2,1,0:T(8,128)(2,1)}, u32[]{:S(2)}, u32[]{:S(2)}) collective-permute-start(bf16[2,136,1088]{2,1,0:T(8,128)(2,1)} %broadcast_select_fusion.13), channel_id=1, source_target_pairs={{0,4},{4,0},{8,12},{12,8},{16,20},{20,16},{24,28},{28,24},{1,5},{5... | collective-permute-start | bytes 1775624 | tf_op jit(solution)/shard_map/ppermute | solution.py:48
  151.0 31.6 %collective-permute-start.21 = (bf16[2,136,1088]{2,1,0:T(8,128)(2,1)}, bf16[2,136,1088]{2,1,0:T(8,128)(2,1)}, u32[]{:S(2)}, u32[]{:S(2)}) collective-permute-start(bf16[2,136,1088]{2,1,0:T(8,128)(2,1)} %broadcast_select_fusion.12), channel_id=1, source_target_pairs={{0,4},{4,0},{8,12},{12,8},{16,20},{20,16},{24,28},{28,24},{1,5},{5... | collective-permute-start | bytes 1775624 | tf_op jit(solution)/shard_map/ppermute | solution.py:48
  152.0 44.8 %collective-permute-start.29 = (bf16[2,136,1088]{2,1,0:T(8,128)(2,1)}, bf16[2,136,1088]{2,1,0:T(8,128)(2,1)}, u32[]{:S(2)}, u32[]{:S(2)}) collective-permute-start(bf16[2,136,1088]{2,1,0:T(8,128)(2,1)} %broadcast_select_fusion.8), channel_id=1, source_target_pairs={{0,4},{4,0},{8,12},{12,8},{16,20},{20,16},{24,28},{28,24},{1,5},{5... | collective-permute-start | bytes 1775624 | tf_op jit(solution)/shard_map/ppermute | solution.py:48
  161.6 79.7 %collective-permute-start.26 = (bf16[2,2,136,1088]{3,2,1,0:T(8,128)(2,1)}, bf16[2,2,136,1088]{3,2,1,0:T(8,128)(2,1)}, u32[]{:S(2)}, u32[]{:S(2)}) collective-permute-start(bf16[2,2,136,1088]{3,2,1,0:T(8,128)(2,1)} %pad_maximum_fusion.5), channel_id=1, source_target_pairs={{0,2},{1,3},{2,0},{3,1},{4,6},{5,7},{6,4},{7,5},{8,10},{9,11},{10,... | collective-permute-start | bytes 3551240 | tf_op jit(solution)/shard_map/ppermute | solution.py:48
  185.7 49.1 %collective-permute-start.32 = (bf16[2,2,136,1088]{3,2,1,0:T(8,128)(2,1)}, bf16[2,2,136,1088]{3,2,1,0:T(8,128)(2,1)}, u32[]{:S(2)}, u32[]{:S(2)}) collective-permute-start(bf16[2,2,136,1088]{3,2,1,0:T(8,128)(2,1)} %get-tuple-element.114), channel_id=1, source_target_pairs={{0,1},{1,0},{2,3},{3,2},{4,5},{5,4},{6,7},{7,6},{8,9},{9,8},{10,11... | collective-permute-start | bytes 3551240 | tf_op jit(solution)/shard_map/ppermute | solution.py:48
  187.2 42.2 %collective-permute-start.22 = (bf16[2,2,136,1088]{3,2,1,0:T(8,128)(2,1)}, bf16[2,2,136,1088]{3,2,1,0:T(8,128)(2,1)}, u32[]{:S(2)}, u32[]{:S(2)}) collective-permute-start(bf16[2,2,136,1088]{3,2,1,0:T(8,128)(2,1)} %pad_maximum_fusion.4), channel_id=1, source_target_pairs={{0,2},{1,3},{2,0},{3,1},{4,6},{5,7},{6,4},{7,5},{8,10},{9,11},{10,... | collective-permute-start | bytes 3551240 | tf_op jit(solution)/shard_map/ppermute | solution.py:48
  196.5 145.1 %all-gather.6.cloned.1.call-start = ((), (), s32[]{:S(2)}) async-start(), calls=%async_computation.4 | async-start | bytes 5570560 | tf_op jit(solution)/shard_map/all_gather | solution.py:310
  231.0 37.2 %collective-permute-start.30 = (bf16[2,2,136,1088]{3,2,1,0:T(8,128)(2,1)S(1)}, bf16[2,2,136,1088]{3,2,1,0:T(8,128)(2,1)S(1)}, u32[]{:S(2)}, u32[]{:S(2)}) collective-permute-start(bf16[2,2,136,1088]{3,2,1,0:T(8,128)(2,1)S(1)} %pad_maximum_fusion.6), channel_id=1, source_target_pairs={{0,2},{1,3},{2,0},{3,1},{4,6},{5,7},{6,4},{7,5},{8,10},{9,11},{10,... | collective-permute-start | bytes 3551240 | tf_op jit(solution)/shard_map/ppermute | solution.py:48
  273.1 599.6 %reduce-scatter.5.cloned.1.call-start = ((), (), s32[]{:S(2)}) async-start(), calls=%async_computation.3 | async-start | bytes 5570560 | tf_op jit(solution)/shard_map/reduce_scatter | solution.py:417
  591.4 96.6 %collective-permute-start.60 = (bf16[2,2,2,136,1088]{4,3,2,1,0:T(8,128)(2,1)}, bf16[2,2,2,136,1088]{4,3,2,1,0:T(8,128)(2,1)}, u32[]{:S(2)}, u32[]{:S(2)}) collective-permute-start(bf16[2,2,2,136,1088]{4,3,2,1,0:T(8,128)(2,1)} %fusion.56), channel_id=1, source_target_pairs={{0,1},{1,0},{2,3},{3,2},{4,5},{5,4},{6,7},{7,6},{8,9},{9,8},{10,11... | collective-permute-start | bytes 7102472 | tf_op jit(solution)/shard_map/ppermute | solution.py:48
  594.1 83.6 %collective-permute-start.63 = (bf16[2,2,2,136,1088]{4,3,2,1,0:T(8,128)(2,1)}, bf16[2,2,2,136,1088]{4,3,2,1,0:T(8,128)(2,1)}, u32[]{:S(2)}, u32[]{:S(2)}) collective-permute-start(bf16[2,2,2,136,1088]{4,3,2,1,0:T(8,128)(2,1)} %fusion.52), channel_id=1, source_target_pairs={{0,1},{1,0},{2,3},{3,2},{4,5},{5,4},{6,7},{7,6},{8,9},{9,8},{10,11... | collective-permute-start | bytes 7102472 | tf_op jit(solution)/shard_map/ppermute | solution.py:48
  596.0 87.1 %collective-permute-start.66 = (bf16[2,2,2,136,1088]{4,3,2,1,0:T(8,128)(2,1)}, bf16[2,2,2,136,1088]{4,3,2,1,0:T(8,128)(2,1)}, u32[]{:S(2)}, u32[]{:S(2)}) collective-permute-start(bf16[2,2,2,136,1088]{4,3,2,1,0:T(8,128)(2,1)} %fusion.48), channel_id=1, source_target_pairs={{0,1},{1,0},{2,3},{3,2},{4,5},{5,4},{6,7},{7,6},{8,9},{9,8},{10,11... | collective-permute-start | bytes 7102472 | tf_op jit(solution)/shard_map/ppermute | solution.py:48
  598.2 200.3 %collective-permute-start.57 = (bf16[2,2,2,136,1088]{4,3,2,1,0:T(8,128)(2,1)}, bf16[2,2,2,136,1088]{4,3,2,1,0:T(8,128)(2,1)}, u32[]{:S(2)}, u32[]{:S(2)}) collective-permute-start(bf16[2,2,2,136,1088]{4,3,2,1,0:T(8,128)(2,1)} %fusion.60), channel_id=1, source_target_pairs={{0,1},{1,0},{2,3},{3,2},{4,5},{5,4},{6,7},{7,6},{8,9},{9,8},{10,11... | collective-permute-start | bytes 7102472 | tf_op jit(solution)/shard_map/ppermute | solution.py:48
  598.3 278.8 %reduce-scatter.3.cloned.1.call-start = ((), (), s32[]{:S(2)}) async-start(), calls=%async_computation.2 | async-start | bytes 5570560 | tf_op jit(solution)/shard_map/reduce_scatter | solution.py:416
  681.2 83.0 %collective-permute-start.64 = (bf16[2,2,136,1088]{3,2,1,0:T(8,128)(2,1)S(1)}, bf16[2,2,136,1088]{3,2,1,0:T(8,128)(2,1)S(1)}, u32[]{:S(2)}, u32[]{:S(2)}) collective-permute-start(bf16[2,2,136,1088]{3,2,1,0:T(8,128)(2,1)S(1)} %select_bitcast_fusion.1), channel_id=1, source_target_pairs={{0,2},{1,3},{2,0},{3,1},{4,6},{5,7},{6,4},{7,5},{8,10},{9,11},{10,... | collective-permute-start | bytes 3551240 | tf_op jit(solution)/shard_map/ppermute | solution.py:48
  686.2 76.2 %collective-permute-start.67 = (bf16[2,2,136,1088]{3,2,1,0:T(8,128)(2,1)S(1)}, bf16[2,2,136,1088]{3,2,1,0:T(8,128)(2,1)S(1)}, u32[]{:S(2)}, u32[]{:S(2)}) collective-permute-start(bf16[2,2,136,1088]{3,2,1,0:T(8,128)(2,1)S(1)} %select_bitcast_fusion), channel_id=1, source_target_pairs={{0,2},{1,3},{2,0},{3,1},{4,6},{5,7},{6,4},{7,5},{8,10},{9,11},{10,... | collective-permute-start | bytes 3551240 | tf_op jit(solution)/shard_map/ppermute | solution.py:48
  691.1 97.6 %collective-permute-start.61 = (bf16[2,2,136,1088]{3,2,1,0:T(8,128)(2,1)S(1)}, bf16[2,2,136,1088]{3,2,1,0:T(8,128)(2,1)S(1)}, u32[]{:S(2)}, u32[]{:S(2)}) collective-permute-start(bf16[2,2,136,1088]{3,2,1,0:T(8,128)(2,1)S(1)} %select_bitcast_fusion.2), channel_id=1, source_target_pairs={{0,2},{1,3},{2,0},{3,1},{4,6},{5,7},{6,4},{7,5},{8,10},{9,11},{10,... | collective-permute-start | bytes 3551240 | tf_op jit(solution)/shard_map/ppermute | solution.py:48
  764.7 26.8 %collective-permute-start.65 = (bf16[2,136,1088]{2,1,0:T(8,128)(2,1)S(1)}, bf16[2,136,1088]{2,1,0:T(8,128)(2,1)S(1)}, u32[]{:S(2)}, u32[]{:S(2)}) collective-permute-start(bf16[2,136,1088]{2,1,0:T(8,128)(2,1)S(1)} %dynamic-slice_bitcast_fusion.5), channel_id=1, source_target_pairs={{0,4},{4,0},{8,12},{12,8},{16,20},{20,16},{24,28},{28,24},{1,5},{5... | collective-permute-start | bytes 1775624 | tf_op jit(solution)/shard_map/ppermute | solution.py:48
  831.2 26.1 %collective-permute-start.59 = (bf16[2,136,1088]{2,1,0:T(8,128)(2,1)}, bf16[2,136,1088]{2,1,0:T(8,128)(2,1)S(1)}, u32[]{:S(2)}, u32[]{:S(2)}) collective-permute-start(bf16[2,136,1088]{2,1,0:T(8,128)(2,1)} %dynamic-slice_bitcast_fusion.7), channel_id=1, source_target_pairs={{0,4},{4,0},{8,12},{12,8},{16,20},{20,16},{24,28},{28,24},{1,5},{5... | collective-permute-start | bytes 1775624 | tf_op jit(solution)/shard_map/ppermute | solution.py:48
  889.1 33.0 %collective-permute-start.43 = (bf16[2,2,136,1088]{3,2,1,0:T(8,128)(2,1)S(1)}, bf16[2,2,136,1088]{3,2,1,0:T(8,128)(2,1)S(1)}, u32[]{:S(2)}, u32[]{:S(2)}) collective-permute-start(bf16[2,2,136,1088]{3,2,1,0:T(8,128)(2,1)S(1)} %bitcast.569), channel_id=1, source_target_pairs={{0,1},{1,0},{2,3},{3,2},{4,5},{5,4},{6,7},{7,6},{8,9},{9,8},{10,11... | collective-permute-start | bytes 3551240 | tf_op jit(solution)/shard_map/ppermute | solution.py:48
  898.4 28.9 %collective-permute-start.46 = (bf16[2,136,1088]{2,1,0:T(8,128)(2,1)S(1)}, bf16[2,136,1088]{2,1,0:T(8,128)(2,1)S(1)}, u32[]{:S(2)}, u32[]{:S(2)}) collective-permute-start(bf16[2,136,1088]{2,1,0:T(8,128)(2,1)S(1)} %dynamic-slice_bitcast_fusion.9), channel_id=1, source_target_pairs={{0,4},{4,0},{8,12},{12,8},{16,20},{20,16},{24,28},{28,24},{1,5},{5... | collective-permute-start | bytes 1775624 | tf_op jit(solution)/shard_map/ppermute | solution.py:48
  954.8 39.9 %collective-permute-start.76 = (bf16[2,2,136,1088]{3,2,1,0:T(8,128)(2,1)}, bf16[2,2,136,1088]{3,2,1,0:T(8,128)(2,1)}, u32[]{:S(2)}, u32[]{:S(2)}) collective-permute-start(bf16[2,2,136,1088]{3,2,1,0:T(8,128)(2,1)} %pad_maximum_fusion.7), channel_id=1, source_target_pairs={{0,1},{1,0},{2,3},{3,2},{4,5},{5,4},{6,7},{7,6},{8,9},{9,8},{10,11... | collective-permute-start | bytes 3551240 | tf_op jit(solution)/shard_map/ppermute | solution.py:48
  955.3 31.9 %collective-permute-start.37 = (f32[13056]{0:T(1024)S(1)}, f32[13056]{0:T(1024)S(1)}, u32[]{:S(2)}, u32[]{:S(2)}) collective-permute-start(f32[13056]{0:T(1024)S(1)} %add.565), channel_id=1, source_target_pairs={{0,2},{1,3},{2,0},{3,1},{4,6},{5,7},{6,4},{7,5},{8,10},{9,11},{10,... | collective-permute-start | bytes 156680 | tf_op jit(solution)/shard_map/ppermute | solution.py:48
  (189 other events, 2788.1 us)
Sparse Core Ops, SparseCore 0:
  196.7 51.2 all-gather.7
  273.2 35.6 all-gather.5
  598.4 48.0 reduce-scatter.4
  677.9 70.6 reduce-scatter.2

commit v2 on v1

--- a/solution.py
+++ b/solution.py
@@ -1,6 +1,10 @@
+import functools
+
 import jax
 import jax.numpy as jnp
 from jax import lax
+from jax.experimental import pallas as pl
+from jax.experimental.pallas import tpu as pltpu
 from jax.sharding import PartitionSpec as P
 
 HEAD_DIM = 64
@@ -231,17 +235,232 @@
     return value
 
 
-def score_table(query_rows, key_rows, query_segs, key_segs, query_place, key_place, head_count):
-    query_heads = query_rows.reshape(query_rows.shape[0], head_count, HEAD_DIM)
-    key_heads = key_rows.reshape(key_rows.shape[0], head_count, HEAD_DIM)
-    raw = (
-        jnp.einsum("qhd,khd->hqk", query_heads, key_heads, preferred_element_type=jnp.float32)
-        * 0.125
-    )
-    allowed = (key_place[None, :] <= query_place[:, None]) & (
-        key_segs[None, :] == query_segs[:, None]
-    )
-    return jnp.where(allowed[None], raw, masked_score)
+def dot_nt(left, right):
+    return lax.dot_general(
+        left, right, (((1,), (1,)), ((), ())), preferred_element_type=jnp.float32
+    )
+
+
+def dot_tn(left, right):
+    return lax.dot_general(
+        left, right, (((0,), (0,)), ((), ())), preferred_element_type=jnp.float32
+    )
+
+
+def lane_masks(pair, features, rows):
+    lane = lax.broadcasted_iota(jnp.int32, (rows, 2 * HEAD_DIM), 1)
+    inside = lane + pair * (2 * HEAD_DIM) < features
+    return inside & (lane < HEAD_DIM), inside & (lane >= HEAD_DIM), inside
+
+
+def allowed_pairs(key_segs, query_segs, diagonal):
+    allowed = key_segs == query_segs
+    if diagonal:
+        shape = allowed.shape
+        key_at = lax.broadcasted_iota(jnp.int32, shape, 0)
+        query_at = lax.broadcasted_iota(jnp.int32, shape, 1)
+        allowed = allowed & (key_at <= query_at)
+    return allowed
+
+
+def attend_kernel(features, place_ref, q_ref, k_ref, v_ref, kseg_ref, qseg_ref, o_ref, lse_ref):
+    rows = q_ref.shape[0]
+    masks = lane_masks(pl.program_id(1), features, rows)
+    scaled = q_ref[...].astype(jnp.float32) * 0.125
+    queries = [jnp.where(masks[h], scaled, 0.0).astype(jnp.bfloat16) for h in range(2)]
+    query_segs = qseg_ref[...]
+
+    def block(at, carry, diagonal):
+        start = pl.multiple_of(at * rows, rows)
+        keys = jnp.where(masks[2], k_ref[pl.ds(start, rows), :], 0.0).astype(jnp.bfloat16)
+        values = jnp.where(masks[2], v_ref[pl.ds(start, rows), :], 0.0).astype(jnp.bfloat16)
+        allowed = allowed_pairs(kseg_ref[pl.ds(start, rows), :], query_segs, diagonal)
+        out = []
+        for h in range(2):
+            largest, total, mixed = carry[h]
+            scores = jnp.where(allowed, dot_nt(keys, queries[h]), masked_score)
+            newest = jnp.maximum(largest, jnp.max(scores, axis=0, keepdims=True))
+            weights = jnp.exp(scores - newest)
+            shrink = jnp.exp(largest - newest)
+            total = total * shrink + jnp.sum(weights, axis=0, keepdims=True)
+            mixed = mixed * shrink + dot_tn(values, weights.astype(jnp.bfloat16))
+            out.append((newest, total, mixed))
+        return tuple(out)
+
+    first = (
+        jnp.full((1, rows), masked_score, jnp.float32),
+        jnp.zeros((1, rows), jnp.float32),
+        jnp.zeros((2 * HEAD_DIM, rows), jnp.float32),
+    )
+    place = place_ref[0]
+    carry = lax.fori_loop(0, place, lambda at, c: block(at, c, False), (first, first))
+    carry = block(place, carry, True)
+    parts = []
+    for h in range(2):
+        largest, total, mixed = carry[h]
+        parts.append(mixed[h * HEAD_DIM : (h + 1) * HEAD_DIM] / total)
+        lse_ref[h : h + 1, :] = largest + jnp.log(total)
+    o_ref[...] = jnp.concatenate(parts, axis=0).T.astype(o_ref.dtype)
+
+
+def attend_grads_kernel(
+    features,
+    place_ref,
+    q_ref,
+    k_ref,
+    v_ref,
+    g_ref,
+    o_ref,
+    lse_ref,
+    kseg_ref,
+    qseg_ref,
+    dq_ref,
+    dk_ref,
+    dv_ref,
+):
+    rows = q_ref.shape[0]
+    masks = lane_masks(pl.program_id(1), features, rows)
+    scaled = q_ref[...].astype(jnp.float32) * 0.125
+    grads = g_ref[...].astype(jnp.float32)
+    queries = [jnp.where(masks[h], scaled, 0.0).astype(jnp.bfloat16) for h in range(2)]
+    grad_heads = [jnp.where(masks[h], grads, 0.0).astype(jnp.bfloat16) for h in range(2)]
+    products = jnp.where(masks[2], grads * o_ref[...].astype(jnp.float32), 0.0).T
+    deltas = [
+        jnp.sum(products[h * HEAD_DIM : (h + 1) * HEAD_DIM], axis=0, keepdims=True)
+        for h in range(2)
+    ]
+    lses = [lse_ref[h : h + 1, :] for h in range(2)]
+    query_segs = qseg_ref[...]
+
+    def block(at, carry, diagonal):
+        start = pl.multiple_of(at * rows, rows)
+        keys = jnp.where(masks[2], k_ref[pl.ds(start, rows), :], 0.0).astype(jnp.bfloat16)
+        values = jnp.where(masks[2], v_ref[pl.ds(start, rows), :], 0.0).astype(jnp.bfloat16)
+        allowed = allowed_pairs(kseg_ref[pl.ds(start, rows), :], query_segs, diagonal)
+        out, grad_keys, grad_values = [], 0.0, 0.0
+        for h in range(2):
+            scores = jnp.where(allowed, dot_nt(keys, queries[h]), masked_score)
+            probs = jnp.exp(scores - lses[h])
+            grad_scores = probs * (dot_nt(values, grad_heads[h]) - deltas[h])
+            grad_scores = grad_scores.astype(jnp.bfloat16)
+            out.append(carry[h] + dot_tn(keys, grad_scores))
+            grad_keys += jnp.dot(grad_scores, queries[h], preferred_element_type=jnp.float32)
+            grad_values += jnp.dot(
+                probs.astype(jnp.bfloat16), grad_heads[h], preferred_element_type=jnp.float32
+            )
+        dk_ref[pl.ds(start, rows), :] = grad_keys.astype(dk_ref.dtype)
+        dv_ref[pl.ds(start, rows), :] = grad_values.astype(dv_ref.dtype)
+        return tuple(out)
+
+    place = place_ref[0]
+    blank = jnp.zeros((2 * HEAD_DIM, rows), jnp.float32)
+    carry = lax.fori_loop(0, place, lambda at, c: block(at, c, False), (blank, blank))
+    carry = block(place, carry, True)
+
+    def clear(at, _):
+        start = pl.multiple_of(at * rows, rows)
+        dk_ref[pl.ds(start, rows), :] = jnp.zeros((rows, 2 * HEAD_DIM), dk_ref.dtype)
+        dv_ref[pl.ds(start, rows), :] = jnp.zeros((rows, 2 * HEAD_DIM), dv_ref.dtype)
+        return 0
+
+    lax.fori_loop(place + 1, k_ref.shape[0] // rows, clear, 0)
+    both = [carry[h][h * HEAD_DIM : (h + 1) * HEAD_DIM] for h in range(2)]
+    dq_ref[...] = (jnp.concatenate(both, axis=0).T * 0.125).astype(dq_ref.dtype)
+
+
+def attention_specs(sequences, stretch, length, features):
+    wide = 2 * HEAD_DIM
+    pairs = -(-features // wide)
+    own = pl.BlockSpec((None, stretch, wide), lambda s, p: (s, 0, p))
+    whole = pl.BlockSpec((None, length, wide), lambda s, p: (s, 0, p))
+    lse = pl.BlockSpec((None, None, 2, stretch), lambda s, p: (s, p, 0, 0))
+    key_segs = pl.BlockSpec((None, length, 1), lambda s, p: (s, 0, 0))
+    query_segs = pl.BlockSpec((None, 1, stretch), lambda s, p: (s, 0, 0))
+    place = pl.BlockSpec(memory_space=pltpu.SMEM)
+    return pairs, own, whole, lse, key_segs, query_segs, place
+
+
+def attend(place, queries, keys, values, key_segs, query_segs):
+    sequences, stretch, features = queries.shape
+    length = keys.shape[1]
+    pairs, own, whole, lse, kseg, qseg, at = attention_specs(sequences, stretch, length, features)
+    return pl.pallas_call(
+        functools.partial(attend_kernel, features),
+        grid=(sequences, pairs),
+        in_specs=[at, own, whole, whole, kseg, qseg],
+        out_specs=[own, lse],
+        out_shape=[
+            jax.ShapeDtypeStruct(queries.shape, jnp.bfloat16),
+            jax.ShapeDtypeStruct((sequences, pairs, 2, stretch), jnp.float32),
+        ],
+        compiler_params=pltpu.CompilerParams(vmem_limit_bytes=40 * 2**20),
+        cost_estimate=pl.CostEstimate(
+            flops=16 * pairs * sequences * stretch * length * HEAD_DIM,
+            bytes_accessed=8 * queries.size + 4 * keys.size,
+            transcendentals=0,
+        ),
+    )(place, queries, keys, values, key_segs, query_segs)
+
+
+def attend_grads(place, queries, keys, values, grads, attended, lse_rows, key_segs, query_segs):
+    sequences, stretch, features = queries.shape
+    length = keys.shape[1]
+    pairs, own, whole, lse, kseg, qseg, at = attention_specs(sequences, stretch, length, features)
+    return pl.pallas_call(
+        functools.partial(attend_grads_kernel, features),
+        grid=(sequences, pairs),
+        in_specs=[at, own, whole, whole, own, own, lse, kseg, qseg],
+        out_specs=[own, whole, whole],
+        out_shape=[
+            jax.ShapeDtypeStruct(queries.shape, jnp.bfloat16),
+            jax.ShapeDtypeStruct(keys.shape, jnp.bfloat16),
+            jax.ShapeDtypeStruct(keys.shape, jnp.bfloat16),
+        ],
+        compiler_params=pltpu.CompilerParams(vmem_limit_bytes=40 * 2**20),
+        cost_estimate=pl.CostEstimate(
+            flops=40 * pairs * sequences * stretch * length * HEAD_DIM,
+            bytes_accessed=8 * queries.size + 8 * keys.size,
+            transcendentals=0,
+        ),
+    )(place, queries, keys, values, grads, attended, lse_rows, key_segs, query_segs)
+
+
+def gather_small(links, vector):
+    full = jnp.zeros((links.shards, vector.shape[0]), vector.dtype)
+    for k, pair in enumerate(links.gather_pairs(vector)):
+        full = set_at(full, pair, 2 * links.block_at(k))
+    return full
+
+
+def gather_stretches(links, mine):
+    have = mine[:, None]
+    bit = links.places // 2
+    while bit >= 1:
+        pairs = [(i, i ^ bit) for i in range(links.places)]
+        if bit == links.places // 2:
+            pairs = [(i, j) for i, j in pairs if i < j]
+        other = lax.ppermute(have, "context", pairs)
+        lower = (links.place // bit) % 2 == 0
+        first, last = jnp.where(lower, have, other), jnp.where(lower, other, have)
+        have = jnp.stack([first, last], axis=2)
+        have = have.reshape(have.shape[0], -1, *have.shape[3:])
+        bit //= 2
+    return have
+
+
+def reduce_stretches(links, parts):
+    bit = 1
+    while bit < links.places:
+        split = parts.reshape(-1, 2, *parts.shape[1:])
+        digit = (links.place // bit) % 2
+        sent = lax.dynamic_index_in_dim(split, 1 - digit, 1, keepdims=False)
+        kept = lax.dynamic_index_in_dim(split, digit, 1, keepdims=False)
+        pairs = [(i, i ^ bit) for i in range(links.places)]
+        if bit == links.places // 2:
+            pairs = [(i, j) for i, j in pairs if i > j]
+        parts = add_low(kept, lax.ppermute(sent, "context", pairs))
+        bit *= 2
+    return parts[0]
 
 
 def local(
@@ -271,7 +490,7 @@
     small = (
         ln1_gain, ln1_bias, bias_query, bias_value, bias_out, ln2_gain, ln2_bias, bias_down, bias_up
     )
-    small_all = lax.all_gather(jnp.concatenate(small), "fsdp", axis=0)
+    small_all = gather_small(links, jnp.concatenate(small))
     small_full, start = [], 0
     for vector in small:
         small_full.append(small_all[:, start : start + vector.shape[0]].reshape(-1))
@@ -296,41 +515,24 @@
     shift_two = shift_two.astype(jnp.float32)
     inputs = block_input.reshape(tokens, features).astype(jnp.float32)
     normed = normalize(inputs, gain_one, shift_one).astype(jnp.bfloat16)
-    queries, keys_own, values_own = (
-        jnp.dot(normed, full_first[j], preferred_element_type=jnp.float32) for j in range(3)
-    )
+    inputs_all = gather_stretches(links, block_input).reshape(-1, features)
+    normed_all = normalize(inputs_all.astype(jnp.float32), gain_one, shift_one)
+    normed_all = normed_all.astype(jnp.bfloat16)
+    queries = jnp.dot(normed, full_first[0], preferred_element_type=jnp.float32)
+    keys_all = jnp.dot(normed_all, full_first[1], preferred_element_type=jnp.float32)
+    values_all = jnp.dot(normed_all, full_first[2], preferred_element_type=jnp.float32)
     queries = (queries + query_bias.astype(jnp.float32)).astype(jnp.bfloat16)
-    keys_own = keys_own.astype(jnp.bfloat16)
-    values_own = (values_own + value_bias.astype(jnp.float32)).astype(jnp.bfloat16)
+    keys_all = keys_all.astype(jnp.bfloat16).reshape(sequences, length_all, features)
+    values_all = values_all + value_bias.astype(jnp.float32)
+    values_all = values_all.astype(jnp.bfloat16).reshape(sequences, length_all, features)
     query_seqs = queries.reshape(sequences, stretch, features)
-    key_seqs = keys_own.reshape(sequences, stretch, features)
-    value_seqs = values_own.reshape(sequences, stretch, features)
-    keys_all, values_all = (
-        lax.all_gather(key_seqs, "context", axis=1, tiled=True),
-        lax.all_gather(value_seqs, "context", axis=1, tiled=True),
-    )
-    query_place = offset + jnp.arange(stretch, dtype=jnp.int32)
-    key_place = jnp.arange(length_all, dtype=jnp.int32)
-    own_segs = lax.dynamic_slice_in_dim(segment_ids, offset, stretch, 1)
-
-    def forward_one(item):
-        query_rows, key_rows, value_rows, segs_own, segs_all = item
-        scores = score_table(
-            query_rows, key_rows, segs_own, segs_all, query_place, key_place, head_count
-        )
-        largest = jnp.max(scores, axis=-1, keepdims=True)
-        weights = jnp.exp(scores - largest)
-        totals = jnp.sum(weights, axis=-1, keepdims=True)
-        probs = (weights / totals).astype(jnp.bfloat16)
-        value_heads = value_rows.reshape(length_all, head_count, HEAD_DIM)
-        mixed = jnp.einsum("hqk,khd->qhd", probs, value_heads, preferred_element_type=jnp.float32)
-        lse_rows = largest[:, :, 0] + jnp.log(totals[:, :, 0])
-        return (mixed.reshape(stretch, features).astype(jnp.bfloat16), lse_rows)
-
-    attended, lse_kept = lax.map(
-        forward_one, (query_seqs, keys_all, values_all, own_segs, segment_ids)
-    )
-    attended = attended.reshape(tokens, features)
+    own_segs = lax.dynamic_slice_in_dim(segment_ids, offset, stretch, 1)[:, None, :]
+    key_segs = segment_ids[:, :, None]
+    place = links.place.astype(jnp.int32).reshape(1)
+    attended_seqs, lse_kept = attend(
+        place, query_seqs, keys_all, values_all, key_segs, own_segs
+    )
+    attended = attended_seqs.reshape(tokens, features)
     middle = (
         inputs
         + jnp.dot(attended, full_out, preferred_element_type=jnp.float32)
@@ -375,57 +577,36 @@
     grad_attended = contract_cols(grad_middle_low, full_out).astype(jnp.bfloat16)
     grad_att_seqs = grad_attended.reshape(sequences, stretch, features)
 
-    def local_grads(item):
-        query_rows, key_rows, value_rows, grad_rows, segs_own, segs_all, lse_rows = item
-        scores = score_table(
-            query_rows, key_rows, segs_own, segs_all, query_place, key_place, head_count
-        )
-        probs = jnp.exp(scores - lse_rows[:, :, None])
-        grad_heads = grad_rows.reshape(stretch, head_count, HEAD_DIM)
-        value_heads = value_rows.reshape(length_all, head_count, HEAD_DIM)
-        key_heads = key_rows.reshape(length_all, head_count, HEAD_DIM)
-        grad_probs = jnp.einsum(
-            "qhd,khd->hqk", grad_heads, value_heads, preferred_element_type=jnp.float32
-        )
-        deltas = jnp.sum(probs * grad_probs, axis=-1)
-        grad_scores = (probs * (grad_probs - deltas[:, :, None])).astype(jnp.bfloat16)
-        grad_query = (
-            jnp.einsum(
-                "hqk,khd->qhd", grad_scores, key_heads, preferred_element_type=jnp.float32
-            ).reshape(stretch, features)
-            * 0.125
-        )
-        query_heads = query_rows.reshape(stretch, head_count, HEAD_DIM)
-        key_part = (
-            jnp.einsum(
-                "hqk,qhd->khd", grad_scores, query_heads, preferred_element_type=jnp.float32
-            ).reshape(length_all, features)
-            * 0.125
-        )
-        value_part = jnp.einsum(
-            "hqk,qhd->khd",
-            probs.astype(jnp.bfloat16),
-            grad_heads,
-            preferred_element_type=jnp.float32,
-        ).reshape(length_all, features)
-        return (grad_query, key_part.astype(jnp.bfloat16), value_part.astype(jnp.bfloat16))
-
-    local_items = (query_seqs, keys_all, values_all, grad_att_seqs, own_segs, segment_ids, lse_kept)
-    grad_queries, key_parts, value_parts = lax.map(local_grads, local_items)
-    grad_keys, grad_values = (
-        lax.psum_scatter(key_parts, "context", scatter_dimension=1, tiled=True),
-        lax.psum_scatter(value_parts, "context", scatter_dimension=1, tiled=True),
-    )
-    grad_queries = grad_queries.reshape(tokens, features).astype(jnp.bfloat16)
-    grad_keys = grad_keys.reshape(tokens, features).astype(jnp.bfloat16)
-    grad_values = grad_values.reshape(tokens, features).astype(jnp.bfloat16)
+    grad_queries, key_parts, value_parts = attend_grads(
+        place,
+        query_seqs,
+        keys_all,
+        values_all,
+        grad_att_seqs,
+        attended_seqs,
+        lse_kept,
+        key_segs,
+        own_segs,
+    )
+    grad_queries = grad_queries.reshape(tokens, features)
+    key_rows = key_parts.reshape(-1, features)
+    value_rows = value_parts.reshape(-1, features)
+    parts = jnp.stack([key_parts, value_parts])
+    parts = parts.reshape(2, sequences, links.places, stretch, features).transpose(2, 0, 1, 3, 4)
+    own_parts = reduce_stretches(links, parts)
+    grad_keys = own_parts[0].reshape(tokens, features)
+    grad_values = own_parts[1].reshape(tokens, features)
     grads_first = jnp.stack(
-        [contract_rows(normed, part) for part in (grad_queries, grad_keys, grad_values)]
-        + [grad_w_out]
+        [
+            contract_rows(normed, grad_queries),
+            contract_rows(normed_all, key_rows),
+            contract_rows(normed_all, value_rows),
+            grad_w_out,
+        ]
     ).astype(jnp.bfloat16)
     first_sums = reduce_first(links, grads_first)
     grad_b_query = jnp.sum(grad_queries.astype(jnp.float32), axis=0)
-    grad_b_value = jnp.sum(grad_values.astype(jnp.float32), axis=0)
+    grad_b_value = jnp.sum(value_rows.astype(jnp.float32), axis=0)
     grad_normed = (
         contract_cols(grad_queries, full_first[0])
         + contract_cols(grad_keys, full_first[1])

time: 1040 us -> 948 us (0.912)
  matrix products: 304 us -> 150 us
  starting transfers between devices: 114 us -> 222 us
  other arithmetic: 191 us -> 119 us
  blocking collectives: 46.3 us -> 0 us
  Pallas kernels: 0 us -> 35.6 us
  waiting for transfers between devices: 239 us -> 268 us
  local copies, waits for them, and re-layouts: 117 us -> 140 us
  between operations: 17.1 us -> 3.49 us
    dot_general x9 -> x3, matrix products: 189 us -> 16.1 us  [the longest x1 7.07 us: local(): jnp.dot(normed_all, full_first[2], preferred_element_type=jnp.float32)]
    ppermute x53 -> x57, starting transfers between devices: 53.1 us -> 124 us  [swap(): return lax.ppermute(value, axis, [(i, i ^ bit) for i in range(count)])]
    convert_element_type x1, other arithmetic: 59.5 us -> 3.27 us  [local(): normed_all = normed_all.astype(jnp.bfloat16)]
    unnamed x1 -> x0, blocking collectives: 46.3 us -> none
    pallas_call x0 -> x2, Pallas kernels: none -> 35.6 us  [the longest x1 22.9 us: attend_grads(): pl.pallas_call(functools.partial(attend_grads_kernel, features), grid=(se...]
    ppermute x0 -> x4, waiting for transfers between devices: none -> 30.7 us  [the longest x2 18.5 us: reduce_stretches(): parts = add_low(kept, lax.ppermute(sent, 'context', pairs))]
    reduce_sum x1 -> x2, other arithmetic: 22.8 us -> 0.98 us  [the longest x1 0.74 us: local(): grad_b_value = jnp.sum(value_rows.astype(jnp.float32), axis=0)]
    ppermute x53 -> x57, waiting for transfers between devices: 183 us -> 162 us  [swap(): return lax.ppermute(value, axis, [(i, i ^ bit) for i in range(count)])]
  transfers between devices with their start and end apart: 81 -> 91, of which waited for: 23 -> 30; matrix products, arithmetic and copies ran while one was open for 32% -> 27% of each run, Pallas kernels for 0% -> 1%
where the time goes in v2:
time: 948 us; the launch traced here: 938 us
  waiting for transfers between devices  268 us (28%)
  starting transfers between devices  222 us (23%)
  matrix products  150 us (16%)
  local copies, waits for them, and re-layouts  140 us (15%)
  other arithmetic  119 us (13%)
  Pallas kernels  35.6 us (4%)
    ppermute x57, waiting for transfers between devices, swap(): return lax.ppermute(value, axis, [(i, i ^ bit) for i in range(count)])  162 us
    ppermute x57, starting transfers between devices, swap(): return lax.ppermute(value, axis, [(i, i ^ bit) for i in range(count)])  124 us
    dot_general x9, matrix products, contract_rows(): lax.dot_general(left, right, (((0,), (0,)), ((), ())), preferred_element_...  65.6 us
    ppermute x9, waiting for transfers between devices, left(): return lax.ppermute(value, 'fsdp', pairs)  51.8 us
    ppermute x6, starting transfers between devices, reduce_line(): lax.ppermute(going_right.astype(jnp.bfloat16), 'fsdp', right_pairs)  40.4 us
    dot_general x9, matrix products, contract_cols(): lax.dot_general(left, right, (((1,), (1,)), ((), ())), preferred_element_...  38 us
    pallas_call x1, Pallas kernels, attend_grads(): pl.pallas_call(functools.partial(attend_grads_kernel, features), grid=(se...  22.9 us
  transfers between devices with their start and end apart: 91, of which 30 were waited for; matrix products, arithmetic and copies ran while one was open for 27% of the time, Pallas kernels for 1%

profile of v2, /device:TPU:0, one launch (start us, length us, event | category | flops | bytes accessed | tf_op | source)
XLA Modules:
  0.0 938.2 jit_solution(1262739465852185786)
XLA Ops:
  51.1 11.9 %collective-permute-done.8 = bf16[1632]{0:T(1024)(128)(2,1)S(1)} collective-permute-done((bf16[1632]{0:T(1024)(128)(2,1)S(1)}, bf16[1632]{0:T(1024)(128)(2,1)S(1)}, u32[]{:S(2)}, u32[]{:S(2)}) %collective-permute-start.8) | collective-permute-done | bytes 3296 | tf_op jit(solution)/shard_map/ppermute | solution.py:66
  92.0 12.2 %collective-permute-done.24 = bf16[1,1,512,1088]{2,3,1,0:T(8,128)(2,1)S(1)} collective-permute-done((bf16[1,1,512,1088]{2,3,1,0:T(8,128)(2,1)S(1)}, bf16[1,1,512,1088]{2,3,1,0:T(8,128)(2,1)S(1)}, u32[]{:S(2)}, u32[]{:S(2)}) %collective-permute-start.24) | collective-permute-done | bytes 1114144 | tf_op jit(solution)/shard_map/ppermute | solution.py:442
  120.1 9.9 %collective-permute-done.36 = bf16[2,136,1088]{2,1,0:T(8,128)(2,1)S(1)} collective-permute-done((bf16[2,136,1088]{2,1,0:T(8,128)(2,1)}, bf16[2,136,1088]{2,1,0:T(8,128)(2,1)S(1)}, u32[]{:S(2)}, u32[]{:S(2)}) %collective-permute-start.36) | collective-permute-done | bytes 591904 | tf_op jit(solution)/shard_map/ppermute | solution.py:66
  135.8 11.1 %collective-permute-done.21 = bf16[2,136,1088]{2,1,0:T(8,128)(2,1)S(1)} collective-permute-done((bf16[2,136,1088]{2,1,0:T(8,128)(2,1)S(1)}, bf16[2,136,1088]{2,1,0:T(8,128)(2,1)S(1)}, u32[]{:S(2)}, u32[]{:S(2)}) %collective-permute-start.21) | collective-permute-done | bytes 591904 | tf_op jit(solution)/shard_map/ppermute | solution.py:66
  184.7 10.4 %collective-permute-done.33 = bf16[2,136,1088]{2,1,0:T(8,128)(2,1)S(1)} collective-permute-done((bf16[2,136,1088]{2,1,0:T(8,128)(2,1)S(1)}, bf16[2,136,1088]{2,1,0:T(8,128)(2,1)S(1)}, u32[]{:S(2)}, u32[]{:S(2)}) %collective-permute-start.33) | collective-permute-done | bytes 591904 | tf_op jit(solution)/shard_map/ppermute | solution.py:52
  199.0 9.3 collective-permute-done.41
  244.5 21.3 %collective-permute-done.34 = bf16[2,2,136,1088]{3,2,1,0:T(8,128)(2,1)} collective-permute-done((bf16[2,2,136,1088]{3,2,1,0:T(8,128)(2,1)}, bf16[2,2,136,1088]{3,2,1,0:T(8,128)(2,1)}, u32[]{:S(2)}, u32[]{:S(2)}) %collective-permute-start.34) | collective-permute-done | bytes 1183776 | tf_op jit(solution)/shard_map/ppermute | solution.py:52
  287.5 12.8 %shard_map.271 = (bf16[1,512,1088]{2,1,0:T(8,128)(2,1)S(1)}, f32[1,9,2,512]{3,2,1,0:T(2,128)S(1)}) custom-call(s32[1]{0:T(128)} %bitcast.1.place_ref, bf16[1,512,1088]{2,1,0:T(8,128)(2,1)S(1)} %fusion.47.q_ref, bf16[1,2048,1088]{2,1,0:T(8,128)(2,1)S(1)} %fusion.17.k_ref, bf16[1,2048,1088]{2,1,0:T(8,128)(2,1)S(1)} %fusion.18.v_ref, ...), custom_call_target="tpu_custom_call" | custom-call | flops 9663676416 | bytes 13369344 | tf_op jit(solution)/shard_map/pallas_call | solution.py:387
  307.0 11.7 %collective-permute-start.39 = (bf16[2,2,136,1088]{3,2,0,1:T(8,128)(2,1)S(1)}, bf16[2,2,136,1088]{3,2,0,1:T(8,128)(2,1)S(1)}, u32[]{:S(2)}, u32[]{:S(2)}) collective-permute-start(bf16[2,2,136,1088]{3,2,0,1:T(8,128)(2,1)S(1)} %get-tuple-element.43), channel_id=1, source_target_pairs={{0,1},{1,0},{2,3},{3,2},{4,5},{5,4},{6,7},{7,6},{8,9},{9,8},{10,11... | collective-permute-start | bytes 3551240 | tf_op jit(solution)/shard_map/ppermute | solution.py:52
  344.6 20.6 %convert_reduce_fusion.2 = (f32[4352]{0:T(1024)}, bf16[512,4352]{0,1:T(8,128)(2,1)}) fusion(f32[4352]{0:T(1024)S(1)} %reshape.870, f32[512,1088]{0,1:T(8,128)} %fusion.139, f32[512,1088]{0,1:T(8,128)} %fusion.138, f32[512,1088]{0,1:T(8,128)} %fusion.137, f32[512,1088]{0,1:T(8,128)} %fusion.136, bf16[4352,1088]{1,0:T(8,128)(2,1)} %bitcast.74, ...), kind=kOutput, calls=%fused_computation.31 | convolution fusion | flops 4906545152 | bytes 23988224 | tf_op jit(solution)/shard_map/dot_general | solution.py:34
  393.5 13.5 %fusion.23 = bf16[1,1088,1088]{2,1,0:T(8,128)(2,1)} fusion(bf16[512,1088]{0,1:T(8,128)(2,1)S(1)} %copy-done.88, bf16[512,4352]{0,1:T(8,128)(2,1)S(1)} %copy-done.89), kind=kOutput, calls=%fused_computation.48 | convolution fusion | flops 1213337600 | bytes 4595712 | tf_op jit(solution)/shard_map/dot_general | solution.py:28
  407.0 13.5 %convolution_convert_fusion = bf16[4352,1088]{0,1:T(8,128)(2,1)} fusion(bf16[1,512,1088]{1,2,0:T(8,128)(2,1)S(1)} %copy-done.54, f32[512,1088]{0,1:T(8,128)} %fusion.139, f32[512,1088]{0,1:T(8,128)} %fusion.138, f32[512,1088]{0,1:T(8,128)} %fusion.137, f32[512,1088]{0,1:T(8,128)} %fusion.136, f32[4352]{0:T(1024)S(1)} %reshape.870), kind=kOutput, calls=%fused_computation | convolution fusion | flops 4882317312 | bytes 19514368 | tf_op jit(solution)/shard_map/dot_general | solution.py:28
  420.5 22.9 %shard_map.272 = (bf16[1,512,1088]{2,1,0:T(8,128)(2,1)S(1)}, bf16[1,2048,1088]{2,1,0:T(8,128)(2,1)S(1)}, bf16[1,2048,1088]{2,1,0:T(8,128)(2,1)}) custom-call(s32[1]{0:T(128)} %bitcast.1.place_ref, bf16[1,512,1088]{2,1,0:T(8,128)(2,1)S(1)} %fusion.47.q_ref, bf16[1,2048,1088]{2,1,0:T(8,128)(2,1)} %copy-done.1, bf16[1,2048,1088]{2,1,0:T(8,128)(2,1)} %copy-done.2, ...), custom_call_target="tpu_custom_call" | custom-call | flops 24159191040 | bytes 22282240 | tf_op jit(solution)/shard_map/pallas_call | solution.py:409
  443.3 12.9 %fusion.20 = bf16[1,1088,1088]{2,1,0:T(8,128)(2,1)} fusion(bf16[2048,1088]{1,0:T(8,128)(2,1)} %bitcast.582, bf16[1,2048,1088]{2,1,0:T(8,128)(2,1)} %get-tuple-element.24), kind=kOutput, calls=%fused_computation.45 | convolution fusion | flops 4849799168 | bytes 11280384 | tf_op jit(solution)/shard_map/dot_general | solution.py:28
  463.2 11.3 %fusion.19 = bf16[1,1088,1088]{2,1,0:T(8,128)(2,1)} fusion(bf16[2048,1088]{1,0:T(8,128)(2,1)} %bitcast.583, bf16[1,2048,1088]{2,1,0:T(8,128)(2,1)} %copy-done), kind=kOutput, calls=%fused_computation.44 | convolution fusion | flops 4849799168 | bytes 11280384 | tf_op jit(solution)/shard_map/dot_general | solution.py:28
  481.1 7.9 pad_maximum_fusion.2
  493.7 15.6 %collective-permute-start.48 = (bf16[2,2,1,512,1088]{3,4,2,1,0:T(8,128)(2,1)}, bf16[2,2,1,512,1088]{3,4,2,1,0:T(8,128)(2,1)}, u32[]{:S(2)}, u32[]{:S(2)}) collective-permute-start(bf16[2,2,1,512,1088]{3,4,2,1,0:T(8,128)(2,1)} %dynamic-slice_bitcast_fusion), channel_id=1, source_target_pairs={{0,1},{1,0},{2,3},{3,2},{4,5},{5,4},{6,7},{7,6},{8,9},{9,8},{10,11... | collective-permute-start | bytes 13369352 | tf_op jit(solution)/shard_map/ppermute | solution.py:461
  541.9 13.9 %copy.170 = bf16[4352,1088]{1,0:T(8,128)(2,1)} copy(bf16[4352,1088]{0,1:T(8,128)(2,1)} %convolution_convert_fusion) | data formatting | bytes 18939904 | tf_op jit(solution)/shard_map/convert_element_type | solution.py:555
  590.8 10.4 %collective-permute-done.62 = bf16[2,136,1088]{2,1,0:T(8,128)(2,1)S(1)} collective-permute-done((bf16[2,136,1088]{2,1,0:T(8,128)(2,1)S(1)}, bf16[2,136,1088]{2,1,0:T(8,128)(2,1)S(1)}, u32[]{:S(2)}, u32[]{:S(2)}) %collective-permute-start.62) | collective-permute-done | bytes 591904 | tf_op jit(solution)/shard_map/ppermute | solution.py:52
  606.1 10.8 %collective-permute-done.60 = bf16[2,136,1088]{2,1,0:T(8,128)(2,1)S(1)} collective-permute-done((bf16[2,136,1088]{2,1,0:T(8,128)(2,1)}, bf16[2,136,1088]{2,1,0:T(8,128)(2,1)S(1)}, u32[]{:S(2)}, u32[]{:S(2)}) %collective-permute-start.60) | collective-permute-done | bytes 591904 | tf_op jit(solution)/shard_map/ppermute | solution.py:52
  626.9 54.1 %collective-permute-start.81 = (bf16[2,2,136,1088]{3,2,1,0:T(8,128)(2,1)S(1)}, bf16[2,2,136,1088]{3,2,1,0:T(8,128)(2,1)S(1)}, u32[]{:S(2)}, u32[]{:S(2)}) collective-permute-start(bf16[2,2,136,1088]{3,2,1,0:T(8,128)(2,1)S(1)} %select_bitcast_fusion.2), channel_id=1, source_target_pairs={{0,2},{1,3},{2,0},{3,1},{4,6},{5,7},{6,4},{7,5},{8,10},{9,11},{10,... | collective-permute-start | bytes 3551240 | tf_op jit(solution)/shard_map/ppermute | solution.py:52
  694.5 15.1 %collective-permute-done.81 = bf16[2,2,136,1088]{3,2,1,0:T(8,128)(2,1)S(1)} collective-permute-done((bf16[2,2,136,1088]{3,2,1,0:T(8,128)(2,1)S(1)}, bf16[2,2,136,1088]{3,2,1,0:T(8,128)(2,1)S(1)}, u32[]{:S(2)}, u32[]{:S(2)}) %collective-permute-start.81) | collective-permute-done | bytes 1183776 | tf_op jit(solution)/shard_map/ppermute | solution.py:52
  712.1 24.3 %collective-permute-done.78 = bf16[2,2,136,1088]{3,2,1,0:T(8,128)(2,1)S(1)} collective-permute-done((bf16[2,2,136,1088]{3,2,1,0:T(8,128)(2,1)S(1)}, bf16[2,2,136,1088]{3,2,1,0:T(8,128)(2,1)S(1)}, u32[]{:S(2)}, u32[]{:S(2)}) %collective-permute-start.78) | collective-permute-done | bytes 1183776 | tf_op jit(solution)/shard_map/ppermute | solution.py:52
  736.4 9.3 collective-permute-start.65
  746.2 17.0 %collective-permute-done.75 = bf16[2,2,136,1088]{3,2,1,0:T(8,128)(2,1)S(1)} collective-permute-done((bf16[2,2,136,1088]{3,2,1,0:T(8,128)(2,1)S(1)}, bf16[2,2,136,1088]{3,2,1,0:T(8,128)(2,1)S(1)}, u32[]{:S(2)}, u32[]{:S(2)}) %collective-permute-start.75) | collective-permute-done | bytes 1183776 | tf_op jit(solution)/shard_map/ppermute | solution.py:52
  765.3 13.0 %collective-permute-done.82 = bf16[2,136,1088]{2,1,0:T(8,128)(2,1)S(1)} collective-permute-done((bf16[2,136,1088]{2,1,0:T(8,128)(2,1)S(1)}, bf16[2,136,1088]{2,1,0:T(8,128)(2,1)S(1)}, u32[]{:S(2)}, u32[]{:S(2)}) %collective-permute-start.82) | collective-permute-done | bytes 591904 | tf_op jit(solution)/shard_map/ppermute | solution.py:52
  786.8 10.6 %collective-permute-start.83 = (bf16[2,136,1088]{2,1,0:T(8,128)(2,1)S(1)}, bf16[2,136,1088]{2,1,0:T(8,128)(2,1)S(1)}, u32[]{:S(2)}, u32[]{:S(2)}) collective-permute-start(bf16[2,136,1088]{2,1,0:T(8,128)(2,1)S(1)} %fusion.86), channel_id=1, source_target_pairs={{0,8},{4,12},{1,9},{5,13},{2,10},{6,14},{3,11},{7,15}} | collective-permute-start | bytes 1775624 | tf_op jit(solution)/shard_map/ppermute | solution.py:103
  800.4 9.5 %collective-permute-done.83 = bf16[2,136,1088]{2,1,0:T(8,128)(2,1)S(1)} collective-permute-done((bf16[2,136,1088]{2,1,0:T(8,128)(2,1)S(1)}, bf16[2,136,1088]{2,1,0:T(8,128)(2,1)S(1)}, u32[]{:S(2)}, u32[]{:S(2)}) %collective-permute-start.83) | collective-permute-done | bytes 591904 | tf_op jit(solution)/shard_map/ppermute | solution.py:103
  836.6 11.0 %collective-permute-done.68 = bf16[2,136,1088]{2,1,0:T(8,128)(2,1)S(1)} collective-permute-done((bf16[2,136,1088]{2,1,0:T(8,128)(2,1)S(1)}, bf16[2,136,1088]{2,1,0:T(8,128)(2,1)S(1)}, u32[]{:S(2)}, u32[]{:S(2)}) %collective-permute-start.68) | collective-permute-done | bytes 591904 | tf_op jit(solution)/shard_map/ppermute | solution.py:104
  852.5 8.7 collective-permute-start.85
  863.8 18.5 %collective-permute-done.49 = bf16[1,2,1,512,1088]{3,4,2,1,0:T(8,128)(2,1)S(1)} collective-permute-done((bf16[1,2,1,512,1088]{3,4,2,1,0:T(8,128)(2,1)S(1)}, bf16[1,2,1,512,1088]{3,4,2,1,0:T(8,128)(2,1)S(1)}, u32[]{:S(2)}, u32[]{:S(2)}) %collective-permute-start.49) | collective-permute-done | bytes 2228256 | tf_op jit(solution)/shard_map/ppermute | solution.py:461
  895.4 15.6 %fusion.45 = bf16[1,512,1088]{1,2,0:T(8,128)(2,1)} fusion(f32[512,1088]{0,1:T(8,128)S(1)} %copy-done.5, bf16[4352,1088]{1,0:T(8,128)(2,1)} %bitcast.74, f32[1088]{0:T(1024)} %reshape.871, f32[512,1088]{0,1:T(8,128)} %fusion.139, f32[512,1088]{0,1:T(8,128)} %fusion.138, f32[512,1088]{0,1:T(8,128)} %fusion.137, f32[512,1088]{0,1:T(8,128)} %fusion.136, ...), kind=kOutput, calls=%fused_computation.106 | convolution fusion | flops 4879253504 | bytes 21746944 | tf_op jit(solution)/shard_map/dot_general | solution.py:549
  (620 shorter events, 463.9 us)
Async XLA Ops:
  19.7 53.6 %collective-permute-start.10 = (bf16[2,136,1088]{2,1,0:T(8,128)(2,1)}, bf16[2,136,1088]{2,1,0:T(8,128)(2,1)}, u32[]{:S(2)}, u32[]{:S(2)}) collective-permute-start(bf16[2,136,1088]{2,1,0:T(8,128)(2,1)} %fusion.120), channel_id=1, source_target_pairs={{0,4},{4,0},{8,12},{12,8},{16,20},{20,16},{24,28},{28,24},{1,5},{5... | collective-permute-start | bytes 1775624 | tf_op jit(solution)/shard_map/ppermute | solution.py:52
  19.8 71.4 %collective-permute-start.12 = (bf16[2,136,1088]{2,1,0:T(8,128)(2,1)}, bf16[2,136,1088]{2,1,0:T(8,128)(2,1)}, u32[]{:S(2)}, u32[]{:S(2)}) collective-permute-start(bf16[2,136,1088]{2,1,0:T(8,128)(2,1)} %fusion.120), channel_id=1, source_target_pairs={{8,0},{12,4},{16,8},{20,12},{24,16},{28,20},{9,1},{13,5},{17,9},{2... | collective-permute-start | bytes 1775624 | tf_op jit(solution)/shard_map/ppermute | solution.py:66
  26.8 64.5 %collective-permute-start.13 = (bf16[2,136,1088]{2,1,0:T(8,128)(2,1)}, bf16[2,136,1088]{2,1,0:T(8,128)(2,1)}, u32[]{:S(2)}, u32[]{:S(2)}) collective-permute-start(bf16[2,136,1088]{2,1,0:T(8,128)(2,1)} %fusion.120), channel_id=1, source_target_pairs={{0,8},{4,12},{8,16},{12,20},{16,24},{20,28},{1,9},{5,13},{9,17},{1... | collective-permute-start | bytes 1775624 | tf_op jit(solution)/shard_map/ppermute | solution.py:59
  34.3 45.8 %collective-permute-start.26 = (bf16[2,136,1088]{2,1,0:T(8,128)(2,1)}, bf16[2,136,1088]{2,1,0:T(8,128)(2,1)}, u32[]{:S(2)}, u32[]{:S(2)}) collective-permute-start(bf16[2,136,1088]{2,1,0:T(8,128)(2,1)} %fusion.117), channel_id=1, source_target_pairs={{0,4},{4,0},{8,12},{12,8},{16,20},{20,16},{24,28},{28,24},{1,5},{5... | collective-permute-start | bytes 1775624 | tf_op jit(solution)/shard_map/ppermute | solution.py:52
  91.2 81.2 %collective-permute-start.11 = (bf16[2,2,136,1088]{3,2,0,1:T(8,128)(2,1)S(1)}, bf16[2,2,136,1088]{3,2,0,1:T(8,128)(2,1)S(1)}, u32[]{:S(2)}, u32[]{:S(2)}) collective-permute-start(bf16[2,2,136,1088]{3,2,0,1:T(8,128)(2,1)S(1)} %maximum_bitcast_fusion.1), channel_id=1, source_target_pairs={{0,1},{1,0},{2,3},{3,2},{4,5},{5,4},{6,7},{7,6},{8,9},{9,8},{10,11... | collective-permute-start | bytes 3551240 | tf_op jit(solution)/shard_map/ppermute | solution.py:52
  105.6 59.0 %collective-permute-start.27 = (bf16[2,2,136,1088]{3,2,1,0:T(8,128)(2,1)S(1)}, bf16[2,2,136,1088]{3,2,1,0:T(8,128)(2,1)S(1)}, u32[]{:S(2)}, u32[]{:S(2)}) collective-permute-start(bf16[2,2,136,1088]{3,2,1,0:T(8,128)(2,1)S(1)} %pad_maximum_fusion.5), channel_id=1, source_target_pairs={{0,2},{1,3},{2,0},{3,1},{4,6},{5,7},{6,4},{7,5},{8,10},{9,11},{10,... | collective-permute-start | bytes 3551240 | tf_op jit(solution)/shard_map/ppermute | solution.py:52
  120.1 94.0 %collective-permute-start.25 = (bf16[1,2,512,1088]{2,3,1,0:T(8,128)(2,1)}, bf16[1,2,512,1088]{2,3,1,0:T(8,128)(2,1)}, u32[]{:S(2)}, u32[]{:S(2)}) collective-permute-start(bf16[1,2,512,1088]{2,3,1,0:T(8,128)(2,1)} %maximum_bitcast_fusion), channel_id=1, source_target_pairs={{0,1},{1,0},{2,3},{3,2},{4,5},{5,4},{6,7},{7,6},{8,9},{9,8},{10,11... | collective-permute-start | bytes 6684680 | tf_op jit(solution)/shard_map/ppermute | solution.py:442
  163.7 70.2 %collective-permute-start.20 = (bf16[2,2,136,1088]{3,2,0,1:T(8,128)(2,1)}, bf16[2,2,136,1088]{3,2,0,1:T(8,128)(2,1)}, u32[]{:S(2)}, u32[]{:S(2)}) collective-permute-start(bf16[2,2,136,1088]{3,2,0,1:T(8,128)(2,1)} %maximum_bitcast_fusion.3), channel_id=1, source_target_pairs={{0,1},{1,0},{2,3},{3,2},{4,5},{5,4},{6,7},{7,6},{8,9},{9,8},{10,11... | collective-permute-start | bytes 3551240 | tf_op jit(solution)/shard_map/ppermute | solution.py:52
  172.4 37.6 %collective-permute-start.44 = (bf16[2,2,136,1088]{3,2,1,0:T(8,128)(2,1)}, bf16[2,2,136,1088]{3,2,1,0:T(8,128)(2,1)}, u32[]{:S(2)}, u32[]{:S(2)}) collective-permute-start(bf16[2,2,136,1088]{3,2,1,0:T(8,128)(2,1)} %get-tuple-element.55), channel_id=1, source_target_pairs={{0,1},{1,0},{2,3},{3,2},{4,5},{5,4},{6,7},{7,6},{8,9},{9,8},{10,11... | collective-permute-start | bytes 3551240 | tf_op jit(solution)/shard_map/ppermute | solution.py:52
  208.2 98.3 %collective-permute-start.38 = (bf16[2,2,136,1088]{3,2,1,0:T(8,128)(2,1)}, bf16[2,2,136,1088]{3,2,1,0:T(8,128)(2,1)}, u32[]{:S(2)}, u32[]{:S(2)}) collective-permute-start(bf16[2,2,136,1088]{3,2,1,0:T(8,128)(2,1)} %pad_maximum_fusion.7), channel_id=1, source_target_pairs={{0,2},{1,3},{2,0},{3,1},{4,6},{5,7},{6,4},{7,5},{8,10},{9,11},{10,... | collective-permute-start | bytes 3551240 | tf_op jit(solution)/shard_map/ppermute | solution.py:52
  214.1 51.7 %collective-permute-start.34 = (bf16[2,2,136,1088]{3,2,1,0:T(8,128)(2,1)}, bf16[2,2,136,1088]{3,2,1,0:T(8,128)(2,1)}, u32[]{:S(2)}, u32[]{:S(2)}) collective-permute-start(bf16[2,2,136,1088]{3,2,1,0:T(8,128)(2,1)} %pad_maximum_fusion.6), channel_id=1, source_target_pairs={{0,2},{1,3},{2,0},{3,1},{4,6},{5,7},{6,4},{7,5},{8,10},{9,11},{10,... | collective-permute-start | bytes 3551240 | tf_op jit(solution)/shard_map/ppermute | solution.py:52
  230.0 92.8 %collective-permute-start.42 = (bf16[2,2,136,1088]{3,2,1,0:T(8,128)(2,1)}, bf16[2,2,136,1088]{3,2,1,0:T(8,128)(2,1)S(1)}, u32[]{:S(2)}, u32[]{:S(2)}) collective-permute-start(bf16[2,2,136,1088]{3,2,1,0:T(8,128)(2,1)} %pad_maximum_fusion.8), channel_id=1, source_target_pairs={{0,2},{1,3},{2,0},{3,1},{4,6},{5,7},{6,4},{7,5},{8,10},{9,11},{10,... | collective-permute-start | bytes 3551240 | tf_op jit(solution)/shard_map/ppermute | solution.py:52
  268.9 49.8 %collective-permute-start.45 = (bf16[2,2,136,1088]{3,2,1,0:T(8,128)(2,1)}, bf16[2,2,136,1088]{3,2,1,0:T(8,128)(2,1)S(1)}, u32[]{:S(2)}, u32[]{:S(2)}) collective-permute-start(bf16[2,2,136,1088]{3,2,1,0:T(8,128)(2,1)} %get-tuple-element.53), channel_id=1, source_target_pairs={{0,1},{1,0},{2,3},{3,2},{4,5},{5,4},{6,7},{7,6},{8,9},{9,8},{10,11... | collective-permute-start | bytes 3551240 | tf_op jit(solution)/shard_map/ppermute | solution.py:52
  493.7 317.1 %collective-permute-start.48 = (bf16[2,2,1,512,1088]{3,4,2,1,0:T(8,128)(2,1)}, bf16[2,2,1,512,1088]{3,4,2,1,0:T(8,128)(2,1)}, u32[]{:S(2)}, u32[]{:S(2)}) collective-permute-start(bf16[2,2,1,512,1088]{3,4,2,1,0:T(8,128)(2,1)} %dynamic-slice_bitcast_fusion), channel_id=1, source_target_pairs={{0,1},{1,0},{2,3},{3,2},{4,5},{5,4},{6,7},{7,6},{8,9},{9,8},{10,11... | collective-permute-start | bytes 13369352 | tf_op jit(solution)/shard_map/ppermute | solution.py:461
  521.2 57.8 %collective-permute-start.61 = (bf16[2,2,136,1088]{3,2,1,0:T(8,128)(2,1)}, bf16[2,2,136,1088]{3,2,1,0:T(8,128)(2,1)}, u32[]{:S(2)}, u32[]{:S(2)}) collective-permute-start(bf16[2,2,136,1088]{3,2,1,0:T(8,128)(2,1)} %bitcast.548), channel_id=1, source_target_pairs={{0,1},{1,0},{2,3},{3,2},{4,5},{5,4},{6,7},{7,6},{8,9},{9,8},{10,11... | collective-permute-start | bytes 3551240 | tf_op jit(solution)/shard_map/ppermute | solution.py:52
  522.4 58.5 %collective-permute-start.59 = (bf16[2,2,136,1088]{3,2,1,0:T(8,128)(2,1)}, bf16[2,2,136,1088]{3,2,1,0:T(8,128)(2,1)}, u32[]{:S(2)}, u32[]{:S(2)}) collective-permute-start(bf16[2,2,136,1088]{3,2,1,0:T(8,128)(2,1)} %bitcast.549), channel_id=1, source_target_pairs={{0,1},{1,0},{2,3},{3,2},{4,5},{5,4},{6,7},{7,6},{8,9},{9,8},{10,11... | collective-permute-start | bytes 3551240 | tf_op jit(solution)/shard_map/ppermute | solution.py:52
  524.0 58.9 %collective-permute-start.57 = (bf16[2,2,136,1088]{3,2,1,0:T(8,128)(2,1)}, bf16[2,2,136,1088]{3,2,1,0:T(8,128)(2,1)}, u32[]{:S(2)}, u32[]{:S(2)}) collective-permute-start(bf16[2,2,136,1088]{3,2,1,0:T(8,128)(2,1)} %bitcast.550), channel_id=1, source_target_pairs={{0,1},{1,0},{2,3},{3,2},{4,5},{5,4},{6,7},{7,6},{8,9},{9,8},{10,11... | collective-permute-start | bytes 3551240 | tf_op jit(solution)/shard_map/ppermute | solution.py:52
  525.2 59.7 %collective-permute-start.55 = (bf16[2,2,136,1088]{3,2,1,0:T(8,128)(2,1)}, bf16[2,2,136,1088]{3,2,1,0:T(8,128)(2,1)}, u32[]{:S(2)}, u32[]{:S(2)}) collective-permute-start(bf16[2,2,136,1088]{3,2,1,0:T(8,128)(2,1)} %bitcast.551), channel_id=1, source_target_pairs={{0,1},{1,0},{2,3},{3,2},{4,5},{5,4},{6,7},{7,6},{8,9},{9,8},{10,11... | collective-permute-start | bytes 3551240 | tf_op jit(solution)/shard_map/ppermute | solution.py:52
  580.8 39.0 %collective-permute-start.77 = (bf16[2,2,2,136,1088]{4,3,2,1,0:T(8,128)(2,1)}, bf16[2,2,2,136,1088]{4,3,2,1,0:T(8,128)(2,1)S(1)}, u32[]{:S(2)}, u32[]{:S(2)}) collective-permute-start(bf16[2,2,2,136,1088]{4,3,2,1,0:T(8,128)(2,1)} %fusion.53), channel_id=1, source_target_pairs={{0,1},{1,0},{2,3},{3,2},{4,5},{5,4},{6,7},{7,6},{8,9},{9,8},{10,11... | collective-permute-start | bytes 7102472 | tf_op jit(solution)/shard_map/ppermute | solution.py:52
  582.9 38.5 %collective-permute-start.74 = (bf16[2,2,2,136,1088]{4,3,2,1,0:T(8,128)(2,1)}, bf16[2,2,2,136,1088]{4,3,2,1,0:T(8,128)(2,1)S(1)}, u32[]{:S(2)}, u32[]{:S(2)}) collective-permute-start(bf16[2,2,2,136,1088]{4,3,2,1,0:T(8,128)(2,1)} %fusion.57), channel_id=1, source_target_pairs={{0,1},{1,0},{2,3},{3,2},{4,5},{5,4},{6,7},{7,6},{8,9},{9,8},{10,11... | collective-permute-start | bytes 7102472 | tf_op jit(solution)/shard_map/ppermute | solution.py:52
  617.2 64.8 %collective-permute-start.58 = (bf16[2,136,1088]{2,1,0:T(8,128)(2,1)}, bf16[2,136,1088]{2,1,0:T(8,128)(2,1)S(1)}, u32[]{:S(2)}, u32[]{:S(2)}) collective-permute-start(bf16[2,136,1088]{2,1,0:T(8,128)(2,1)} %dynamic-slice_bitcast_fusion.12), channel_id=1, source_target_pairs={{0,4},{4,0},{8,12},{12,8},{16,20},{20,16},{24,28},{28,24},{1,5},{5... | collective-permute-start | bytes 1775624 | tf_op jit(solution)/shard_map/ppermute | solution.py:52
  619.9 215.2 %collective-permute-start.56 = (bf16[2,136,1088]{2,1,0:T(8,128)(2,1)}, bf16[2,136,1088]{2,1,0:T(8,128)(2,1)}, u32[]{:S(2)}, u32[]{:S(2)}) collective-permute-start(bf16[2,136,1088]{2,1,0:T(8,128)(2,1)} %dynamic-slice_bitcast_fusion.13), channel_id=1, source_target_pairs={{0,4},{4,0},{8,12},{12,8},{16,20},{20,16},{24,28},{28,24},{1,5},{5... | collective-permute-start | bytes 1775624 | tf_op jit(solution)/shard_map/ppermute | solution.py:52
  621.5 67.0 %collective-permute-start.64 = (bf16[2,136,1088]{2,1,0:T(8,128)(2,1)S(1)}, bf16[2,136,1088]{2,1,0:T(8,128)(2,1)S(1)}, u32[]{:S(2)}, u32[]{:S(2)}) collective-permute-start(bf16[2,136,1088]{2,1,0:T(8,128)(2,1)S(1)} %fusion.81), channel_id=1, source_target_pairs={{0,8},{4,12},{8,16},{12,20},{1,9},{5,13},{9,17},{13,21},{2,10},{6,... | collective-permute-start | bytes 1775624 | tf_op jit(solution)/shard_map/ppermute | solution.py:103
  626.9 82.6 %collective-permute-start.81 = (bf16[2,2,136,1088]{3,2,1,0:T(8,128)(2,1)S(1)}, bf16[2,2,136,1088]{3,2,1,0:T(8,128)(2,1)S(1)}, u32[]{:S(2)}, u32[]{:S(2)}) collective-permute-start(bf16[2,2,136,1088]{3,2,1,0:T(8,128)(2,1)S(1)} %select_bitcast_fusion.2), channel_id=1, source_target_pairs={{0,2},{1,3},{2,0},{3,1},{4,6},{5,7},{6,4},{7,5},{8,10},{9,11},{10,... | collective-permute-start | bytes 3551240 | tf_op jit(solution)/shard_map/ppermute | solution.py:52
  682.0 54.4 %collective-permute-start.78 = (bf16[2,2,136,1088]{3,2,1,0:T(8,128)(2,1)S(1)}, bf16[2,2,136,1088]{3,2,1,0:T(8,128)(2,1)S(1)}, u32[]{:S(2)}, u32[]{:S(2)}) collective-permute-start(bf16[2,2,136,1088]{3,2,1,0:T(8,128)(2,1)S(1)} %select_bitcast_fusion.3), channel_id=1, source_target_pairs={{0,2},{1,3},{2,0},{3,1},{4,6},{5,7},{6,4},{7,5},{8,10},{9,11},{10,... | collective-permute-start | bytes 3551240 | tf_op jit(solution)/shard_map/ppermute | solution.py:52
  690.5 72.7 %collective-permute-start.75 = (bf16[2,2,136,1088]{3,2,1,0:T(8,128)(2,1)S(1)}, bf16[2,2,136,1088]{3,2,1,0:T(8,128)(2,1)S(1)}, u32[]{:S(2)}, u32[]{:S(2)}) collective-permute-start(bf16[2,2,136,1088]{3,2,1,0:T(8,128)(2,1)S(1)} %select_bitcast_fusion.4), channel_id=1, source_target_pairs={{0,2},{1,3},{2,0},{3,1},{4,6},{5,7},{6,4},{7,5},{8,10},{9,11},{10,... | collective-permute-start | bytes 3551240 | tf_op jit(solution)/shard_map/ppermute | solution.py:52
  709.5 77.2 %collective-permute-start.72 = (bf16[2,2,136,1088]{3,2,1,0:T(8,128)(2,1)S(1)}, bf16[2,2,136,1088]{3,2,1,0:T(8,128)(2,1)S(1)}, u32[]{:S(2)}, u32[]{:S(2)}) collective-permute-start(bf16[2,2,136,1088]{3,2,1,0:T(8,128)(2,1)S(1)} %select_bitcast_fusion.5), channel_id=1, source_target_pairs={{0,2},{1,3},{2,0},{3,1},{4,6},{5,7},{6,4},{7,5},{8,10},{9,11},{10,... | collective-permute-start | bytes 3551240 | tf_op jit(solution)/shard_map/ppermute | solution.py:52
  736.4 100.2 %collective-permute-start.65 = (bf16[2,136,1088]{2,1,0:T(8,128)(2,1)}, bf16[2,136,1088]{2,1,0:T(8,128)(2,1)}, u32[]{:S(2)}, u32[]{:S(2)}) collective-permute-start(bf16[2,136,1088]{2,1,0:T(8,128)(2,1)} %get-tuple-element.34), channel_id=1, source_target_pairs={{0,8},{4,12},{8,16},{12,20},{16,24},{20,28},{1,9},{5,13},{9,17},{1... | collective-permute-start | bytes 1775624 | tf_op jit(solution)/shard_map/ppermute | solution.py:103
  829.0 53.4 %collective-permute-start.49 = (bf16[1,2,1,512,1088]{3,4,2,1,0:T(8,128)(2,1)S(1)}, bf16[1,2,1,512,1088]{3,4,2,1,0:T(8,128)(2,1)S(1)}, u32[]{:S(2)}, u32[]{:S(2)}) collective-permute-start(bf16[1,2,1,512,1088]{3,4,2,1,0:T(8,128)(2,1)S(1)} %dynamic-slice_bitcast_fusion.5), channel_id=1, source_target_pairs={{2,0},{3,1},{6,4},{7,5},{10,8},{11,9},{14,12},{15,13},{18,16},{19,... | collective-permute-start | bytes 6684680 | tf_op jit(solution)/shard_map/ppermute | solution.py:461
  835.1 58.1 %collective-permute-start.73 = (bf16[2,136,1088]{2,1,0:T(8,128)(2,1)}, bf16[2,136,1088]{2,1,0:T(8,128)(2,1)}, u32[]{:S(2)}, u32[]{:S(2)}) collective-permute-start(bf16[2,136,1088]{2,1,0:T(8,128)(2,1)} %dynamic-slice_bitcast_fusion.9), channel_id=1, source_target_pairs={{0,4},{4,0},{8,12},{12,8},{16,20},{20,16},{24,28},{28,24},{1,5},{5... | collective-permute-start | bytes 1775624 | tf_op jit(solution)/shard_map/ppermute | solution.py:52
  850.0 63.9 %collective-permute-start.69 = (bf16[2,136,1088]{2,1,0:T(8,128)(2,1)}, bf16[2,136,1088]{2,1,0:T(8,128)(2,1)}, u32[]{:S(2)}, u32[]{:S(2)}) collective-permute-start(bf16[2,136,1088]{2,1,0:T(8,128)(2,1)} %add_convert_fusion.7), channel_id=1, source_target_pairs={{0,2},{1,3},{2,0},{3,1},{4,6},{5,7},{6,4},{7,5},{8,10},{9,11},{10,... | collective-permute-start | bytes 1775624 | tf_op jit(solution)/shard_map/ppermute | solution.py:52
  852.5 40.7 %collective-permute-start.85 = (bf16[2,136,1088]{2,1,0:T(8,128)(2,1)}, bf16[2,136,1088]{2,1,0:T(8,128)(2,1)}, u32[]{:S(2)}, u32[]{:S(2)}) collective-permute-start(bf16[2,136,1088]{2,1,0:T(8,128)(2,1)} %get-tuple-element.32), channel_id=1, source_target_pairs={{0,8},{4,12},{8,16},{12,20},{16,24},{20,28},{1,9},{5,13},{9,17},{1... | collective-permute-start | bytes 1775624 | tf_op jit(solution)/shard_map/ppermute | solution.py:103
  (178 other events, 3446.8 us)

commit v3 on v2

--- a/solution.py
+++ b/solution.py
@@ -142,7 +142,7 @@
     return full.reshape(4, links.shards * rows, features)
 
 
-def gather_second(links, w_up, w_down):
+def begin_second(links, w_up, w_down):
     rows = w_up.shape[0]
     features = w_down.shape[1]
     own_up = lax.dynamic_slice_in_dim(quarters(w_up, features), 2 * links.core, 2, 0)
@@ -150,10 +150,15 @@
         w_down.reshape(2, 2, rows, features), links.core, 0, keepdims=False
     )
     mine = jnp.where(links.even, own_up, own_down)
+    pairs = links.gather_pairs(mine)
+    return pairs, [links.swap(pair, "context", 2) for pair in pairs]
+
+
+def finish_second(links, pairs, others):
+    rows, features = pairs[0].shape[-2:]
     up = jnp.zeros((4, links.shards, rows, features), jnp.bfloat16)
     down = jnp.zeros((links.shards, 2, 2, rows, features), jnp.bfloat16)
-    for k, pair in enumerate(links.gather_pairs(mine)):
-        other = links.swap(pair, "context", 2)
+    for k, (pair, other) in enumerate(zip(pairs, others)):
         up_half = jnp.where(links.even, pair, other).transpose(1, 0, 2, 3)
         down_half = jnp.where(links.even, other, pair)
         up_other = links.swap(up_half, "context", 1)
@@ -175,22 +180,41 @@
     return add_low(kept, links.swap(sent, "fsdp", 1))
 
 
-def reduce_second(links, grad_up, grad_down):
+def core_halves(links, grads):
+    halves = []
+    for j in range(2):
+        kept = jnp.where(links.core == 0, grads[j], grads[2 + j])
+        sent = jnp.where(links.core == 0, grads[2 + j], grads[j])
+        halves.append(add_low(kept, links.swap(sent, "context", 1)))
+    return halves
+
+
+def core_rows(links, grad_down):
     features = grad_down.shape[1]
-    rows = features // links.shards
-    up = grad_up.reshape(2, 2, links.depth, 2, rows, features)
-    down = grad_down.reshape(links.depth, 2, 2, 2, rows, features)
+    split = grad_down.reshape(links.depth, 2, 2, 2, features // links.shards, features)
+    sent = lax.dynamic_index_in_dim(split, 1 - links.core, 2, keepdims=False)
+    kept = lax.dynamic_index_in_dim(split, links.core, 2, keepdims=False)
+    return add_low(kept, links.swap(sent, "context", 1))
+
+
+def block_of(links, halves, at):
+    features = halves[0].shape[1]
+    parts = [
+        half.reshape(links.depth, 2, features // links.shards, features) for half in halves
+    ]
+    return jnp.stack(
+        [lax.dynamic_index_in_dim(part, at, 0, keepdims=False) for part in parts], axis=1
+    )
+
+
+def reduce_second(links, up_halves, down_half):
     blocks = []
     for k in range(links.depth):
         at = links.block_at(k)
-        up_k = lax.dynamic_index_in_dim(up, at, 2, keepdims=False).transpose(0, 2, 1, 3, 4)
-        down_k = lax.dynamic_index_in_dim(down, at, 0, keepdims=False).transpose(1, 0, 2, 3, 4)
-        both = jnp.stack([up_k, down_k])
-        sent = lax.dynamic_index_in_dim(both, 1 - links.core, 1, keepdims=False)
-        kept = lax.dynamic_index_in_dim(both, links.core, 1, keepdims=False)
-        halves = add_low(kept, links.swap(sent, "context", 1))
-        sent = jnp.where(links.even, halves[1], halves[0])
-        kept = jnp.where(links.even, halves[0], halves[1])
+        up_k = block_of(links, up_halves, at)
+        down_k = lax.dynamic_index_in_dim(down_half, at, 0, keepdims=False)
+        sent = jnp.where(links.even, down_k, up_k)
+        kept = jnp.where(links.even, up_k, down_k)
         block = add_low(kept, links.swap(sent, "context", 2))
         block = links.sum_same_parity(block)
         blocks.append(other_x(links, block))
@@ -210,16 +234,10 @@
 
 
 def reduce_first(links, grads):
-    features = grads.shape[1]
-    rows = features // links.shards
-    split = grads.reshape(2, 2, links.depth, 2, rows, features)
-    blocks = []
-    for k in range(links.depth):
-        part = lax.dynamic_index_in_dim(split, links.block_at(k), 2, keepdims=False)
-        part = part.transpose(0, 2, 1, 3, 4)
-        sent = lax.dynamic_index_in_dim(part, 1 - links.core, 0, keepdims=False)
-        kept = lax.dynamic_index_in_dim(part, links.core, 0, keepdims=False)
-        blocks.append(other_x(links, add_low(kept, links.swap(sent, "context", 1))))
+    halves = core_halves(links, grads)
+    blocks = [
+        other_x(links, block_of(links, halves, links.block_at(k))) for k in range(links.depth)
+    ]
     mine = links.reduce_line(blocks).astype(jnp.bfloat16)
     mine = add_low(mine, links.swap(mine, "context", 2))
     mine = links.sum_same_parity(mine)
@@ -507,7 +525,7 @@
         up_bias,
     ) = small_full
     full_first = gather_first(links, w_qkv, w_out)
-    full_up, full_down = gather_second(links, w_up, w_down)
+    second_pairs, second_others = begin_second(links, w_up, w_down)
     full_out = full_first[3]
     gain_one = gain_one.astype(jnp.float32)
     shift_one = shift_one.astype(jnp.float32)
@@ -532,6 +550,10 @@
     attended_seqs, lse_kept = attend(
         place, query_seqs, keys_all, values_all, key_segs, own_segs
     )
+    attended_seqs, second_pairs, second_others = lax.optimization_barrier(
+        (attended_seqs, second_pairs, second_others)
+    )
+    full_up, full_down = finish_second(links, second_pairs, second_others)
     attended = attended_seqs.reshape(tokens, features)
     middle = (
         inputs
@@ -557,13 +579,14 @@
     grad_hidden = contract_cols(grad_out, full_down)
     gelu_value, gelu_pull = jax.vjp(gelu_tanh, pre_act)
     grad_pre = gelu_pull(grad_hidden)[0].astype(jnp.bfloat16)
-    grad_w_up = jnp.stack(
-        [
-            contract_rows(normed_two, grad_pre[:, j * features : (j + 1) * features])
-            for j in range(4)
-        ]
-    ).astype(jnp.bfloat16)
-    second_sums = reduce_second(links, grad_w_up, grad_w_down)
+    grads_up = [
+        contract_rows(normed_two, grad_pre[:, j * features : (j + 1) * features]).astype(
+            jnp.bfloat16
+        )
+        for j in range(4)
+    ]
+    down_half = core_rows(links, grad_w_down)
+    up_halves = core_halves(links, grads_up)
     grad_b_up = jnp.sum(grad_pre.astype(jnp.float32), axis=0)
     grad_normed_two = sum(
         contract_cols(grad_pre[:, j * features : (j + 1) * features], full_up[j]) for j in range(4)
@@ -577,6 +600,10 @@
     grad_attended = contract_cols(grad_middle_low, full_out).astype(jnp.bfloat16)
     grad_att_seqs = grad_attended.reshape(sequences, stretch, features)
 
+    grad_att_seqs, up_halves, down_half = lax.optimization_barrier(
+        (grad_att_seqs, up_halves, down_half)
+    )
+    second_sums = reduce_second(links, up_halves, down_half)
     grad_queries, key_parts, value_parts = attend_grads(
         place,
         query_seqs,
@@ -596,14 +623,15 @@
     own_parts = reduce_stretches(links, parts)
     grad_keys = own_parts[0].reshape(tokens, features)
     grad_values = own_parts[1].reshape(tokens, features)
-    grads_first = jnp.stack(
-        [
+    grads_first = [
+        grad.astype(jnp.bfloat16)
+        for grad in (
             contract_rows(normed, grad_queries),
             contract_rows(normed_all, key_rows),
             contract_rows(normed_all, value_rows),
             grad_w_out,
-        ]
-    ).astype(jnp.bfloat16)
+        )
+    ]
     first_sums = reduce_first(links, grads_first)
     grad_b_query = jnp.sum(grad_queries.astype(jnp.float32), axis=0)
     grad_b_value = jnp.sum(value_rows.astype(jnp.float32), axis=0)

time: 948 us -> 922 us (0.973)
  waiting for transfers between devices: 268 us -> 332 us
  local copies, waits for them, and re-layouts: 140 us -> 94.5 us
  starting transfers between devices: 222 us -> 194 us
  other arithmetic: 119 us -> 106 us
    ppermute x57 -> x54, waiting for transfers between devices: 162 us -> 250 us  [swap(): return lax.ppermute(value, axis, [(i, i ^ bit) for i in range(count)])]
    another operation x8 -> x4, local copies, waits for them, and re-layouts: 21.8 us -> 2.32 us
    ppermute x2, waiting for transfers between devices: 18.5 us -> 0.01 us  [reduce_stretches(): parts = add_low(kept, lax.ppermute(sent, 'context', pairs))]
    ppermute x2, starting transfers between devices: 17 us -> 1.5 us  [reduce_stretches(): parts = add_low(kept, lax.ppermute(sent, 'context', pairs))]
    ppermute x6, starting transfers between devices: 40.4 us -> 27.4 us  [reduce_line(): lax.ppermute(going_right.astype(jnp.bfloat16), 'fsdp', right_pairs)]
    dot_general x9, matrix products: 65.6 us -> 55.3 us  [contract_rows(): lax.dot_general(left, right, (((0,), (0,)), ((), ())), preferred_element_...]
    convert_element_type x17 -> x11, other arithmetic: 18.3 us -> 26.7 us  [add_low(): (left.astype(jnp.float32) + right.astype(jnp.float32)).astype(jnp.bfloat16)]
    ppermute x57 -> x54, starting transfers between devices: 124 us -> 122 us  [swap(): return lax.ppermute(value, axis, [(i, i ^ bit) for i in range(count)])]
  transfers between devices with their start and end apart: 91 -> 88, of which waited for: 30 -> 34; matrix products, arithmetic and copies ran while one was open for 27% -> 22% of each run, Pallas kernels for 1% -> 1%
where the time goes in v3:
time: 922 us; the launch traced here: 913 us
  waiting for transfers between devices  332 us (36%)
  starting transfers between devices  194 us (21%)
  matrix products  145 us (16%)
  other arithmetic  106 us (11%)
  local copies, waits for them, and re-layouts  94.5 us (10%)
  Pallas kernels  37.5 us (4%)
    ppermute x54, waiting for transfers between devices, swap(): return lax.ppermute(value, axis, [(i, i ^ bit) for i in range(count)])  250 us
    ppermute x54, starting transfers between devices, swap(): return lax.ppermute(value, axis, [(i, i ^ bit) for i in range(count)])  122 us
    dot_general x9, matrix products, contract_rows(): lax.dot_general(left, right, (((0,), (0,)), ((), ())), preferred_element_...  55.3 us
    ppermute x9, waiting for transfers between devices, left(): return lax.ppermute(value, 'fsdp', pairs)  51.6 us
    dot_general x9, matrix products, contract_cols(): lax.dot_general(left, right, (((1,), (1,)), ((), ())), preferred_element_...  43.2 us
    ppermute x6, starting transfers between devices, reduce_line(): lax.ppermute(going_right.astype(jnp.bfloat16), 'fsdp', right_pairs)  27.4 us
    convert_element_type x11, other arithmetic, add_low(): (left.astype(jnp.float32) + right.astype(jnp.float32)).astype(jnp.bfloat16)  26.7 us
    pallas_call x1, Pallas kernels, attend_grads(): pl.pallas_call(functools.partial(attend_grads_kernel, features), grid=(se...  25 us
  transfers between devices with their start and end apart: 88, of which 34 were waited for; matrix products, arithmetic and copies ran while one was open for 22% of the time, Pallas kernels for 1%

profile of v3, /device:TPU:0, one launch (start us, length us, event | category | flops | bytes accessed | tf_op | source)
XLA Modules:
  0.0 912.6 jit_solution(1340161892900025212)
XLA Ops:
  46.4 7.7 collective-permute-done.8
  82.9 18.4 %collective-permute-done.24 = bf16[1,1,512,1088]{2,3,1,0:T(8,128)(2,1)} collective-permute-done((bf16[1,1,512,1088]{2,3,1,0:T(8,128)(2,1)S(1)}, bf16[1,1,512,1088]{2,3,1,0:T(8,128)(2,1)}, u32[]{:S(2)}, u32[]{:S(2)}) %collective-permute-start.24) | collective-permute-done | bytes 1114144 | tf_op jit(solution)/shard_map/ppermute | solution.py:460
  107.7 25.1 %collective-permute-done.32 = bf16[2,136,1088]{2,1,0:T(8,128)(2,1)S(1)} collective-permute-done((bf16[2,136,1088]{2,1,0:T(8,128)(2,1)}, bf16[2,136,1088]{2,1,0:T(8,128)(2,1)S(1)}, u32[]{:S(2)}, u32[]{:S(2)}) %collective-permute-start.32) | collective-permute-done | bytes 591904 | tf_op jit(solution)/shard_map/ppermute | solution.py:66
  135.1 15.3 %collective-permute-done.21 = bf16[2,136,1088]{2,1,0:T(8,128)(2,1)S(1)} collective-permute-done((bf16[2,136,1088]{2,1,0:T(8,128)(2,1)S(1)}, bf16[2,136,1088]{2,1,0:T(8,128)(2,1)S(1)}, u32[]{:S(2)}, u32[]{:S(2)}) %collective-permute-start.21) | collective-permute-done | bytes 591904 | tf_op jit(solution)/shard_map/ppermute | solution.py:66
  156.9 9.2 %collective-permute-done.33 = bf16[2,136,1088]{2,1,0:T(8,128)(2,1)S(1)} collective-permute-done((bf16[2,136,1088]{2,1,0:T(8,128)(2,1)S(1)}, bf16[2,136,1088]{2,1,0:T(8,128)(2,1)S(1)}, u32[]{:S(2)}, u32[]{:S(2)}) %collective-permute-start.33) | collective-permute-done | bytes 591904 | tf_op jit(solution)/shard_map/ppermute | solution.py:52
  172.6 24.0 %collective-permute-done.16 = bf16[2,136,1088]{2,1,0:T(8,128)(2,1)S(1)} collective-permute-done((bf16[2,136,1088]{2,1,0:T(8,128)(2,1)S(1)}, bf16[2,136,1088]{2,1,0:T(8,128)(2,1)S(1)}, u32[]{:S(2)}, u32[]{:S(2)}) %collective-permute-start.16) | collective-permute-done | bytes 591904 | tf_op jit(solution)/shard_map/ppermute | solution.py:52
  202.1 7.9 collective-permute-done.31
  213.5 6.8 collective-permute-done.35
  252.6 7.1 fusion.18.k_ref
  259.7 7.1 fusion.19.v_ref
  269.0 12.5 %shard_map.271 = (bf16[1,512,1088]{2,1,0:T(8,128)(2,1)S(1)}, f32[1,9,2,512]{3,2,1,0:T(2,128)S(1)}) custom-call(s32[1]{0:T(128)} %bitcast.1.place_ref, bf16[1,512,1088]{2,1,0:T(8,128)(2,1)S(1)} %fusion.36.q_ref, bf16[1,2048,1088]{2,1,0:T(8,128)(2,1)S(1)} %fusion.18.k_ref, bf16[1,2048,1088]{2,1,0:T(8,128)(2,1)S(1)} %fusion.19.v_ref, ...), custom_call_target="tpu_custom_call" | custom-call | flops 9663676416 | bytes 13369344 | tf_op jit(solution)/shard_map/pallas_call | solution.py:405
  281.6 10.1 %collective-permute-done.37 = bf16[2,2,136,1088]{3,2,1,0:T(8,128)(2,1)S(1)} collective-permute-done((bf16[2,2,136,1088]{3,2,1,0:T(8,128)(2,1)S(1)}, bf16[2,2,136,1088]{3,2,1,0:T(8,128)(2,1)S(1)}, u32[]{:S(2)}, u32[]{:S(2)}) %collective-permute-start.37) | collective-permute-done | bytes 1183776 | tf_op jit(solution)/shard_map/ppermute | solution.py:52
  340.4 20.5 %convert_reduce_fusion.2 = (f32[4352]{0:T(1024)}, bf16[512,4352]{0,1:T(8,128)(2,1)}) fusion(f32[4352]{0:T(1024)S(1)} %reshape.842, f32[512,1088]{0,1:T(8,128)} %fusion.121, f32[512,1088]{0,1:T(8,128)} %fusion.120, f32[512,1088]{0,1:T(8,128)} %fusion.119, f32[512,1088]{0,1:T(8,128)} %fusion.118, bf16[4352,1088]{1,0:T(8,128)(2,1)} %bitcast.74, ...), kind=kOutput, calls=%fused_computation.31 | convolution fusion | flops 4906545152 | bytes 23988224 | tf_op jit(solution)/shard_map/dot_general | solution.py:34
  369.5 13.4 %convolution_convert_fusion = bf16[4352,1088]{0,1:T(8,128)(2,1)} fusion(bf16[1,512,1088]{1,2,0:T(8,128)(2,1)S(1)} %copy-done.53, f32[512,1088]{0,1:T(8,128)} %fusion.121, f32[512,1088]{0,1:T(8,128)} %fusion.120, f32[512,1088]{0,1:T(8,128)} %fusion.119, f32[512,1088]{0,1:T(8,128)} %fusion.118, f32[4352]{0:T(1024)S(1)} %reshape.842), kind=kOutput, calls=%fused_computation | convolution fusion | flops 4882317312 | bytes 19514368 | tf_op jit(solution)/shard_map/dot_general | solution.py:28
  391.6 15.4 %fusion.34 = bf16[1,512,1088]{1,2,0:T(8,128)(2,1)} fusion(f32[512,1088]{0,1:T(8,128)S(1)} %get-tuple-element.184, bf16[4352,1088]{1,0:T(8,128)(2,1)} %bitcast.74, f32[1088]{0:T(1024)S(1)} %copy-done.99, f32[512,1088]{0,1:T(8,128)} %fusion.121, f32[512,1088]{0,1:T(8,128)} %fusion.120, f32[512,1088]{0,1:T(8,128)} %fusion.119, f32[512,1088]{0,1:T(8,128)} %fusion.118, ...), kind=kOutput, calls=%fused_computation.79 | convolution fusion | flops 4879253504 | bytes 21746944 | tf_op jit(solution)/shard_map/dot_general | solution.py:571
  407.0 14.1 %copy.85 = bf16[4352,1088]{1,0:T(8,128)(2,1)} copy(bf16[4352,1088]{0,1:T(8,128)(2,1)} %convolution_convert_fusion) | data formatting | bytes 18939904 | tf_op jit(solution)/shard_map/convert_element_type | solution.py:577
  457.6 25.0 %shard_map.272 = (bf16[1,512,1088]{2,1,0:T(8,128)(2,1)S(1)}, bf16[1,2048,1088]{2,1,0:T(8,128)(2,1)S(1)}, bf16[1,2048,1088]{2,1,0:T(8,128)(2,1)}) custom-call(s32[1]{0:T(128)} %bitcast.1.place_ref, bf16[1,512,1088]{2,1,0:T(8,128)(2,1)S(1)} %copy-done.8, bf16[1,2048,1088]{2,1,0:T(8,128)(2,1)} %copy-done.9, bf16[1,2048,1088]{2,1,0:T(8,128)(2,1)} %copy-done.10, ...), custom_call_target="tpu_custom_call" | custom-call | flops 24159191040 | bytes 22282240 | tf_op jit(solution)/shard_map/pallas_call | solution.py:427
  485.1 10.0 %convolution_convert_fusion.8 = bf16[1088,1088]{1,0:T(8,128)(2,1)S(1)} fusion(bf16[2048,1088]{1,0:T(8,128)(2,1)} %bitcast.446, bf16[1,2048,1088]{2,1,0:T(8,128)(2,1)S(1)} %get-tuple-element.46), kind=kOutput, calls=%fused_computation.40 | convolution fusion | flops 4849799168 | bytes 11280384 | tf_op jit(solution)/shard_map/dot_general | solution.py:28
  495.2 8.3 broadcast_select_fusion.1
  503.5 16.1 %collective-permute-start.58 = (bf16[1088,1088]{1,0:T(8,128)(2,1)}, bf16[1088,1088]{1,0:T(8,128)(2,1)}, u32[]{:S(2)}, u32[]{:S(2)}) collective-permute-start(bf16[1088,1088]{1,0:T(8,128)(2,1)} %get-tuple-element.193), channel_id=1, source_target_pairs={{0,1},{1,0},{2,3},{3,2},{4,5},{5,4},{6,7},{7,6},{8,9},{9,8},{10,11... | collective-permute-start | bytes 7102472 | tf_op jit(solution)/shard_map/ppermute | solution.py:52
  523.2 56.5 %collective-permute-start.72 = (bf16[2,2,136,1088]{3,2,1,0:T(8,128)(2,1)}, bf16[2,2,136,1088]{3,2,1,0:T(8,128)(2,1)}, u32[]{:S(2)}, u32[]{:S(2)}) collective-permute-start(bf16[2,2,136,1088]{3,2,1,0:T(8,128)(2,1)} %get-tuple-element.96), channel_id=1, source_target_pairs={{0,2},{1,3},{2,0},{3,1},{4,6},{5,7},{6,4},{7,5},{8,10},{9,11},{10,... | collective-permute-start | bytes 3551240 | tf_op jit(solution)/shard_map/ppermute | solution.py:52
  599.1 7.9 pad_maximum_fusion
  608.4 26.9 %collective-permute-done.74 = bf16[2,2,136,1088]{3,2,1,0:T(8,128)(2,1)} collective-permute-done((bf16[2,2,136,1088]{3,2,1,0:T(8,128)(2,1)}, bf16[2,2,136,1088]{3,2,1,0:T(8,128)(2,1)}, u32[]{:S(2)}, u32[]{:S(2)}) %collective-permute-start.74) | collective-permute-done | bytes 1183776 | tf_op jit(solution)/shard_map/ppermute | solution.py:52
  635.3 26.9 %collective-permute-done.76 = bf16[2,2,136,1088]{3,2,1,0:T(8,128)(2,1)} collective-permute-done((bf16[2,2,136,1088]{3,2,1,0:T(8,128)(2,1)}, bf16[2,2,136,1088]{3,2,1,0:T(8,128)(2,1)}, u32[]{:S(2)}, u32[]{:S(2)}) %collective-permute-start.76) | collective-permute-done | bytes 1183776 | tf_op jit(solution)/shard_map/ppermute | solution.py:52
  662.1 26.2 %collective-permute-done.78 = bf16[2,2,136,1088]{3,2,1,0:T(8,128)(2,1)} collective-permute-done((bf16[2,2,136,1088]{3,2,1,0:T(8,128)(2,1)}, bf16[2,2,136,1088]{3,2,1,0:T(8,128)(2,1)}, u32[]{:S(2)}, u32[]{:S(2)}) %collective-permute-start.78) | collective-permute-done | bytes 1183776 | tf_op jit(solution)/shard_map/ppermute | solution.py:52
  698.5 13.0 %collective-permute-done.79 = bf16[2,136,1088]{2,1,0:T(8,128)(2,1)S(1)} collective-permute-done((bf16[2,136,1088]{2,1,0:T(8,128)(2,1)S(1)}, bf16[2,136,1088]{2,1,0:T(8,128)(2,1)S(1)}, u32[]{:S(2)}, u32[]{:S(2)}) %collective-permute-start.79) | collective-permute-done | bytes 591904 | tf_op jit(solution)/shard_map/ppermute | solution.py:52
  715.7 7.6 collective-permute-done.77
  742.8 11.9 %collective-permute-done.63 = bf16[2,136,1088]{2,1,0:T(8,128)(2,1)S(1)} collective-permute-done((bf16[2,136,1088]{2,1,0:T(8,128)(2,1)S(1)}, bf16[2,136,1088]{2,1,0:T(8,128)(2,1)S(1)}, u32[]{:S(2)}, u32[]{:S(2)}) %collective-permute-start.63) | collective-permute-done | bytes 591904 | tf_op jit(solution)/shard_map/ppermute | solution.py:52
  760.4 7.7 collective-permute-done.62
  808.8 41.5 %collective-permute-done.86 = bf16[2,136,1088]{2,1,0:T(8,128)(2,1)S(1)} collective-permute-done((bf16[2,136,1088]{2,1,0:T(8,128)(2,1)S(1)}, bf16[2,136,1088]{2,1,0:T(8,128)(2,1)S(1)}, u32[]{:S(2)}, u32[]{:S(2)}) %collective-permute-start.86) | collective-permute-done | bytes 591904 | tf_op jit(solution)/shard_map/ppermute | solution.py:52
  865.9 6.8 collective-permute-done.69
  878.3 13.4 %collective-permute-done.54 = f32[13056]{0:T(1024)S(1)} collective-permute-done((f32[13056]{0:T(1024)S(1)}, f32[13056]{0:T(1024)S(1)}, u32[]{:S(2)}, u32[]{:S(2)}) %collective-permute-start.54) | collective-permute-done | bytes 52256 | tf_op jit(solution)/shard_map/ppermute | solution.py:52
  (566 shorter events, 388.8 us)
Async XLA Ops:
  19.6 61.7 %collective-permute-start.12 = (bf16[2,136,1088]{2,1,0:T(8,128)(2,1)}, bf16[2,136,1088]{2,1,0:T(8,128)(2,1)}, u32[]{:S(2)}, u32[]{:S(2)}) collective-permute-start(bf16[2,136,1088]{2,1,0:T(8,128)(2,1)} %fusion.85), channel_id=1, source_target_pairs={{8,0},{12,4},{16,8},{20,12},{24,16},{28,20},{9,1},{13,5},{17,9},{2... | collective-permute-start | bytes 1775624 | tf_op jit(solution)/shard_map/ppermute | solution.py:66
  20.9 44.6 %collective-permute-start.10 = (bf16[2,136,1088]{2,1,0:T(8,128)(2,1)}, bf16[2,136,1088]{2,1,0:T(8,128)(2,1)}, u32[]{:S(2)}, u32[]{:S(2)}) collective-permute-start(bf16[2,136,1088]{2,1,0:T(8,128)(2,1)} %fusion.85), channel_id=1, source_target_pairs={{0,4},{4,0},{8,12},{12,8},{16,20},{20,16},{24,28},{28,24},{1,5},{5... | collective-permute-start | bytes 1775624 | tf_op jit(solution)/shard_map/ppermute | solution.py:52
  26.3 55.1 %collective-permute-start.13 = (bf16[2,136,1088]{2,1,0:T(8,128)(2,1)}, bf16[2,136,1088]{2,1,0:T(8,128)(2,1)}, u32[]{:S(2)}, u32[]{:S(2)}) collective-permute-start(bf16[2,136,1088]{2,1,0:T(8,128)(2,1)} %fusion.85), channel_id=1, source_target_pairs={{0,8},{4,12},{8,16},{12,20},{16,24},{20,28},{1,9},{5,13},{9,17},{1... | collective-permute-start | bytes 1775624 | tf_op jit(solution)/shard_map/ppermute | solution.py:59
  37.2 66.2 %collective-permute-start.28 = (bf16[2,136,1088]{2,1,0:T(8,128)(2,1)}, bf16[2,136,1088]{2,1,0:T(8,128)(2,1)}, u32[]{:S(2)}, u32[]{:S(2)}) collective-permute-start(bf16[2,136,1088]{2,1,0:T(8,128)(2,1)} %fusion.82), channel_id=1, source_target_pairs={{0,8},{4,12},{8,16},{12,20},{16,24},{20,28},{1,9},{5,13},{9,17},{1... | collective-permute-start | bytes 1775624 | tf_op jit(solution)/shard_map/ppermute | solution.py:59
  65.5 38.0 %collective-permute-start.27 = (bf16[2,136,1088]{2,1,0:T(8,128)(2,1)}, bf16[2,136,1088]{2,1,0:T(8,128)(2,1)}, u32[]{:S(2)}, u32[]{:S(2)}) collective-permute-start(bf16[2,136,1088]{2,1,0:T(8,128)(2,1)} %fusion.82), channel_id=1, source_target_pairs={{8,0},{12,4},{16,8},{20,12},{24,16},{28,20},{9,1},{13,5},{17,9},{2... | collective-permute-start | bytes 1775624 | tf_op jit(solution)/shard_map/ppermute | solution.py:66
  72.9 28.4 %collective-permute-start.24 = (bf16[1,1,512,1088]{2,3,1,0:T(8,128)(2,1)S(1)}, bf16[1,1,512,1088]{2,3,1,0:T(8,128)(2,1)}, u32[]{:S(2)}, u32[]{:S(2)}) collective-permute-start(bf16[1,1,512,1088]{2,3,1,0:T(8,128)(2,1)S(1)} %bitcast.434), channel_id=1, source_target_pairs={{0,2},{1,3},{4,6},{5,7},{8,10},{9,11},{12,14},{13,15},{16,18},{17,... | collective-permute-start | bytes 3342344 | tf_op jit(solution)/shard_map/ppermute | solution.py:460
  81.4 200.2 %collective-permute-start.36 = (bf16[2,2,136,1088]{3,2,1,0:T(8,128)(2,1)S(1)}, bf16[2,2,136,1088]{3,2,1,0:T(8,128)(2,1)}, u32[]{:S(2)}, u32[]{:S(2)}) collective-permute-start(bf16[2,2,136,1088]{3,2,1,0:T(8,128)(2,1)S(1)} %pad_maximum_fusion.3), channel_id=1, source_target_pairs={{0,2},{1,3},{2,0},{3,1},{4,6},{5,7},{6,4},{7,5},{8,10},{9,11},{10,... | collective-permute-start | bytes 3551240 | tf_op jit(solution)/shard_map/ppermute | solution.py:52
  103.5 66.7 %collective-permute-start.11 = (bf16[2,2,136,1088]{3,2,0,1:T(8,128)(2,1)S(1)}, bf16[2,2,136,1088]{3,2,0,1:T(8,128)(2,1)S(1)}, u32[]{:S(2)}, u32[]{:S(2)}) collective-permute-start(bf16[2,2,136,1088]{3,2,0,1:T(8,128)(2,1)S(1)} %copy-done.83), channel_id=1, source_target_pairs={{0,1},{1,0},{2,3},{3,2},{4,5},{5,4},{6,7},{7,6},{8,9},{9,8},{10,11... | collective-permute-start | bytes 3551240 | tf_op jit(solution)/shard_map/ppermute | solution.py:52
  104.3 28.5 %collective-permute-start.32 = (bf16[2,136,1088]{2,1,0:T(8,128)(2,1)}, bf16[2,136,1088]{2,1,0:T(8,128)(2,1)S(1)}, u32[]{:S(2)}, u32[]{:S(2)}) collective-permute-start(bf16[2,136,1088]{2,1,0:T(8,128)(2,1)} %collective-permute-done.27), channel_id=1, source_target_pairs={{8,0},{12,4},{16,8},{20,12},{9,1},{13,5},{17,9},{21,13},{10,2},{14... | collective-permute-start | bytes 1775624 | tf_op jit(solution)/shard_map/ppermute | solution.py:66
  105.7 28.5 %collective-permute-start.19 = (bf16[2,136,1088]{2,1,0:T(8,128)(2,1)S(1)}, bf16[2,136,1088]{2,1,0:T(8,128)(2,1)S(1)}, u32[]{:S(2)}, u32[]{:S(2)}) collective-permute-start(bf16[2,136,1088]{2,1,0:T(8,128)(2,1)S(1)} %broadcast_select_fusion.15), channel_id=1, source_target_pairs={{0,4},{4,0},{8,12},{12,8},{16,20},{20,16},{24,28},{28,24},{1,5},{5... | collective-permute-start | bytes 1775624 | tf_op jit(solution)/shard_map/ppermute | solution.py:52
  107.5 114.2 %collective-permute-start.25 = (bf16[1,2,512,1088]{2,3,1,0:T(8,128)(2,1)S(1)}, bf16[1,2,512,1088]{2,3,1,0:T(8,128)(2,1)S(1)}, u32[]{:S(2)}, u32[]{:S(2)}) collective-permute-start(bf16[1,2,512,1088]{2,3,1,0:T(8,128)(2,1)S(1)} %maximum_bitcast_fusion), channel_id=1, source_target_pairs={{0,1},{1,0},{2,3},{3,2},{4,5},{5,4},{6,7},{7,6},{8,9},{9,8},{10,11... | collective-permute-start | bytes 6684680 | tf_op jit(solution)/shard_map/ppermute | solution.py:460
  166.1 33.3 %collective-permute-start.22 = (bf16[2,136,1088]{2,1,0:T(8,128)(2,1)S(1)}, bf16[2,136,1088]{2,1,0:T(8,128)(2,1)S(1)}, u32[]{:S(2)}, u32[]{:S(2)}) collective-permute-start(bf16[2,136,1088]{2,1,0:T(8,128)(2,1)S(1)} %broadcast_select_fusion.13), channel_id=1, source_target_pairs={{0,4},{4,0},{8,12},{12,8},{16,20},{20,16},{24,28},{28,24},{1,5},{5... | collective-permute-start | bytes 1775624 | tf_op jit(solution)/shard_map/ppermute | solution.py:52
  170.2 26.4 %collective-permute-start.16 = (bf16[2,136,1088]{2,1,0:T(8,128)(2,1)S(1)}, bf16[2,136,1088]{2,1,0:T(8,128)(2,1)S(1)}, u32[]{:S(2)}, u32[]{:S(2)}) collective-permute-start(bf16[2,136,1088]{2,1,0:T(8,128)(2,1)S(1)} %broadcast_select_fusion.17), channel_id=1, source_target_pairs={{0,4},{4,0},{8,12},{12,8},{16,20},{20,16},{24,28},{28,24},{1,5},{5... | collective-permute-start | bytes 1775624 | tf_op jit(solution)/shard_map/ppermute | solution.py:52
  170.9 39.1 %collective-permute-start.31 = (bf16[2,136,1088]{2,1,0:T(8,128)(2,1)S(1)}, bf16[2,136,1088]{2,1,0:T(8,128)(2,1)S(1)}, u32[]{:S(2)}, u32[]{:S(2)}) collective-permute-start(bf16[2,136,1088]{2,1,0:T(8,128)(2,1)S(1)} %broadcast_select_fusion.16), channel_id=1, source_target_pairs={{0,4},{4,0},{8,12},{12,8},{16,20},{20,16},{24,28},{28,24},{1,5},{5... | collective-permute-start | bytes 1775624 | tf_op jit(solution)/shard_map/ppermute | solution.py:52
  199.4 82.1 %collective-permute-start.38 = (bf16[2,2,136,1088]{3,2,1,0:T(8,128)(2,1)}, bf16[2,2,136,1088]{3,2,1,0:T(8,128)(2,1)}, u32[]{:S(2)}, u32[]{:S(2)}) collective-permute-start(bf16[2,2,136,1088]{3,2,1,0:T(8,128)(2,1)} %pad_maximum_fusion.5), channel_id=1, source_target_pairs={{0,2},{1,3},{2,0},{3,1},{4,6},{5,7},{6,4},{7,5},{8,10},{9,11},{10,... | collective-permute-start | bytes 3551240 | tf_op jit(solution)/shard_map/ppermute | solution.py:52
  210.0 30.6 %collective-permute-start.20 = (bf16[2,2,136,1088]{3,2,0,1:T(8,128)(2,1)}, bf16[2,2,136,1088]{3,2,0,1:T(8,128)(2,1)}, u32[]{:S(2)}, u32[]{:S(2)}) collective-permute-start(bf16[2,2,136,1088]{3,2,0,1:T(8,128)(2,1)} %maximum_bitcast_fusion.3), channel_id=1, source_target_pairs={{0,1},{1,0},{2,3},{3,2},{4,5},{5,4},{6,7},{7,6},{8,9},{9,8},{10,11... | collective-permute-start | bytes 3551240 | tf_op jit(solution)/shard_map/ppermute | solution.py:52
  234.3 47.3 %collective-permute-start.39 = (bf16[2,2,136,1088]{3,2,1,0:T(8,128)(2,1)}, bf16[2,2,136,1088]{3,2,1,0:T(8,128)(2,1)S(1)}, u32[]{:S(2)}, u32[]{:S(2)}) collective-permute-start(bf16[2,2,136,1088]{3,2,1,0:T(8,128)(2,1)} %pad_maximum_fusion.6), channel_id=1, source_target_pairs={{0,2},{1,3},{2,0},{3,1},{4,6},{5,7},{6,4},{7,5},{8,10},{9,11},{10,... | collective-permute-start | bytes 3551240 | tf_op jit(solution)/shard_map/ppermute | solution.py:52
  240.6 51.1 %collective-permute-start.37 = (bf16[2,2,136,1088]{3,2,1,0:T(8,128)(2,1)S(1)}, bf16[2,2,136,1088]{3,2,1,0:T(8,128)(2,1)S(1)}, u32[]{:S(2)}, u32[]{:S(2)}) collective-permute-start(bf16[2,2,136,1088]{3,2,1,0:T(8,128)(2,1)S(1)} %copy-done.21), channel_id=1, source_target_pairs={{0,2},{1,3},{2,0},{3,1},{4,6},{5,7},{6,4},{7,5},{8,10},{9,11},{10,... | collective-permute-start | bytes 3551240 | tf_op jit(solution)/shard_map/ppermute | solution.py:52
  503.5 227.6 %collective-permute-start.58 = (bf16[1088,1088]{1,0:T(8,128)(2,1)}, bf16[1088,1088]{1,0:T(8,128)(2,1)}, u32[]{:S(2)}, u32[]{:S(2)}) collective-permute-start(bf16[1088,1088]{1,0:T(8,128)(2,1)} %get-tuple-element.193), channel_id=1, source_target_pairs={{0,1},{1,0},{2,3},{3,2},{4,5},{5,4},{6,7},{7,6},{8,9},{9,8},{10,11... | collective-permute-start | bytes 7102472 | tf_op jit(solution)/shard_map/ppermute | solution.py:52
  523.2 85.2 %collective-permute-start.72 = (bf16[2,2,136,1088]{3,2,1,0:T(8,128)(2,1)}, bf16[2,2,136,1088]{3,2,1,0:T(8,128)(2,1)}, u32[]{:S(2)}, u32[]{:S(2)}) collective-permute-start(bf16[2,2,136,1088]{3,2,1,0:T(8,128)(2,1)} %get-tuple-element.96), channel_id=1, source_target_pairs={{0,2},{1,3},{2,0},{3,1},{4,6},{5,7},{6,4},{7,5},{8,10},{9,11},{10,... | collective-permute-start | bytes 3551240 | tf_op jit(solution)/shard_map/ppermute | solution.py:52
  579.8 55.5 %collective-permute-start.74 = (bf16[2,2,136,1088]{3,2,1,0:T(8,128)(2,1)}, bf16[2,2,136,1088]{3,2,1,0:T(8,128)(2,1)}, u32[]{:S(2)}, u32[]{:S(2)}) collective-permute-start(bf16[2,2,136,1088]{3,2,1,0:T(8,128)(2,1)} %get-tuple-element.97), channel_id=1, source_target_pairs={{0,2},{1,3},{2,0},{3,1},{4,6},{5,7},{6,4},{7,5},{8,10},{9,11},{10,... | collective-permute-start | bytes 3551240 | tf_op jit(solution)/shard_map/ppermute | solution.py:52
  579.8 82.3 %collective-permute-start.76 = (bf16[2,2,136,1088]{3,2,1,0:T(8,128)(2,1)}, bf16[2,2,136,1088]{3,2,1,0:T(8,128)(2,1)}, u32[]{:S(2)}, u32[]{:S(2)}) collective-permute-start(bf16[2,2,136,1088]{3,2,1,0:T(8,128)(2,1)} %get-tuple-element.98), channel_id=1, source_target_pairs={{0,2},{1,3},{2,0},{3,1},{4,6},{5,7},{6,4},{7,5},{8,10},{9,11},{10,... | collective-permute-start | bytes 3551240 | tf_op jit(solution)/shard_map/ppermute | solution.py:52
  581.8 106.6 %collective-permute-start.78 = (bf16[2,2,136,1088]{3,2,1,0:T(8,128)(2,1)}, bf16[2,2,136,1088]{3,2,1,0:T(8,128)(2,1)}, u32[]{:S(2)}, u32[]{:S(2)}) collective-permute-start(bf16[2,2,136,1088]{3,2,1,0:T(8,128)(2,1)} %get-tuple-element.99), channel_id=1, source_target_pairs={{0,2},{1,3},{2,0},{3,1},{4,6},{5,7},{6,4},{7,5},{8,10},{9,11},{10,... | collective-permute-start | bytes 3551240 | tf_op jit(solution)/shard_map/ppermute | solution.py:52
  608.4 125.5 %collective-permute-start.59 = (bf16[1088,1088]{1,0:T(8,128)(2,1)}, bf16[1088,1088]{1,0:T(8,128)(2,1)}, u32[]{:S(2)}, u32[]{:S(2)}) collective-permute-start(bf16[1088,1088]{1,0:T(8,128)(2,1)} %get-tuple-element.195), channel_id=1, source_target_pairs={{0,1},{1,0},{2,3},{3,2},{4,5},{5,4},{6,7},{7,6},{8,9},{9,8},{10,11... | collective-permute-start | bytes 7102472 | tf_op jit(solution)/shard_map/ppermute | solution.py:52
  696.5 93.2 %collective-permute-start.51 = (bf16[2,2,1,512,1088]{3,4,2,1,0:T(8,128)(2,1)S(1)}, bf16[2,2,1,512,1088]{3,4,2,1,0:T(8,128)(2,1)}, u32[]{:S(2)}, u32[]{:S(2)}) collective-permute-start(bf16[2,2,1,512,1088]{3,4,2,1,0:T(8,128)(2,1)S(1)} %dynamic-slice_bitcast_fusion.1), channel_id=1, source_target_pairs={{0,1},{1,0},{2,3},{3,2},{4,5},{5,4},{6,7},{7,6},{8,9},{9,8},{10,11... | collective-permute-start | bytes 13369352 | tf_op jit(solution)/shard_map/ppermute | solution.py:479
  696.9 26.5 %collective-permute-start.77 = (bf16[2,136,1088]{2,1,0:T(8,128)(2,1)S(1)}, bf16[2,136,1088]{2,1,0:T(8,128)(2,1)S(1)}, u32[]{:S(2)}, u32[]{:S(2)}) collective-permute-start(bf16[2,136,1088]{2,1,0:T(8,128)(2,1)S(1)} %dynamic-slice_bitcast_fusion.6), channel_id=1, source_target_pairs={{0,4},{4,0},{8,12},{12,8},{16,20},{20,16},{24,28},{28,24},{1,5},{5... | collective-permute-start | bytes 1775624 | tf_op jit(solution)/shard_map/ppermute | solution.py:52
  739.2 29.0 %collective-permute-start.62 = (bf16[2,136,1088]{2,1,0:T(8,128)(2,1)S(1)}, bf16[2,136,1088]{2,1,0:T(8,128)(2,1)S(1)}, u32[]{:S(2)}, u32[]{:S(2)}) collective-permute-start(bf16[2,136,1088]{2,1,0:T(8,128)(2,1)S(1)} %fusion.91), channel_id=1, source_target_pairs={{0,4},{4,0},{8,12},{12,8},{16,20},{20,16},{24,28},{28,24},{1,5},{5... | collective-permute-start | bytes 1775624 | tf_op jit(solution)/shard_map/ppermute | solution.py:52
  793.5 60.8 %collective-permute-start.52 = (bf16[1,2,1,512,1088]{3,4,2,1,0:T(8,128)(2,1)S(1)}, bf16[1,2,1,512,1088]{3,4,2,1,0:T(8,128)(2,1)S(1)}, u32[]{:S(2)}, u32[]{:S(2)}) collective-permute-start(bf16[1,2,1,512,1088]{3,4,2,1,0:T(8,128)(2,1)S(1)} %dynamic-slice_bitcast_fusion.2), channel_id=1, source_target_pairs={{2,0},{3,1},{6,4},{7,5},{10,8},{11,9},{14,12},{15,13},{18,16},{19,... | collective-permute-start | bytes 6684680 | tf_op jit(solution)/shard_map/ppermute | solution.py:479
  797.0 53.3 %collective-permute-start.86 = (bf16[2,136,1088]{2,1,0:T(8,128)(2,1)S(1)}, bf16[2,136,1088]{2,1,0:T(8,128)(2,1)S(1)}, u32[]{:S(2)}, u32[]{:S(2)}) collective-permute-start(bf16[2,136,1088]{2,1,0:T(8,128)(2,1)S(1)} %add_convert_fusion.11), channel_id=1, source_target_pairs={{0,2},{1,3},{2,0},{3,1},{4,6},{5,7},{6,4},{7,5},{8,10},{9,11},{10,... | collective-permute-start | bytes 1775624 | tf_op jit(solution)/shard_map/ppermute | solution.py:52
  800.3 65.6 %collective-permute-start.60 = (bf16[2,136,1088]{2,1,0:T(8,128)(2,1)}, bf16[2,136,1088]{2,1,0:T(8,128)(2,1)}, u32[]{:S(2)}, u32[]{:S(2)}) collective-permute-start(bf16[2,136,1088]{2,1,0:T(8,128)(2,1)} %fusion.99), channel_id=1, source_target_pairs={{0,4},{4,0},{8,12},{12,8},{16,20},{20,16},{24,28},{28,24},{1,5},{5... | collective-permute-start | bytes 1775624 | tf_op jit(solution)/shard_map/ppermute | solution.py:52
  800.9 65.0 %collective-permute-start.66 = (bf16[2,136,1088]{2,1,0:T(8,128)(2,1)}, bf16[2,136,1088]{2,1,0:T(8,128)(2,1)}, u32[]{:S(2)}, u32[]{:S(2)}) collective-permute-start(bf16[2,136,1088]{2,1,0:T(8,128)(2,1)} %get-tuple-element.60), channel_id=1, source_target_pairs={{0,8},{4,12},{8,16},{12,20},{16,24},{20,28},{1,9},{5,13},{9,17},{1... | collective-permute-start | bytes 1775624 | tf_op jit(solution)/shard_map/ppermute | solution.py:103
  808.0 43.6 %collective-permute-start.68 = (bf16[2,136,1088]{2,1,0:T(8,128)(2,1)S(1)}, bf16[2,136,1088]{2,1,0:T(8,128)(2,1)S(1)}, u32[]{:S(2)}, u32[]{:S(2)}) collective-permute-start(bf16[2,136,1088]{2,1,0:T(8,128)(2,1)S(1)} %fusion.47), channel_id=1, source_target_pairs={{16,8},{20,12},{24,16},{28,20},{17,9},{21,13},{25,17},{29,21},{18,... | collective-permute-start | bytes 1775624 | tf_op jit(solution)/shard_map/ppermute | solution.py:104
  (164 other events, 3294.9 us)
